TPU v7x, 256 devices: a whole 4x4x8 slice. The times are simulated.
256 devices in a mesh: cache: 32 (over z, x), tensor: 8 (over y, core).
Axes of the slice: x: 4, y: 4, z: 8, core: 2. Of those that a mesh axis runs over, the one named last changes fastest.
Arguments:
- queries: bfloat16 [256, 4, 8192], P('cache', None, 'tensor'), may hold values from -12 to 12
- new_kv: bfloat16 [256, 4, 2, 1024], P('cache', None, None, 'tensor'), may hold values from -12 to 12
- prefix_kv: bfloat16 [2, 196608, 1024], P(None, 'cache', 'tensor'), may hold values from -6 to 6
- suffix_kv: bfloat16 [256, 2, 512, 1024], P('cache', None, None, 'tensor'), may hold values from -9 to 9
- suffix_len: int32 [256], P('cache'), may hold values from 1 to 512, as said below
- branch_prompt: int32 [256, 1], P('cache'), may hold values from 0 to 7; in each aligned block of 8 rows (0 to 7, 8 to 15, ...) at most 2 rows name the same one
- out_weight: bfloat16 [8192, 8192], P('tensor', 'cache'), may hold values from -1 to 1
Outputs:
- attn_out: bfloat16 [256, 4, 8192], P('tensor', None, 'cache')
Inputs may be any that keep to these rules, and one draw needn't show every extreme that they name: `branch_prompt`: among the 8 rows of one cache index no prompt is named more than 2 times, a bound that some block reaches. `suffix_len`: some branch has a full suffix and some a suffix of one token.
All inputs are finite; a program needn't handle non-finite values.
Results may differ from a plain program's by a relative error of at most 0.01745.
Values may be sent and summed in bfloat16 or wider, within the bound.
No kernel may reach another device: no remote copies, remote signals or barrier semaphores. Data moves between devices by JAX's collectives and lax.ppermute only.
A program may use at most 64 MiB of HBM per device.

v0:
```python
import jax
import jax.numpy as jnp
from jax import lax
from jax.sharding import PartitionSpec as P

HEAD_DIM = 128
PROMPT_LEN = 24576


def per_device(queries, new_kv, prefix_kv, suffix_kv, suffix_len, branch_prompt, out_weight):
    ncache = lax.axis_size("cache")
    branches, steps, qwidth = queries.shape
    kvwidth = new_kv.shape[-1]
    kv_dev = kvwidth // HEAD_DIM
    group = qwidth // kvwidth
    cache_len = prefix_kv.shape[1]
    prompts = cache_len * ncache // PROMPT_LEN
    span = PROMPT_LEN // cache_len
    slots = max(2, (branches + prompts - 1) // prompts)
    scale = HEAD_DIM ** (-0.5)
    prompt_ids = branch_prompt[:, 0]
    earlier = jnp.arange(branches)[None, :] < jnp.arange(branches)[:, None]
    same = prompt_ids[:, None] == prompt_ids[None, :]
    ranks = jnp.sum(same & earlier, axis=1)
    block = min(512, cache_len)
    key_blocks = prefix_kv[0].reshape(cache_len // block, block, kv_dev, HEAD_DIM)
    value_blocks = prefix_kv[1].reshape(cache_len // block, block, kv_dev, HEAD_DIM)
    every_query, every_prompt = (
        lax.all_gather(queries, "cache", axis=0, tiled=True),
        lax.all_gather(branch_prompt, "cache", axis=0, tiled=True),
    )
    mine = lax.axis_index("cache") // span
    grid_prompt = every_prompt[:, 0].reshape(ncache, branches)
    same_all = grid_prompt[:, :, None] == grid_prompt[:, None, :]
    ranks_all = jnp.sum(same_all & earlier[None], axis=2)
    pick = (grid_prompt[:, None, :] == mine) & (
        ranks_all[:, None, :] == jnp.arange(slots)[None, :, None]
    )
    grouped = every_query.reshape(ncache, branches, steps * qwidth)
    received = jnp.einsum(
        "acb,abw->acw", pick.astype(jnp.bfloat16), grouped, preferred_element_type=jnp.float32
    )
    received = received.astype(jnp.bfloat16).reshape(ncache, slots, steps, qwidth)
    sources = received.shape[0]
    count = received.shape[1]
    query_heads = received.reshape(sources, count, steps, kv_dev, group, HEAD_DIM)
    shape = (sources, count, steps, kv_dev, group)

    def visit(carry, pair):
        top, total, acc = carry
        key_block, value_block = pair
        scores = (
            jnp.einsum(
                "acsghd,jgd->acsghj", query_heads, key_block, preferred_element_type=jnp.float32
            )
            * scale
        )
        new_top = jnp.maximum(top, jnp.max(scores, axis=-1))
        weights = jnp.exp(scores - new_top[..., None])
        fade = jnp.exp(top - new_top)
        total = total * fade + jnp.sum(weights, axis=-1)
        acc = acc * fade[..., None] + jnp.einsum(
            "acsghj,jgd->acsghd",
            weights.astype(jnp.bfloat16),
            value_block,
            preferred_element_type=jnp.float32,
        )
        return ((new_top, total, acc), None)

    start = (
        jnp.full(shape, -jnp.inf, jnp.float32),
        jnp.zeros(shape, jnp.float32),
        jnp.zeros(shape + (HEAD_DIM,), jnp.float32),
    )
    (top, total, acc), _ = lax.scan(visit, start, (key_blocks, value_blocks))
    back = (
        lax.all_to_all(acc, "cache", split_axis=0, concat_axis=0, tiled=True),
        lax.all_to_all(top, "cache", split_axis=0, concat_axis=0, tiled=True),
        lax.all_to_all(total, "cache", split_axis=0, concat_axis=0, tiled=True),
    )
    back_acc, back_top, back_total = back
    index = (prompt_ids[:, None] * span + jnp.arange(span)[None, :]) * slots + ranks[:, None]
    part_acc = back_acc.reshape((ncache * slots,) + back_acc.shape[2:])[index]
    part_top = back_top.reshape((ncache * slots,) + back_top.shape[2:])[index]
    part_total = back_total.reshape((ncache * slots,) + back_total.shape[2:])[index]
    query_heads = queries.reshape(branches, steps, kv_dev, group, HEAD_DIM)
    suffix_slots = suffix_kv.shape[2]
    suffix_keys = suffix_kv[:, 0].reshape(branches, suffix_slots, kv_dev, HEAD_DIM)
    suffix_values = suffix_kv[:, 1].reshape(branches, suffix_slots, kv_dev, HEAD_DIM)
    fresh_keys = new_kv[:, :, 0].reshape(branches, steps, kv_dev, HEAD_DIM)
    fresh_values = new_kv[:, :, 1].reshape(branches, steps, kv_dev, HEAD_DIM)
    suffix_scores = (
        jnp.einsum(
            "bsghd,bjgd->bsghj", query_heads, suffix_keys, preferred_element_type=jnp.float32
        )
        * scale
    )
    fresh_scores = (
        jnp.einsum("bsghd,bjgd->bsghj", query_heads, fresh_keys, preferred_element_type=jnp.float32)
        * scale
    )
    suffix_live = (jnp.arange(suffix_slots)[None, :] < suffix_len[:, None])[:, None, None, None, :]
    fresh_live = (jnp.arange(steps)[None, :] <= jnp.arange(steps)[:, None])[None, :, None, None, :]
    suffix_scores = jnp.where(suffix_live, suffix_scores, -jnp.inf)
    fresh_scores = jnp.where(fresh_live, fresh_scores, -jnp.inf)
    local_top = jnp.maximum(jnp.max(suffix_scores, axis=-1), jnp.max(fresh_scores, axis=-1))
    suffix_weights = jnp.exp(suffix_scores - local_top[..., None])
    fresh_weights = jnp.exp(fresh_scores - local_top[..., None])
    local_total = jnp.sum(suffix_weights, axis=-1) + jnp.sum(fresh_weights, axis=-1)
    local_acc = jnp.einsum(
        "bsghj,bjgd->bsghd",
        suffix_weights.astype(jnp.bfloat16),
        suffix_values,
        preferred_element_type=jnp.float32,
    )
    local_acc = local_acc + jnp.einsum(
        "bsghj,bjgd->bsghd",
        fresh_weights.astype(jnp.bfloat16),
        fresh_values,
        preferred_element_type=jnp.float32,
    )
    overall = jnp.maximum(local_top, jnp.max(part_top, axis=1))
    local_fade = jnp.exp(local_top - overall)
    part_fade = jnp.exp(part_top - overall[:, None])
    total = local_total * local_fade + jnp.sum(part_total * part_fade, axis=1)
    acc = local_acc * local_fade[..., None] + jnp.sum(part_acc * part_fade[..., None], axis=1)
    mixed = (acc / total[..., None]).astype(jnp.bfloat16).reshape(branches * steps, qwidth)
    partial_value = jnp.dot(
        lax.all_gather(mixed, "cache", axis=0, tiled=True),
        out_weight,
        preferred_element_type=jnp.float32,
    )
    summed = lax.psum_scatter(
        partial_value.astype(jnp.bfloat16), "tensor", scatter_dimension=0, tiled=True
    )
    return summed.reshape(-1, steps, summed.shape[-1])


def solution(mesh):
    return jax.shard_map(
        per_device,
        mesh=mesh,
        in_specs=(
            P("cache", None, "tensor"),
            P("cache", None, None, "tensor"),
            P(None, "cache", "tensor"),
            P("cache", None, None, "tensor"),
            P("cache"),
            P("cache", None),
            P("tensor", "cache"),
        ),
        out_specs=P("tensor", None, "cache"),
        check_vma=False,
    )
```

profile of v0, /device:TPU:17, one launch (start us, length us, event | category | flops | bytes accessed | tf_op | source)
XLA Modules:
  0.0 372.2 jit_solution(17095978734667305395)
XLA Ops:
  10.0 19.0 %all-reduce = s32[256]{0:T(256)S(1)} all-reduce(s32[256]{0:T(256)S(1)} %bitcast_dynamic-update-slice_fusion), channel_id=1, replica_groups=mesh['cache'=32,'tensor'=8] {'cache'}, use_global_device_ids=true, to_apply=%add | all-reduce | flops 256 | bytes 2048
  31.7 3.8 %fusion.57 = (bf16[1,6144,128]{2,1,0:T(8,128)(2,1)}, bf16[1,6144,128]{2,1,0:T(8,128)(2,1)}) fusion(bf16[2,6144,128]{2,1,0:T(8,128)(2,1)} %param.11), kind=kLoop, calls=%fused_computation.86 | loop fusion | bytes 6291456 | tf_op jit(solution)/shard_map/slice | solution.py:27
  35.5 51.2 %all-gather.3.cloned.1.call-done = bf16[256,4,1024]{2,1,0:T(4,128)(2,1)} async-done(((bf16[8,4,1024]{2,1,0:T(4,128)(2,1)}), bf16[256,4,1024]{2,1,0:T(4,128)(2,1)}) %all-gather.3.cloned.1.call-update) | async-done | bytes 2097168 | tf_op jit(solution)/shard_map/all_gather | solution.py:29
  86.7 4.5 %reshape.330 = bf16[32,8,4096]{2,1,0:T(8,128)(2,1)} reshape(bf16[256,4,1024]{2,1,0:T(4,128)(2,1)} %all-gather.3.cloned.1.call-done) | data formatting | bytes 4194304 | tf_op jit(solution)/shard_map/reshape | solution.py:39
  94.2 101.3 %while.15 = (s32[]{:T(128)}, f32[32,2,4,1,8]{0,4,2,1,3:T(8,128)S(1)}, f32[32,2,4,1,8]{0,4,2,1,3:T(8,128)S(1)}, f32[32,2,4,1,8,128]{5,0,4,2,1,3:T(8,128)S(1)}, bf...) while((s32[]{:T(128)}, ...), condition=%wide.region_6.7_spmd.clone, body=%wide.region_3.0_spmd.clone.sunk | while | flops 546058240 | bytes 32375940 | solution.py:75
  94.3 3.5 bitcast_reduce_fusion.3
  97.8 3.2 fusion.75
  102.7 3.5 bitcast_reduce_fusion.3
  106.3 3.2 fusion.75
  111.1 3.5 bitcast_reduce_fusion.3
  114.7 3.2 fusion.75
  119.6 3.5 bitcast_reduce_fusion.3
  128.0 3.5 bitcast_reduce_fusion.3
  131.6 3.2 fusion.75
  136.5 3.5 bitcast_reduce_fusion.3
  144.9 3.5 bitcast_reduce_fusion.3
  153.3 3.5 bitcast_reduce_fusion.3
  156.9 3.2 fusion.75
  161.8 3.5 bitcast_reduce_fusion.3
  165.3 3.2 fusion.75
  170.2 3.5 bitcast_reduce_fusion.3
  178.6 3.5 bitcast_reduce_fusion.3
  182.2 3.2 fusion.75
  187.1 3.5 bitcast_reduce_fusion.3
  196.2 4.9 %all-to-all-start = ((f32[32,2,4,1,8]{4,2,1,3,0:T(4,128)}), f32[32,2,4,1,8]{4,2,1,3,0:T(4,128)S(1)}, u32[]{:S(2)}, u32[]{:S(2)}) async-start(f32[32,2,4,1,8]{4,2,1,3,0:T(4,128)} %copy.54), calls=%async_computation | async-start | bytes 262144 | tf_op jit(solution)/shard_map/all_to_all | solution.py:78
  202.0 8.5 %all-to-all-done = f32[32,2,4,1,8]{4,2,1,3,0:T(4,128)S(1)} async-done(((f32[32,2,4,1,8]{4,2,1,3,0:T(4,128)}), f32[32,2,4,1,8]{4,2,1,3,0:T(4,128)S(1)}, u32[]{:S(2)}, u32[]{:S(2)}) %all-to-all-start) | async-done | bytes 8224 | tf_op jit(solution)/shard_map/all_to_all | solution.py:78
  210.5 3.8 %all-to-all-start.2 = ((f32[32,2,4,1,8]{4,2,1,3,0:T(4,128)}), f32[32,2,4,1,8]{4,2,1,3,0:T(4,128)S(1)}, u32[]{:S(2)}, u32[]{:S(2)}) async-start(f32[32,2,4,1,8]{4,2,1,3,0:T(4,128)} %copy.58), calls=%async_computation.2 | async-start | bytes 262144 | tf_op jit(solution)/shard_map/all_to_all | solution.py:79
  216.1 7.7 %all-to-all-done.2 = f32[32,2,4,1,8]{4,2,1,3,0:T(4,128)S(1)} async-done(((f32[32,2,4,1,8]{4,2,1,3,0:T(4,128)}), f32[32,2,4,1,8]{4,2,1,3,0:T(4,128)S(1)}, u32[]{:S(2)}, u32[]{:S(2)}) %all-to-all-start.2) | async-done | bytes 8224 | tf_op jit(solution)/shard_map/all_to_all | solution.py:79
  223.8 3.9 %all-to-all-start.1 = ((f32[32,2,4,1,8,128]{5,4,2,1,3,0:T(8,128)}), f32[32,2,4,1,8,128]{5,4,2,1,3,0:T(8,128)S(1)}, u32[]{:S(2)}, u32[]{:S(2)}) async-start(f32[32,2,4,1,8,128]{5,4,2,1,3,0:T(8,128)} %copy.57), calls=%async_computation.1 | async-start | bytes 2097152 | tf_op jit(solution)/shard_map/all_to_all | solution.py:77
  232.0 15.1 %all-to-all-done.1 = f32[32,2,4,1,8,128]{5,4,2,1,3,0:T(8,128)S(1)} async-done(((f32[32,2,4,1,8,128]{5,4,2,1,3,0:T(8,128)}), f32[32,2,4,1,8,128]{5,4,2,1,3,0:T(8,128)S(1)}, u32[]{:S(2)}, u32[]{:S(2)}) %all-to-all-start.1) | async-done | bytes 1048608 | tf_op jit(solution)/shard_map/all_to_all | solution.py:77
  250.2 80.0 %all-gather.5.cloned.1.call-done = bf16[1024,1024]{1,0:T(8,128)(2,1)} async-done(((bf16[32,1024]{1,0:T(8,128)(2,1)}), bf16[1024,1024]{1,0:T(8,128)(2,1)}) %all-gather.5.cloned.1.call-update) | async-done | bytes 2097168 | tf_op jit(solution)/shard_map/all_gather | solution.py:129
  333.4 30.8 %reduce-scatter.2.cloned.1.call-done = bf16[128,256]{1,0:T(8,128)(2,1)} async-done(((bf16[1024,256]{1,0:T(8,128)(2,1)}), bf16[128,256]{1,0:T(8,128)(2,1)}) %reduce-scatter.2.cloned.1.call-update) | async-done | bytes 65552 | tf_op jit(solution)/shard_map/reduce_scatter | solution.py:133
  (134 shorter events, 59.7 us)
Async XLA Ops:
  6.5 323.7 %copy-start = (bf16[1024,256]{1,0:T(8,128)(2,1)S(1)}, bf16[1024,256]{1,0:T(8,128)(2,1)}, u32[]{:S(2)}) copy-start(bf16[1024,256]{1,0:T(8,128)(2,1)} %param.15) | copy-start | bytes 1572868
  6.5 80.2 %all-gather.3.cloned.1.call-start = ((), (), s32[]{:S(2)}) async-start(), calls=%async_computation.4 | async-start | bytes 2162688 | tf_op jit(solution)/shard_map/all_gather | solution.py:29
  94.2 120.2 %copy-start.3 = (s32[8]{0:T(128)S(1)}, s32[8]{0:T(128)}, u32[]{:S(2)}) copy-start(s32[8]{0:T(128)} %param.13) | copy-start | bytes 100
  97.8 3.5 copy-start.1
  106.3 3.5 copy-start.1
  114.7 3.5 copy-start.1
  123.1 3.5 copy-start.1
  131.6 3.5 copy-start.1
  140.0 3.5 copy-start.1
  148.4 3.5 copy-start.1
  156.9 3.5 copy-start.1
  165.3 3.5 copy-start.1
  173.8 3.5 copy-start.1
  182.2 3.5 copy-start.1
  190.6 3.5 copy-start.1
  196.2 14.3 %all-to-all-start = ((f32[32,2,4,1,8]{4,2,1,3,0:T(4,128)}), f32[32,2,4,1,8]{4,2,1,3,0:T(4,128)S(1)}, u32[]{:S(2)}, u32[]{:S(2)}) async-start(f32[32,2,4,1,8]{4,2,1,3,0:T(4,128)} %copy.54), calls=%async_computation | async-start | bytes 262144 | tf_op jit(solution)/shard_map/all_to_all | solution.py:78
  210.5 13.3 %all-to-all-start.2 = ((f32[32,2,4,1,8]{4,2,1,3,0:T(4,128)}), f32[32,2,4,1,8]{4,2,1,3,0:T(4,128)S(1)}, u32[]{:S(2)}, u32[]{:S(2)}) async-start(f32[32,2,4,1,8]{4,2,1,3,0:T(4,128)} %copy.58), calls=%async_computation.2 | async-start | bytes 262144 | tf_op jit(solution)/shard_map/all_to_all | solution.py:79
  214.5 13.3 %copy-start.2 = (bf16[8,4,1024]{2,1,0:T(4,128)(2,1)S(1)}, bf16[8,4,1024]{2,1,0:T(4,128)(2,1)}, u32[]{:S(2)}) copy-start(bf16[8,4,1024]{2,1,0:T(4,128)(2,1)} %param.9) | copy-start | bytes 196612
  223.8 23.4 %all-to-all-start.1 = ((f32[32,2,4,1,8,128]{5,4,2,1,3,0:T(8,128)}), f32[32,2,4,1,8,128]{5,4,2,1,3,0:T(8,128)S(1)}, u32[]{:S(2)}, u32[]{:S(2)}) async-start(f32[32,2,4,1,8,128]{5,4,2,1,3,0:T(8,128)} %copy.57), calls=%async_computation.1 | async-start | bytes 2097152 | tf_op jit(solution)/shard_map/all_to_all | solution.py:77
  227.7 102.5 %all-gather.5.cloned.1.call-start = ((), (), s32[]{:S(2)}) async-start(), calls=%async_computation.5 | async-start | bytes 2162688 | tf_op jit(solution)/shard_map/all_gather | solution.py:129
  250.2 114.0 %reduce-scatter.2.cloned.1.call-start = ((), (), s32[]{:S(2)}) async-start(), calls=%async_computation.6 | async-start | bytes 589824 | tf_op jit(solution)/shard_map/reduce_scatter | solution.py:133
Sparse Core Ops, SparseCore 0:
  9.9 76.7 all-gather.2
  250.3 79.8 all-gather.4
  333.5 30.6 reduce-scatter.1
where the time goes:
time: 377 us; the launch traced here: 372 us
  waiting for transfers between devices  194 us (51%)
  matrix products  89.8 us (24%)
  local copies, waits for them, and re-layouts  23.1 us (6%)
  blocking collectives  19 us (5%)
  other arithmetic  18.8 us (5%)
  between operations  14 us (4%)
  starting transfers between devices  12.8 us (3%)
    all_gather x1, waiting for transfers between devices, per_device(): lax.all_gather(mixed, 'cache', axis=0, tiled=True)  80 us
    all_gather x1, waiting for transfers between devices, per_device(): lax.all_gather(queries, 'cache', axis=0, tiled=True)  51.2 us
    dot_general x12, matrix products, visit(): jnp.einsum('acsghd,jgd->acsghj', query_heads, key_block, preferred_elemen...  42.4 us
    dot_general x12, matrix products, visit(): jnp.einsum('acsghj,jgd->acsghd', weights.astype(jnp.bfloat16), value_bloc...  38 us
    reduce_scatter x1, waiting for transfers between devices, per_device(): lax.psum_scatter(partial_value.astype(jnp.bfloat16), 'tensor', scatter_di...  30.8 us
    unnamed x1, blocking collectives  19 us
    reduce_sum x12, other arithmetic, visit(): total = total * fade + jnp.sum(weights, axis=-1)  15.9 us
    all_to_all x1, waiting for transfers between devices, per_device(): lax.all_to_all(acc, 'cache', split_axis=0, concat_axis=0, tiled=True)  15.1 us
  transfers between devices with their start and end apart: 6, of which 6 were waited for; matrix products, arithmetic and copies ran while one was open for 4% of the time, Pallas kernels for 0%

commit v1 on v0

v1 whole, which is shorter than its diff:
```python
import functools

import jax
import jax.numpy as jnp
from jax import lax
from jax.experimental import pallas as pl
from jax.experimental.pallas import tpu as pltpu
from jax.sharding import PartitionSpec as P

HEAD_DIM = 128
PROMPT_LEN = 24576
PROMPTS = 8
SLOTS = 2
LOG2E = 1.4426950408889634
SCORE = LOG2E * HEAD_DIM ** (-0.5)
VMEM_LIMIT = 48 * 1024 * 1024
F32 = jnp.float32
BF16 = jnp.bfloat16


def params():
    return pltpu.CompilerParams(vmem_limit_bytes=VMEM_LIMIT)


def whole(memory_space=pltpu.VMEM):
    return pl.BlockSpec(memory_space=memory_space)


def rank_of(prompt_ref, b):
    rank = jnp.int32(0)
    for earlier in range(b):
        rank += (prompt_ref[earlier] == prompt_ref[b]).astype(jnp.int32)
    return rank


def three_terms(value):
    high = value.astype(BF16).astype(F32)
    rest = value - high
    middle = rest.astype(BF16).astype(F32)
    return high, middle, rest - middle


def pack_kernel(branches, steps, group, prompt_ref, q_ref, packed_ref, rows_ref):
    height = steps * group
    packed_ref[...] = jnp.zeros_like(packed_ref)
    q = q_ref[...].astype(F32)
    for b in range(branches):
        own = q[b * steps : (b + 1) * steps]
        rows = jnp.concatenate(
            [own[:, h * HEAD_DIM : (h + 1) * HEAD_DIM] for h in range(group)], axis=0
        ).astype(BF16)
        rows_ref[b] = rows
        at = pl.multiple_of(rank_of(prompt_ref, b) * height, height)
        packed_ref[prompt_ref[b], pl.ds(at, height), :] = rows


def pack(prompt_ids, queries, group):
    branches, steps, _ = queries.shape
    height = steps * group
    return pl.pallas_call(
        functools.partial(pack_kernel, branches, steps, group),
        in_specs=[whole(pltpu.SMEM), whole()],
        out_specs=[whole(), whole()],
        out_shape=[
            jax.ShapeDtypeStruct((PROMPTS, SLOTS * height, HEAD_DIM), BF16),
            jax.ShapeDtypeStruct((branches, height, HEAD_DIM), BF16),
        ],
        compiler_params=params(),
        name="pack_queries",
    )(prompt_ids, queries.reshape(branches * steps, -1))


def attend_kernel(last, part, q_ref, kv_ref, out_ref, qt_ref, top_ref, total_ref, acc_ref):
    i = pl.program_id(0)
    rows = q_ref.shape[0]

    @pl.when(i == 0)
    def _():
        qt_ref[...] = q_ref[...].T
        top_ref[...] = jnp.full(top_ref.shape, -jnp.inf, F32)
        total_ref[...] = jnp.zeros(total_ref.shape, F32)
        acc_ref[...] = jnp.zeros(acc_ref.shape, F32)

    top, total, acc = top_ref[...], total_ref[...], acc_ref[...]
    for k in range(0, kv_ref.shape[1], part):
        scores = jnp.dot(kv_ref[0, k : k + part, :], qt_ref[...], preferred_element_type=F32)
        new_top = jnp.maximum(top, jnp.max(scores, axis=0, keepdims=True))
        weights = jnp.exp2((scores - new_top) * SCORE)
        fade = jnp.exp2((top - new_top) * SCORE)
        total = total * fade + jnp.sum(weights, axis=0, keepdims=True)
        acc = acc * fade + lax.dot_general(
            kv_ref[1, k : k + part, :],
            weights.astype(BF16),
            (((0,), (0,)), ((), ())),
            preferred_element_type=F32,
        )
        top = new_top
    top_ref[...], total_ref[...], acc_ref[...] = top, total, acc

    @pl.when(i == last)
    def _():
        total = total_ref[...]
        out_ref[0:HEAD_DIM, :] = (acc_ref[...] / total).astype(BF16)
        terms = three_terms(top_ref[...] * SCORE + jnp.log2(total))
        row = lax.broadcasted_iota(jnp.int32, (16, rows), 0)
        stats = jnp.zeros((16, rows), F32)
        for j in range(3):
            stats = jnp.where(row == j, terms[j], stats)
        out_ref[HEAD_DIM : HEAD_DIM + 16, :] = stats.astype(BF16)


def attend(q, kv):
    rows, length = q.shape[0], kv.shape[1]
    block, part = 2048, 1024
    return pl.pallas_call(
        functools.partial(attend_kernel, length // block - 1, part),
        grid=(length // block,),
        in_specs=[
            pl.BlockSpec((rows, HEAD_DIM), lambda i: (0, 0)),
            pl.BlockSpec((2, block, HEAD_DIM), lambda i: (0, i, 0)),
        ],
        out_specs=pl.BlockSpec((HEAD_DIM + 16, rows), lambda i: (0, 0)),
        out_shape=jax.ShapeDtypeStruct((HEAD_DIM + 16, rows), BF16),
        scratch_shapes=[
            pltpu.VMEM((HEAD_DIM, rows), BF16),
            pltpu.VMEM((1, rows), F32),
            pltpu.VMEM((1, rows), F32),
            pltpu.VMEM((HEAD_DIM, rows), F32),
        ],
        compiler_params=params(),
        cost_estimate=pl.CostEstimate(
            flops=8 * rows * length * HEAD_DIM,
            transcendentals=rows * length,
            bytes_accessed=4 * length * HEAD_DIM,
        ),
        name="prefix_attention",
    )(q, kv)


def suffix_kernel(steps, len_ref, q_ref, kv_ref, new_ref, out_ref, lse_ref):
    length = len_ref[pl.program_id(0)]
    slots = kv_ref.shape[2]
    keys = jnp.concatenate([kv_ref[0, 0], new_ref[0, 0]], axis=0)
    values = jnp.concatenate([kv_ref[0, 1], new_ref[0, 1]], axis=0)
    scores = lax.dot_general(
        q_ref[0], keys, (((1,), (1,)), ((), ())), preferred_element_type=F32
    )
    place = lax.broadcasted_iota(jnp.int32, scores.shape, 1)
    step = lax.broadcasted_iota(jnp.int32, scores.shape, 0) % steps
    live = (place < length) | ((place >= slots) & (place - slots <= step))
    scores = jnp.where(live, scores, -jnp.inf)
    top = jnp.max(scores, axis=1, keepdims=True)
    weights = jnp.exp2((scores - top) * SCORE)
    total = jnp.sum(weights, axis=1, keepdims=True)
    acc = jnp.dot(weights.astype(BF16), values, preferred_element_type=F32)
    out_ref[0] = acc / total
    lse_ref[0] = jnp.broadcast_to(top * SCORE + jnp.log2(total), acc.shape)


def suffix(lengths, q_rows, suffix_kv, fresh, steps):
    branches, height, _ = q_rows.shape
    block = pl.BlockSpec((1, height, HEAD_DIM), lambda i: (i, 0, 0))
    return pl.pallas_call(
        functools.partial(suffix_kernel, steps),
        grid=(branches,),
        in_specs=[
            whole(pltpu.SMEM),
            block,
            pl.BlockSpec((1,) + suffix_kv.shape[1:], lambda i: (i, 0, 0, 0)),
            pl.BlockSpec((1,) + fresh.shape[1:], lambda i: (i, 0, 0, 0)),
        ],
        out_specs=[block, block],
        out_shape=[jax.ShapeDtypeStruct((branches, height, HEAD_DIM), F32)] * 2,
        compiler_params=params(),
        name="suffix_attention",
    )(lengths, q_rows, suffix_kv, fresh)


def merge_kernel(homes, *refs):
    *part_refs, out_ref = refs
    parts = [ref[...].astype(F32) for ref in part_refs]
    lses = [jnp.sum(p[HEAD_DIM : HEAD_DIM + 3], axis=0, keepdims=True) for p in parts]
    top = functools.reduce(jnp.maximum, lses)
    shares = [jnp.exp2(lse - top) for lse in lses]
    total = sum(shares)
    acc = sum(p[0:HEAD_DIM] * share for p, share in zip(parts, shares, strict=True))
    rows = acc.shape[1]
    height = rows // homes
    out_ref[:, 0:height, :] = (acc / total).T.astype(BF16).reshape(homes, height, HEAD_DIM)
    terms = three_terms(top + jnp.log2(total))
    row = lax.broadcasted_iota(jnp.int32, (16, rows), 0)
    stats = jnp.zeros((16, rows), F32)
    for j in range(3):
        stats = jnp.where(row == j, terms[j], stats)
    stats = stats.astype(BF16)
    for home in range(homes):
        at = home * height // HEAD_DIM * HEAD_DIM
        out_ref[home, height : height + 16, :] = stats[:, at : at + HEAD_DIM]


def merge(parts, homes):
    height = parts[0].shape[1] // homes
    return pl.pallas_call(
        functools.partial(merge_kernel, homes),
        in_specs=[whole()] * len(parts),
        out_specs=whole(),
        out_shape=jax.ShapeDtypeStruct((homes, height + 16, HEAD_DIM), BF16),
        compiler_params=params(),
        name="merge_parts",
    )(*parts)


def finish_kernel(steps, group, prompt_ref, home_ref, back_ref, own_ref, lse_ref, out_ref, col_ref):
    branches, height, _ = own_ref.shape
    tall = SLOTS * height
    lanes = (home_ref[0] * tall) % HEAD_DIM
    pieces = []
    for b in range(branches):
        prompt = prompt_ref[b]
        at = pl.multiple_of(rank_of(prompt_ref, b) * height, height)
        part = back_ref[prompt, pl.ds(at, height), :].astype(F32)
        stats = back_ref[prompt, tall : tall + 16, :].astype(F32)
        part_lse = jnp.sum(stats[0:3], axis=0, keepdims=True)
        col_ref[b] = jnp.broadcast_to(part_lse, (HEAD_DIM, HEAD_DIM)).T
        part_lse = col_ref[b, pl.ds(pl.multiple_of(lanes + at, height), height), :]
        own_lse = lse_ref[b]
        top = jnp.maximum(part_lse, own_lse)
        part_share = jnp.exp2(part_lse - top)
        own_share = jnp.exp2(own_lse - top)
        mixed = (part * part_share + own_ref[b] * own_share) / (part_share + own_share)
        pieces.append(
            jnp.concatenate([mixed[h * steps : (h + 1) * steps] for h in range(group)], axis=1)
        )
    out_ref[...] = jnp.concatenate(pieces, axis=0).astype(BF16)


def finish(prompt_ids, home, back, own, lse, steps, group):
    branches = own.shape[0]
    return pl.pallas_call(
        functools.partial(finish_kernel, steps, group),
        in_specs=[whole(pltpu.SMEM), whole(pltpu.SMEM), whole(), whole(), whole()],
        out_specs=whole(),
        out_shape=jax.ShapeDtypeStruct((branches * steps, group * HEAD_DIM), BF16),
        scratch_shapes=[pltpu.VMEM((branches, HEAD_DIM, HEAD_DIM), F32)],
        compiler_params=params(),
        name="finish_attention",
    )(prompt_ids, home, back, own, lse)


def project_kernel(place_ref, *refs):
    *mixed_refs, weight_ref, out_ref, rows_ref = refs
    count = len(mixed_refs)
    height = mixed_refs[0].shape[0]

    @pl.when(pl.program_id(0) == 0)
    def _():
        for k, ref in enumerate(mixed_refs):
            at = lax.rem(place_ref[0] + count - k, count) * height
            rows_ref[pl.ds(pl.multiple_of(at, height), height), :] = ref[...]

    out_ref[0] = jnp.dot(rows_ref[...], weight_ref[0], preferred_element_type=F32).astype(
        out_ref.dtype
    )


def project(place, mixed, weight, dtype):
    height, depth = mixed[0].shape
    blocks, _, width = weight.shape
    rows = height * len(mixed)
    return pl.pallas_call(
        project_kernel,
        grid_spec=pltpu.PrefetchScalarGridSpec(
            num_scalar_prefetch=1,
            grid=(blocks // 2,),
            in_specs=[pl.BlockSpec((height, depth), lambda i, place: (0, 0))] * len(mixed)
            + [pl.BlockSpec((1, depth, width), lambda i, place: (place[1] + i, 0, 0))],
            out_specs=pl.BlockSpec((1, rows, width), lambda i, place: (i, 0, 0)),
            scratch_shapes=[pltpu.VMEM((rows, depth), BF16)],
        ),
        out_shape=jax.ShapeDtypeStruct((blocks // 2, rows, width), dtype),
        compiler_params=params(),
        name="project",
    )(place, *mixed, weight)


def per_device(nz, nx, ny, queries, new_kv, prefix_kv, suffix_kv, suffix_len, branch_prompt, out_weight):
    branches, steps, qwidth = queries.shape
    group = qwidth // HEAD_DIM
    height = steps * group
    cache, tensor = lax.axis_index("cache"), lax.axis_index("tensor")
    x, core = cache % nx, tensor % 2
    z_groups = [[z * nx + i for z in range(nz)] for i in range(nx)]
    y_groups = [[y * 2 + c for y in range(ny)] for c in range(2)]

    def along_x(value, k):
        pairs = [(z * nx + i, z * nx + (i + k) % nx) for z in range(nz) for i in range(nx)]
        return lax.ppermute(value, "cache", pairs)

    prompt_ids = branch_prompt[:, 0]
    weight = lax.all_gather(out_weight, "cache", axis_index_groups=z_groups)
    packed, q_rows = pack(prompt_ids, queries, group)
    mine = lax.all_to_all(packed, "cache", 0, 0, axis_index_groups=z_groups, tiled=True)
    mine = mine.reshape(nz * SLOTS * height, HEAD_DIM)
    sent = [along_x(mine, k) for k in range(1, nx)]
    fresh = jnp.pad(new_kv.transpose(0, 2, 1, 3), ((0, 0), (0, 0), (0, 16 - steps), (0, 0)))
    own, own_lse = suffix(suffix_len, q_rows, suffix_kv, fresh, steps)
    parts = [attend(mine, prefix_kv)]
    for k in range(1, nx):
        parts.append(along_x(attend(sent[k - 1], prefix_kv), nx - k))
    merged = merge(parts, nz)
    back = lax.all_to_all(merged, "cache", 0, 0, axis_index_groups=z_groups, tiled=True)
    home = (cache // nx).reshape(1)
    mixed = finish(prompt_ids, home, back, own, own_lse, steps, group)
    plane = [mixed] + [along_x(mixed, k) for k in range(1, nx)]
    half = nz // 2
    theirs = project(jnp.stack([x, (1 - core) * half]), plane, weight, BF16)
    theirs = lax.ppermute(theirs, "tensor", [(t, t ^ 1) for t in range(2 * ny)])
    ours = project(jnp.stack([x, core * half]), plane, weight, F32)
    pair = (ours + theirs.astype(F32)).astype(BF16)
    column = lax.all_to_all(pair, "tensor", 0, 0, axis_index_groups=y_groups, tiled=True)
    column = jnp.sum(column.astype(F32), axis=0).astype(BF16)
    nt = 2 * ny
    pairs = [
        ((z * nx + i) * nt + y * 2 + c, ((c * half + y) * nx + i) * nt + z)
        for z in range(nz)
        for i in range(nx)
        for y in range(ny)
        for c in range(2)
    ]
    result = lax.ppermute(column, ("cache", "tensor"), pairs)
    return result.reshape(-1, steps, result.shape[-1])


def solution(mesh):
    ncache, ntensor = mesh.shape["cache"], mesh.shape["tensor"]
    nz = PROMPTS
    return jax.shard_map(
        functools.partial(per_device, nz, ncache // nz, ntensor // 2),
        mesh=mesh,
        in_specs=(
            P("cache", None, "tensor"),
            P("cache", None, None, "tensor"),
            P(None, "cache", "tensor"),
            P("cache", None, None, "tensor"),
            P("cache"),
            P("cache", None),
            P("tensor", "cache"),
        ),
        out_specs=P("tensor", None, "cache"),
        check_vma=False,
    )
```

time: 377 us -> 124 us (0.33)
  waiting for transfers between devices: 194 us -> 16 us
  matrix products: 89.8 us -> 0 us
  Pallas kernels: 0 us -> 33 us
  other arithmetic: 18.8 us -> 0.26 us
  local copies, waits for them, and re-layouts: 23.1 us -> 8.49 us
  starting transfers between devices: 12.8 us -> 26.9 us
  blocking collectives: 19 us -> 23.6 us
    all_gather x2 -> x1, waiting for transfers between devices: 131 us -> 0.01 us  [per_device(): weight = lax.all_gather(out_weight, 'cache', axis_index_groups=z_groups)]
    dot_general x30 -> x0, matrix products: 89.8 us -> none  [the longest x12 42.4 us: visit(): jnp.einsum('acsghd,jgd->acsghj', query_heads, key_block, preferred_elemen...]
    pallas_call x0 -> x10, Pallas kernels: none -> 33 us  [the longest x4 23.9 us: attend(): pl.pallas_call(functools.partial(attend_kernel, length // block - 1, part...]
    reduce_scatter x1 -> x0, waiting for transfers between devices: 30.8 us -> none  [per_device(): lax.psum_scatter(partial_value.astype(jnp.bfloat16), 'tensor', scatter_di...]
    all_to_all x3 -> x1, waiting for transfers between devices: 31.4 us -> 4.18 us  [per_device(): lax.all_to_all(merged, 'cache', 0, 0, axis_index_groups=z_groups, tiled=T...]
    all_to_all x0 -> x2, blocking collectives: none -> 23.6 us  [the longest x1 15.8 us: per_device(): lax.all_to_all(packed, 'cache', 0, 0, axis_index_groups=z_groups, tiled=T...]
    ppermute x0 -> x11, starting transfers between devices: none -> 23.3 us  [the longest x9 10.4 us: along_x(): return lax.ppermute(value, 'cache', pairs)]
    unnamed x1 -> x0, blocking collectives: 19 us -> none
  transfers between devices with their start and end apart: 6 -> 13, of which waited for: 6 -> 5; matrix products, arithmetic and copies ran while one was open for 4% -> 1% of each run, Pallas kernels for 0% -> 26%
where the time goes in v1:
time: 124 us; the launch traced here: 122 us
  Pallas kernels  33 us (27%)
  starting transfers between devices  26.9 us (22%)
  blocking collectives  23.6 us (19%)
  waiting for transfers between devices  16 us (13%)
  between operations  13.7 us (11%)
  local copies, waits for them, and re-layouts  8.49 us (7%)
    pallas_call x4, Pallas kernels, attend(): pl.pallas_call(functools.partial(attend_kernel, length // block - 1, part...  23.9 us
    all_to_all x1, blocking collectives, per_device(): lax.all_to_all(packed, 'cache', 0, 0, axis_index_groups=z_groups, tiled=T...  15.8 us
    ppermute x9, starting transfers between devices, along_x(): return lax.ppermute(value, 'cache', pairs)  10.4 us
    all_to_all x1, blocking collectives, per_device(): lax.all_to_all(pair, 'tensor', 0, 0, axis_index_groups=y_groups, tiled=True)  7.81 us
    ppermute x1, starting transfers between devices, per_device(): theirs = lax.ppermute(theirs, 'tensor', [(t, t ^ 1) for t in range(2 * ny)])  7.45 us
    unnamed x17, local copies, waits for them, and re-layouts  6.97 us
    ppermute x1, waiting for transfers between devices, per_device(): result = lax.ppermute(column, ('cache', 'tensor'), pairs)  5.78 us
    ppermute x1, starting transfers between devices, per_device(): result = lax.ppermute(column, ('cache', 'tensor'), pairs)  5.44 us
  transfers between devices with their start and end apart: 13, of which 5 were waited for; matrix products, arithmetic and copies ran while one was open for 1% of the time, Pallas kernels for 26%

profile of v1, /device:TPU:17, one launch (start us, length us, event | category | flops | bytes accessed | tf_op | source)
XLA Modules:
  0.0 121.9 jit_solution(11806883746539289411)
XLA Ops:
  6.5 0.7 all-gather.3.cloned.1.call-update
  7.3 0.9 reshape.13.q_ref
  9.4 15.8 %all_to_all.15 = bf16[8,64,128]{2,1,0:T(8,128)(2,1)S(1)} all-to-all(bf16[8,64,128]{2,1,0:T(8,128)(2,1)S(1)} %get-tuple-element.9), channel_id=1, replica_groups={{0,32,64,96,128,160,192,224},{8,40,72,104,136,168,200,232},{16,48,80,11..., dimensions={0} | all-to-all | bytes 262144 | tf_op jit(solution)/shard_map/all_to_all | solution.py:302
  25.1 1.2 collective-permute-start
  26.3 1.5 %collective-permute-start.4 = (bf16[512,128]{1,0:T(8,128)(2,1)S(1)}, bf16[512,128]{1,0:T(8,128)(2,1)S(1)}, u32[]{:S(2)}, u32[]{:S(2)}) collective-permute-start(bf16[512,128]{1,0:T(8,128)(2,1)S(1)} %bitcast.13), channel_id=1, source_target_pairs={{0,24},{8,0},{16,8},{24,16},{32,56},{40,32},{48,40},{56,48},{64,88... | collective-permute-start | bytes 393224 | tf_op jit(solution)/shard_map/ppermute | solution.py:297
  27.8 1.5 %collective-permute-start.2 = (bf16[512,128]{1,0:T(8,128)(2,1)S(1)}, bf16[512,128]{1,0:T(8,128)(2,1)S(1)}, u32[]{:S(2)}, u32[]{:S(2)}) collective-permute-start(bf16[512,128]{1,0:T(8,128)(2,1)S(1)} %bitcast.14), channel_id=1, source_target_pairs={{0,16},{8,24},{16,0},{24,8},{32,48},{40,56},{48,32},{56,40},{64,80... | collective-permute-start | bytes 393224 | tf_op jit(solution)/shard_map/ppermute | solution.py:297
  29.3 1.2 collective-permute-done.q_ref
  30.6 1.9 %copy-done.6 = bf16[2,6144,128]{2,1,0:T(8,128)(2,1)S(1)} copy-done((bf16[2,6144,128]{2,1,0:T(8,128)(2,1)S(1)}, bf16[2,6144,128]{2,1,0:T(8,128)(2,1)}, u32[]{:S(2)}) %copy-start.6) | copy-done | bytes 3145752
  32.5 6.0 %prefix_attention.5 = bf16[144,512]{1,0:T(8,128)(2,1)S(1)} custom-call(bf16[512,128]{1,0:T(8,128)(2,1)S(1)} %collective-permute-done.q_ref, bf16[2,6144,128]{2,1,0:T(8,128)(2,1)S(1)} %copy-done.6), custom_call_target="tpu_custom_call" | custom-call | flops 3221225472 | bytes 3145728 | tf_op jit(solution)/shard_map/prefix_attention/pallas_call | solution.py:115
  38.5 1.3 %collective-permute-start.1 = (bf16[144,512]{1,0:T(8,128)(2,1)S(1)}, bf16[144,512]{1,0:T(8,128)(2,1)S(1)}, u32[]{:S(2)}, u32[]{:S(2)}) collective-permute-start(bf16[144,512]{1,0:T(8,128)(2,1)S(1)} %prefix_attention.5), channel_id=1, source_target_pairs={{0,24},{8,0},{16,8},{24,16},{32,56},{40,32},{48,40},{56,48},{64,88... | collective-permute-start | bytes 442376 | tf_op jit(solution)/shard_map/ppermute | solution.py:297
  39.8 6.0 %prefix_attention.6 = bf16[144,512]{1,0:T(8,128)(2,1)S(1)} custom-call(bf16[512,128]{1,0:T(8,128)(2,1)S(1)} %collective-permute-done.2.q_ref, bf16[2,6144,128]{2,1,0:T(8,128)(2,1)S(1)} %copy-done.6), custom_call_target="tpu_custom_call" | custom-call | flops 3221225472 | bytes 3145728 | tf_op jit(solution)/shard_map/prefix_attention/pallas_call | solution.py:115
  46.4 6.0 %prefix_attention.7 = bf16[144,512]{1,0:T(8,128)(2,1)S(1)} custom-call(bf16[512,128]{1,0:T(8,128)(2,1)S(1)} %collective-permute-done.4.q_ref, bf16[2,6144,128]{2,1,0:T(8,128)(2,1)S(1)} %copy-done.6), custom_call_target="tpu_custom_call" | custom-call | flops 3221225472 | bytes 3145728 | tf_op jit(solution)/shard_map/prefix_attention/pallas_call | solution.py:115
  52.4 0.7 collective-permute-start.5
  53.1 6.0 %prefix_attention.4.refs_0_ = bf16[144,512]{1,0:T(8,128)(2,1)S(1)} custom-call(bf16[512,128]{1,0:T(8,128)(2,1)S(1)} %bitcast.15, bf16[2,6144,128]{2,1,0:T(8,128)(2,1)S(1)} %copy-done.6), custom_call_target="tpu_custom_call" | custom-call | flops 3221225472 | bytes 3145728 | tf_op jit(solution)/shard_map/prefix_attention/pallas_call | solution.py:115
  59.1 0.9 merge_parts.1
  60.0 3.6 %all-to-all-start.1 = ((bf16[8,80,128]{2,1,0:T(8,128)(2,1)}), bf16[8,80,128]{2,1,0:T(8,128)(2,1)S(1)}, u32[]{:S(2)}, u32[]{:S(2)}) async-start(bf16[8,80,128]{2,1,0:T(8,128)(2,1)} %merge_parts.1), calls=%async_computation.1 | async-start | bytes 327680 | tf_op jit(solution)/shard_map/all_to_all | solution.py:311
  63.7 3.7 %suffix_attention.1 = (f32[8,32,128]{2,1,0:T(8,128)S(1)}, f32[8,32,128]{2,1,0:T(8,128)S(1)}) custom-call(s32[8]{0:T(128)S(1)} %copy-done.5, bf16[8,32,128]{2,1,0:T(8,128)(2,1)S(1)} %get-tuple-element.10.q_ref, bf16[8,2,512,128]{3,2,1,0:T(8,128)(2,1)S(1)} %copy-done.2, bf16[8,2,16,128]{3,2,1,0:T(8,128)(2,1)S(1)} %pad.4.new_ref), custom_call_target="tpu_custom_call" | custom-call | tf_op jit(solution)/shard_map/suffix_attention/pallas_call | solution.py:163
  67.4 4.2 %all-to-all-done.1.back_ref = bf16[8,80,128]{2,1,0:T(8,128)(2,1)S(1)} async-done(((bf16[8,80,128]{2,1,0:T(8,128)(2,1)}), bf16[8,80,128]{2,1,0:T(8,128)(2,1)S(1)}, u32[]{:S(2)}, u32[]{:S(2)}) %all-to-all-start.1) | async-done | bytes 163872 | tf_op jit(solution)/shard_map/all_to_all | solution.py:311
  71.6 0.8 finish_attention.1.refs_0_
  72.4 2.1 %collective-permute-start.8 = (bf16[32,1024]{1,0:T(8,128)(2,1)S(1)}, bf16[32,1024]{1,0:T(8,128)(2,1)S(1)}, u32[]{:S(2)}, u32[]{:S(2)}) collective-permute-start(bf16[32,1024]{1,0:T(8,128)(2,1)S(1)} %finish_attention.1.refs_0_), channel_id=1, source_target_pairs={{0,24},{8,0},{16,8},{24,16},{32,56},{40,32},{48,40},{56,48},{64,88... | collective-permute-start | bytes 196616 | tf_op jit(solution)/shard_map/ppermute | solution.py:297
  74.5 1.3 %collective-permute-start.7 = (bf16[32,1024]{1,0:T(8,128)(2,1)S(1)}, bf16[32,1024]{1,0:T(8,128)(2,1)S(1)}, u32[]{:S(2)}, u32[]{:S(2)}) collective-permute-start(bf16[32,1024]{1,0:T(8,128)(2,1)S(1)} %finish_attention.1.refs_0_), channel_id=1, source_target_pairs={{0,16},{8,24},{16,0},{24,8},{32,48},{40,56},{48,32},{56,40},{64,80... | collective-permute-start | bytes 196616 | tf_op jit(solution)/shard_map/ppermute | solution.py:297
  76.1 3.1 %collective-permute-done.7.refs_2_ = bf16[32,1024]{1,0:T(8,128)(2,1)S(1)} collective-permute-done((bf16[32,1024]{1,0:T(8,128)(2,1)S(1)}, bf16[32,1024]{1,0:T(8,128)(2,1)S(1)}, u32[]{:S(2)}, u32[]{:S(2)}) %collective-permute-start.7) | collective-permute-done | bytes 65568 | tf_op jit(solution)/shard_map/ppermute | solution.py:297
  79.1 1.0 collective-permute-done.6.refs_1_
  80.1 2.2 %copy-done = bf16[8192,256]{1,0:T(8,128)(2,1)S(1)} copy-done((bf16[8192,256]{1,0:T(8,128)(2,1)S(1)}, bf16[8192,256]{1,0:T(8,128)(2,1)}, u32[]{:S(2)}) %copy-start) | copy-done | bytes 4194328
  82.3 1.6 %project.3 = bf16[4,128,256]{2,1,0:T(8,128)(2,1)S(1)} custom-call(s32[2]{0:T(128)S(1)} %pad_add_fusion.1.place_ref, bf16[32,1024]{1,0:T(8,128)(2,1)S(1)} %finish_attention.1.refs_0_, bf16[32,1024]{1,0:T(8,128)(2,1)S(1)} %collective-permute-done.6.refs_1_, bf16[32,1024]{1,0:T(8,128)(2,1)S(1)} %collective-permute-done.7.refs_2_, ...), custom_call_target="tpu_custom_call" | custom-call | tf_op jit(solution)/shard_map/project/pallas_call | solution.py:270
  83.9 7.4 %collective-permute-start.9 = (bf16[4,128,256]{2,1,0:T(8,128)(2,1)S(1)}, bf16[4,128,256]{2,1,0:T(8,128)(2,1)S(1)}, u32[]{:S(2)}, u32[]{:S(2)}) collective-permute-start(bf16[4,128,256]{2,1,0:T(8,128)(2,1)S(1)} %project.3), channel_id=1, source_target_pairs={{0,1},{1,0},{2,3},{3,2},{4,5},{5,4},{6,7},{7,6},{8,9},{9,8},{10,11... | collective-permute-start | bytes 786440 | tf_op jit(solution)/shard_map/ppermute | solution.py:317
  91.4 2.2 %copy-done.1 = bf16[8192,256]{1,0:T(8,128)(2,1)S(1)} copy-done((bf16[8192,256]{1,0:T(8,128)(2,1)S(1)}, bf16[8192,256]{1,0:T(8,128)(2,1)}, u32[]{:S(2)}) %copy-start.1) | copy-done | bytes 4194328
  93.6 1.6 %project.2 = f32[4,128,256]{2,1,0:T(8,128)S(1)} custom-call(s32[2]{0:T(128)S(1)} %pad_add_fusion.place_ref, bf16[32,1024]{1,0:T(8,128)(2,1)S(1)} %finish_attention.1.refs_0_, bf16[32,1024]{1,0:T(8,128)(2,1)S(1)} %collective-permute-done.6.refs_1_, bf16[32,1024]{1,0:T(8,128)(2,1)S(1)} %collective-permute-done.7.refs_2_, ...), custom_call_target="tpu_custom_call" | custom-call | tf_op jit(solution)/shard_map/project/pallas_call | solution.py:270
  95.3 7.8 %all_to_all.16 = bf16[4,128,256]{2,1,0:T(8,128)(2,1)S(1)} all-to-all(bf16[4,128,256]{2,1,0:T(8,128)(2,1)S(1)} %add_convert_fusion), channel_id=1, replica_groups={{0,2,4,6},{1,3,5,7},{8,10,12,14},{9,11,13,15},{16,18,20,22},{17,19,21,2..., dimensions={0} | all-to-all | bytes 524288 | tf_op jit(solution)/shard_map/all_to_all | solution.py:320
  103.1 5.4 %collective-permute-start.10 = (bf16[128,256]{1,0:T(8,128)(2,1)S(1)}, bf16[128,256]{1,0:T(8,128)(2,1)S(1)}, u32[]{:S(2)}, u32[]{:S(2)}) collective-permute-start(bf16[128,256]{1,0:T(8,128)(2,1)S(1)} %reduce_sum.12), channel_id=1, source_target_pairs={{0,0},{1,128},{2,32},{3,160},{4,64},{5,192},{6,96},{7,224},{8,8},{... | collective-permute-start | bytes 196616 | tf_op jit(solution)/shard_map/ppermute | solution.py:330
  108.6 5.8 %collective-permute-done.10 = bf16[128,256]{1,0:T(8,128)(2,1)S(1)} collective-permute-done((bf16[128,256]{1,0:T(8,128)(2,1)S(1)}, bf16[128,256]{1,0:T(8,128)(2,1)S(1)}, u32[]{:S(2)}, u32[]{:S(2)}) %collective-permute-start.10) | collective-permute-done | bytes 65568 | tf_op jit(solution)/shard_map/ppermute | solution.py:330
  114.4 0.6 reshape.15
  (31 shorter events, 2.4 us)
Async XLA Ops:
  6.5 73.6 %all-gather.3.cloned.1.call-start = ((), (), s32[]{:S(2)}) async-start(), calls=%async_computation.3 | async-start | bytes 4718592 | tf_op jit(solution)/shard_map/all_gather | solution.py:300
  8.1 0.7 copy-start.3
  25.1 5.4 %collective-permute-start = (bf16[512,128]{1,0:T(8,128)(2,1)S(1)}, bf16[512,128]{1,0:T(8,128)(2,1)S(1)}, u32[]{:S(2)}, u32[]{:S(2)}) collective-permute-start(bf16[512,128]{1,0:T(8,128)(2,1)S(1)} %bitcast.12), channel_id=1, source_target_pairs={{0,8},{8,16},{16,24},{24,0},{32,40},{40,48},{48,56},{56,32},{64,72... | collective-permute-start | bytes 393224 | tf_op jit(solution)/shard_map/ppermute | solution.py:297
  26.3 20.0 %collective-permute-start.4 = (bf16[512,128]{1,0:T(8,128)(2,1)S(1)}, bf16[512,128]{1,0:T(8,128)(2,1)S(1)}, u32[]{:S(2)}, u32[]{:S(2)}) collective-permute-start(bf16[512,128]{1,0:T(8,128)(2,1)S(1)} %bitcast.13), channel_id=1, source_target_pairs={{0,24},{8,0},{16,8},{24,16},{32,56},{40,32},{48,40},{56,48},{64,88... | collective-permute-start | bytes 393224 | tf_op jit(solution)/shard_map/ppermute | solution.py:297
  27.8 12.0 %collective-permute-start.2 = (bf16[512,128]{1,0:T(8,128)(2,1)S(1)}, bf16[512,128]{1,0:T(8,128)(2,1)S(1)}, u32[]{:S(2)}, u32[]{:S(2)}) collective-permute-start(bf16[512,128]{1,0:T(8,128)(2,1)S(1)} %bitcast.14), channel_id=1, source_target_pairs={{0,16},{8,24},{16,0},{24,8},{32,48},{40,56},{48,32},{56,40},{64,80... | collective-permute-start | bytes 393224 | tf_op jit(solution)/shard_map/ppermute | solution.py:297
  30.6 1.9 %copy-start.6 = (bf16[2,6144,128]{2,1,0:T(8,128)(2,1)S(1)}, bf16[2,6144,128]{2,1,0:T(8,128)(2,1)}, u32[]{:S(2)}) copy-start(bf16[2,6144,128]{2,1,0:T(8,128)(2,1)} %kv_ref.8) | copy-start | bytes 9437188
  38.5 20.6 %collective-permute-start.1 = (bf16[144,512]{1,0:T(8,128)(2,1)S(1)}, bf16[144,512]{1,0:T(8,128)(2,1)S(1)}, u32[]{:S(2)}, u32[]{:S(2)}) collective-permute-start(bf16[144,512]{1,0:T(8,128)(2,1)S(1)} %prefix_attention.5), channel_id=1, source_target_pairs={{0,24},{8,0},{16,8},{24,16},{32,56},{40,32},{48,40},{56,48},{64,88... | collective-permute-start | bytes 442376 | tf_op jit(solution)/shard_map/ppermute | solution.py:297
  45.8 13.3 %collective-permute-start.3 = (bf16[144,512]{1,0:T(8,128)(2,1)S(1)}, bf16[144,512]{1,0:T(8,128)(2,1)S(1)}, u32[]{:S(2)}, u32[]{:S(2)}) collective-permute-start(bf16[144,512]{1,0:T(8,128)(2,1)S(1)} %prefix_attention.6), channel_id=1, source_target_pairs={{0,16},{8,24},{16,0},{24,8},{32,48},{40,56},{48,32},{56,40},{64,80... | collective-permute-start | bytes 442376 | tf_op jit(solution)/shard_map/ppermute | solution.py:297
  52.4 11.2 %copy-start.7 = (bf16[8,4,2,128]{3,2,1,0:T(2,128)(2,1)S(1)}, bf16[8,4,2,128]{3,2,1,0:T(2,128)(2,1)}, u32[]{:S(2)}) copy-start(bf16[8,4,2,128]{3,2,1,0:T(2,128)(2,1)} %param.8) | copy-start | bytes 49156
  52.4 11.3 %copy-start.2 = (bf16[8,2,512,128]{3,2,1,0:T(8,128)(2,1)S(1)}, bf16[8,2,512,128]{3,2,1,0:T(8,128)(2,1)}, u32[]{:S(2)}) copy-start(bf16[8,2,512,128]{3,2,1,0:T(8,128)(2,1)} %kv_ref.9) | copy-start | bytes 6291460
  52.4 11.3 %copy-start.5 = (s32[8]{0:T(128)S(1)}, s32[8]{0:T(128)}, u32[]{:S(2)}) copy-start(s32[8]{0:T(128)} %len_ref.1) | copy-start | bytes 100
  52.4 6.7 %collective-permute-start.5 = (bf16[144,512]{1,0:T(8,128)(2,1)S(1)}, bf16[144,512]{1,0:T(8,128)(2,1)S(1)}, u32[]{:S(2)}, u32[]{:S(2)}) collective-permute-start(bf16[144,512]{1,0:T(8,128)(2,1)S(1)} %prefix_attention.7), channel_id=1, source_target_pairs={{0,8},{8,16},{16,24},{24,0},{32,40},{40,48},{48,56},{56,32},{64,72... | collective-permute-start | bytes 442376 | tf_op jit(solution)/shard_map/ppermute | solution.py:297
  59.1 12.5 %copy-start.4 = (s32[8,1]{0,1:T(1,128)S(1)}, s32[8,1]{0,1:T(1,128)}, u32[]{:S(2)}) copy-start(s32[8,1]{0,1:T(1,128)} %param.12) | copy-start | bytes 100
  60.0 11.6 %all-to-all-start.1 = ((bf16[8,80,128]{2,1,0:T(8,128)(2,1)}), bf16[8,80,128]{2,1,0:T(8,128)(2,1)S(1)}, u32[]{:S(2)}, u32[]{:S(2)}) async-start(bf16[8,80,128]{2,1,0:T(8,128)(2,1)} %merge_parts.1), calls=%async_computation.1 | async-start | bytes 327680 | tf_op jit(solution)/shard_map/all_to_all | solution.py:311
  72.4 3.7 %collective-permute-start.8 = (bf16[32,1024]{1,0:T(8,128)(2,1)S(1)}, bf16[32,1024]{1,0:T(8,128)(2,1)S(1)}, u32[]{:S(2)}, u32[]{:S(2)}) collective-permute-start(bf16[32,1024]{1,0:T(8,128)(2,1)S(1)} %finish_attention.1.refs_0_), channel_id=1, source_target_pairs={{0,24},{8,0},{16,8},{24,16},{32,56},{40,32},{48,40},{56,48},{64,88... | collective-permute-start | bytes 196616 | tf_op jit(solution)/shard_map/ppermute | solution.py:297
  74.5 4.6 %collective-permute-start.7 = (bf16[32,1024]{1,0:T(8,128)(2,1)S(1)}, bf16[32,1024]{1,0:T(8,128)(2,1)S(1)}, u32[]{:S(2)}, u32[]{:S(2)}) collective-permute-start(bf16[32,1024]{1,0:T(8,128)(2,1)S(1)} %finish_attention.1.refs_0_), channel_id=1, source_target_pairs={{0,16},{8,24},{16,0},{24,8},{32,48},{40,56},{48,32},{56,40},{64,80... | collective-permute-start | bytes 196616 | tf_op jit(solution)/shard_map/ppermute | solution.py:297
  75.8 4.3 %collective-permute-start.6 = (bf16[32,1024]{1,0:T(8,128)(2,1)S(1)}, bf16[32,1024]{1,0:T(8,128)(2,1)S(1)}, u32[]{:S(2)}, u32[]{:S(2)}) collective-permute-start(bf16[32,1024]{1,0:T(8,128)(2,1)S(1)} %finish_attention.1.refs_0_), channel_id=1, source_target_pairs={{0,8},{8,16},{16,24},{24,0},{32,40},{40,48},{48,56},{56,32},{64,72... | collective-permute-start | bytes 196616 | tf_op jit(solution)/shard_map/ppermute | solution.py:297
  80.1 2.2 %copy-start = (bf16[8192,256]{1,0:T(8,128)(2,1)S(1)}, bf16[8192,256]{1,0:T(8,128)(2,1)}, u32[]{:S(2)}) copy-start(bf16[8192,256]{1,0:T(8,128)(2,1)} %all-gather.3.cloned.1.call-done) | copy-start | bytes 12582916
  83.9 11.3 %collective-permute-start.9 = (bf16[4,128,256]{2,1,0:T(8,128)(2,1)S(1)}, bf16[4,128,256]{2,1,0:T(8,128)(2,1)S(1)}, u32[]{:S(2)}, u32[]{:S(2)}) collective-permute-start(bf16[4,128,256]{2,1,0:T(8,128)(2,1)S(1)} %project.3), channel_id=1, source_target_pairs={{0,1},{1,0},{2,3},{3,2},{4,5},{5,4},{6,7},{7,6},{8,9},{9,8},{10,11... | collective-permute-start | bytes 786440 | tf_op jit(solution)/shard_map/ppermute | solution.py:317
  91.4 2.2 %copy-start.1 = (bf16[8192,256]{1,0:T(8,128)(2,1)S(1)}, bf16[8192,256]{1,0:T(8,128)(2,1)}, u32[]{:S(2)}) copy-start(bf16[8192,256]{1,0:T(8,128)(2,1)} %all-gather.3.cloned.1.call-done) | copy-start | bytes 12582916
  103.1 11.2 %collective-permute-start.10 = (bf16[128,256]{1,0:T(8,128)(2,1)S(1)}, bf16[128,256]{1,0:T(8,128)(2,1)S(1)}, u32[]{:S(2)}, u32[]{:S(2)}) collective-permute-start(bf16[128,256]{1,0:T(8,128)(2,1)S(1)} %reduce_sum.12), channel_id=1, source_target_pairs={{0,0},{1,128},{2,32},{3,160},{4,64},{5,192},{6,96},{7,224},{8,8},{... | collective-permute-start | bytes 196616 | tf_op jit(solution)/shard_map/ppermute | solution.py:330
Sparse Core Ops, SparseCore 0:
  9.1 57.6 all-gather.2

commit v2 on v1

--- a/solution.py
+++ b/solution.py
@@ -13,6 +13,8 @@
 SLOTS = 2
 LOG2E = 1.4426950408889634
 SCORE = LOG2E * HEAD_DIM ** (-0.5)
+PART = 512
+LARGE = 2.0**100
 VMEM_LIMIT = 48 * 1024 * 1024
 F32 = jnp.float32
 BF16 = jnp.bfloat16
@@ -40,12 +42,21 @@
     return high, middle, rest - middle
 
 
-def pack_kernel(branches, steps, group, prompt_ref, q_ref, packed_ref, rows_ref):
+def pack_kernel(
+    branches, steps, group, prompt_hbm, q_hbm, packed_ref, rows_ref, prompt_ref, q_ref, sem
+):
     height = steps * group
+    copies = [
+        pltpu.make_async_copy(prompt_hbm, prompt_ref, sem.at[0]),
+        pltpu.make_async_copy(q_hbm, q_ref, sem.at[1]),
+    ]
+    for copy in copies:
+        copy.start()
     packed_ref[...] = jnp.zeros_like(packed_ref)
-    q = q_ref[...].astype(F32)
+    for copy in copies:
+        copy.wait()
     for b in range(branches):
-        own = q[b * steps : (b + 1) * steps]
+        own = q_ref[b].astype(F32)
         rows = jnp.concatenate(
             [own[:, h * HEAD_DIM : (h + 1) * HEAD_DIM] for h in range(group)], axis=0
         ).astype(BF16)
@@ -59,67 +70,88 @@
     height = steps * group
     return pl.pallas_call(
         functools.partial(pack_kernel, branches, steps, group),
-        in_specs=[whole(pltpu.SMEM), whole()],
+        in_specs=[whole(pltpu.HBM), whole(pltpu.HBM)],
         out_specs=[whole(), whole()],
         out_shape=[
             jax.ShapeDtypeStruct((PROMPTS, SLOTS * height, HEAD_DIM), BF16),
             jax.ShapeDtypeStruct((branches, height, HEAD_DIM), BF16),
         ],
+        scratch_shapes=[
+            pltpu.SMEM((branches,), jnp.int32),
+            pltpu.VMEM(queries.shape, BF16),
+            pltpu.SemaphoreType.DMA((2,)),
+        ],
         compiler_params=params(),
         name="pack_queries",
-    )(prompt_ids, queries.reshape(branches * steps, -1))
-
-
-def attend_kernel(last, part, q_ref, kv_ref, out_ref, qt_ref, top_ref, total_ref, acc_ref):
-    i = pl.program_id(0)
-    rows = q_ref.shape[0]
-
-    @pl.when(i == 0)
-    def _():
-        qt_ref[...] = q_ref[...].T
-        top_ref[...] = jnp.full(top_ref.shape, -jnp.inf, F32)
-        total_ref[...] = jnp.zeros(total_ref.shape, F32)
-        acc_ref[...] = jnp.zeros(acc_ref.shape, F32)
-
-    top, total, acc = top_ref[...], total_ref[...], acc_ref[...]
-    for k in range(0, kv_ref.shape[1], part):
-        scores = jnp.dot(kv_ref[0, k : k + part, :], qt_ref[...], preferred_element_type=F32)
-        new_top = jnp.maximum(top, jnp.max(scores, axis=0, keepdims=True))
-        weights = jnp.exp2((scores - new_top) * SCORE)
-        fade = jnp.exp2((top - new_top) * SCORE)
-        total = total * fade + jnp.sum(weights, axis=0, keepdims=True)
-        acc = acc * fade + lax.dot_general(
-            kv_ref[1, k : k + part, :],
+    )(
+        pltpu.with_memory_space_constraint(prompt_ids, pltpu.HBM),
+        pltpu.with_memory_space_constraint(queries, pltpu.HBM),
+    )
+
+
+def attend_kernel(part, q_ref, kv_ref, out_ref, qt_ref, top_ref, total_ref, acc_ref):
+    rows, length = q_ref.shape[0], kv_ref.shape[1]
+    qt_ref[...] = q_ref[...].T
+
+    def scores_of(k):
+        return jnp.dot(kv_ref[0, pl.ds(k, part), :], qt_ref[...], preferred_element_type=F32)
+
+    def sums_of(k, weights):
+        return lax.dot_general(
+            kv_ref[1, pl.ds(k, part), :],
             weights.astype(BF16),
             (((0,), (0,)), ((), ())),
             preferred_element_type=F32,
         )
-        top = new_top
+
+    following = scores_of(0)
+    top = jnp.max(following, axis=0, keepdims=True)
+    total = jnp.zeros((8, rows), F32)
+    acc = jnp.zeros((HEAD_DIM, rows), F32)
+    for k in range(0, length, part):
+        scores = following
+        if k + part < length:
+            following = scores_of(k + part)
+        weights = jnp.exp2((scores - top) * SCORE)
+        total = total + jnp.sum(weights.reshape(part // 8, 8, rows), axis=0)
+        acc = acc + sums_of(k, weights)
+    total = jnp.sum(total, axis=0, keepdims=True)
     top_ref[...], total_ref[...], acc_ref[...] = top, total, acc
 
-    @pl.when(i == last)
+    @pl.when(jnp.logical_not(jnp.max(total) < LARGE))
     def _():
-        total = total_ref[...]
-        out_ref[0:HEAD_DIM, :] = (acc_ref[...] / total).astype(BF16)
-        terms = three_terms(top_ref[...] * SCORE + jnp.log2(total))
-        row = lax.broadcasted_iota(jnp.int32, (16, rows), 0)
-        stats = jnp.zeros((16, rows), F32)
-        for j in range(3):
-            stats = jnp.where(row == j, terms[j], stats)
-        out_ref[HEAD_DIM : HEAD_DIM + 16, :] = stats.astype(BF16)
+        top_ref[...] = jnp.full((1, rows), -jnp.inf, F32)
+        total_ref[...] = jnp.zeros((1, rows), F32)
+        acc_ref[...] = jnp.zeros((HEAD_DIM, rows), F32)
+
+        @pl.loop(0, length // part)
+        def _(i):
+            k = pl.multiple_of(i * part, part)
+            scores = scores_of(k)
+            top = top_ref[...]
+            new_top = jnp.maximum(top, jnp.max(scores, axis=0, keepdims=True))
+            weights = jnp.exp2((scores - new_top) * SCORE)
+            fade = jnp.exp2((top - new_top) * SCORE)
+            total_ref[...] = total_ref[...] * fade + jnp.sum(weights, axis=0, keepdims=True)
+            acc_ref[...] = acc_ref[...] * fade + sums_of(k, weights)
+            top_ref[...] = new_top
+
+    total = total_ref[...]
+    out_ref[0:HEAD_DIM, :] = (acc_ref[...] / total).astype(BF16)
+    terms = three_terms(top_ref[...] * SCORE + jnp.log2(total))
+    row = lax.broadcasted_iota(jnp.int32, (16, rows), 0)
+    stats = jnp.zeros((16, rows), F32)
+    for j in range(3):
+        stats = jnp.where(row == j, terms[j], stats)
+    out_ref[HEAD_DIM : HEAD_DIM + 16, :] = stats.astype(BF16)
 
 
 def attend(q, kv):
     rows, length = q.shape[0], kv.shape[1]
-    block, part = 2048, 1024
-    return pl.pallas_call(
-        functools.partial(attend_kernel, length // block - 1, part),
-        grid=(length // block,),
-        in_specs=[
-            pl.BlockSpec((rows, HEAD_DIM), lambda i: (0, 0)),
-            pl.BlockSpec((2, block, HEAD_DIM), lambda i: (0, i, 0)),
-        ],
-        out_specs=pl.BlockSpec((HEAD_DIM + 16, rows), lambda i: (0, 0)),
+    return pl.pallas_call(
+        functools.partial(attend_kernel, PART),
+        in_specs=[whole(), whole()],
+        out_specs=whole(),
         out_shape=jax.ShapeDtypeStruct((HEAD_DIM + 16, rows), BF16),
         scratch_shapes=[
             pltpu.VMEM((HEAD_DIM, rows), BF16),
@@ -247,40 +279,84 @@
     )(prompt_ids, home, back, own, lse)
 
 
+def load_kernel(count, source_ref, out_ref, sem):
+    size = source_ref.shape[0] // count
+    copies = [
+        pltpu.make_async_copy(
+            source_ref.at[pl.ds(i * size, size)], out_ref.at[pl.ds(i * size, size)], sem.at[i]
+        )
+        for i in range(count)
+    ]
+    for copy in copies:
+        copy.start()
+    for copy in copies:
+        copy.wait()
+
+
+def load(value, count):
+    return pl.pallas_call(
+        functools.partial(load_kernel, count),
+        in_specs=[whole(pl.ANY)],
+        out_specs=whole(),
+        out_shape=pltpu.VMEM(value.shape, value.dtype),
+        scratch_shapes=[pltpu.SemaphoreType.DMA((count,))],
+        compiler_params=params(),
+        cost_estimate=pl.CostEstimate(
+            flops=0, transcendentals=0, bytes_accessed=2 * value.size * value.dtype.itemsize
+        ),
+        name="load",
+    )(value)
+
+
 def project_kernel(place_ref, *refs):
-    *mixed_refs, weight_ref, out_ref, rows_ref = refs
+    *mixed_refs, weight_ref, theirs_ref, ours_ref, rows_ref = refs
     count = len(mixed_refs)
     height = mixed_refs[0].shape[0]
-
-    @pl.when(pl.program_id(0) == 0)
-    def _():
-        for k, ref in enumerate(mixed_refs):
-            at = lax.rem(place_ref[0] + count - k, count) * height
-            rows_ref[pl.ds(pl.multiple_of(at, height), height), :] = ref[...]
-
-    out_ref[0] = jnp.dot(rows_ref[...], weight_ref[0], preferred_element_type=F32).astype(
-        out_ref.dtype
-    )
-
-
-def project(place, mixed, weight, dtype):
+    for k, ref in enumerate(mixed_refs):
+        at = lax.rem(place_ref[0] + count - k, count) * height
+        rows_ref[pl.ds(pl.multiple_of(at, height), height), :] = ref[...]
+    half = ours_ref.shape[0]
+    core, odd = place_ref[1], place_ref[2]
+    for out_ref, first in ((theirs_ref, (1 - core) * half), (ours_ref, core * half)):
+        for i in range(half):
+            block = first + lax.rem(i + odd * (half // 2), half)
+            out_ref[i] = jnp.dot(
+                rows_ref[...], weight_ref[block], preferred_element_type=F32
+            ).astype(out_ref.dtype)
+
+
+def project(place, mixed, weight):
     height, depth = mixed[0].shape
     blocks, _, width = weight.shape
     rows = height * len(mixed)
+    shape = (blocks // 2, rows, width)
     return pl.pallas_call(
         project_kernel,
-        grid_spec=pltpu.PrefetchScalarGridSpec(
-            num_scalar_prefetch=1,
-            grid=(blocks // 2,),
-            in_specs=[pl.BlockSpec((height, depth), lambda i, place: (0, 0))] * len(mixed)
-            + [pl.BlockSpec((1, depth, width), lambda i, place: (place[1] + i, 0, 0))],
-            out_specs=pl.BlockSpec((1, rows, width), lambda i, place: (i, 0, 0)),
-            scratch_shapes=[pltpu.VMEM((rows, depth), BF16)],
-        ),
-        out_shape=jax.ShapeDtypeStruct((blocks // 2, rows, width), dtype),
+        in_specs=[whole(pltpu.SMEM)] + [whole()] * (len(mixed) + 1),
+        out_specs=[whole(), whole()],
+        out_shape=[jax.ShapeDtypeStruct(shape, BF16), jax.ShapeDtypeStruct(shape, F32)],
+        scratch_shapes=[pltpu.VMEM((rows, depth), BF16)],
         compiler_params=params(),
         name="project",
     )(place, *mixed, weight)
+
+
+def sum_kernel(*refs):
+    *piece_refs, out_ref = refs
+    total = sum(ref[...].astype(F32) for ref in piece_refs)
+    out_ref[...] = total.reshape(out_ref.shape).astype(BF16)
+
+
+def sum_pieces(pieces, steps):
+    rows, width = pieces[0].shape
+    return pl.pallas_call(
+        sum_kernel,
+        in_specs=[whole()] * len(pieces),
+        out_specs=whole(),
+        out_shape=jax.ShapeDtypeStruct((rows // steps, steps, width), BF16),
+        compiler_params=params(),
+        name="sum_pieces",
+    )(*pieces)
 
 
 def per_device(nz, nx, ny, queries, new_kv, prefix_kv, suffix_kv, suffix_len, branch_prompt, out_weight):
@@ -288,47 +364,52 @@
     group = qwidth // HEAD_DIM
     height = steps * group
     cache, tensor = lax.axis_index("cache"), lax.axis_index("tensor")
-    x, core = cache % nx, tensor % 2
+    x, y, core = cache % nx, tensor // 2, tensor % 2
     z_groups = [[z * nx + i for z in range(nz)] for i in range(nx)]
-    y_groups = [[y * 2 + c for y in range(ny)] for c in range(2)]
 
     def along_x(value, k):
         pairs = [(z * nx + i, z * nx + (i + k) % nx) for z in range(nz) for i in range(nx)]
         return lax.ppermute(value, "cache", pairs)
 
     prompt_ids = branch_prompt[:, 0]
+    packed, q_rows = pack(prompt_ids, queries, group)
     weight = lax.all_gather(out_weight, "cache", axis_index_groups=z_groups)
-    packed, q_rows = pack(prompt_ids, queries, group)
     mine = lax.all_to_all(packed, "cache", 0, 0, axis_index_groups=z_groups, tiled=True)
+    kv = load(prefix_kv, 2)
+    mine, kv = lax.optimization_barrier((mine, kv))
     mine = mine.reshape(nz * SLOTS * height, HEAD_DIM)
     sent = [along_x(mine, k) for k in range(1, nx)]
     fresh = jnp.pad(new_kv.transpose(0, 2, 1, 3), ((0, 0), (0, 0), (0, 16 - steps), (0, 0)))
     own, own_lse = suffix(suffix_len, q_rows, suffix_kv, fresh, steps)
-    parts = [attend(mine, prefix_kv)]
+    parts = [attend(mine, kv)]
     for k in range(1, nx):
-        parts.append(along_x(attend(sent[k - 1], prefix_kv), nx - k))
+        parts.append(along_x(attend(sent[k - 1], kv), nx - k))
     merged = merge(parts, nz)
     back = lax.all_to_all(merged, "cache", 0, 0, axis_index_groups=z_groups, tiled=True)
     home = (cache // nx).reshape(1)
     mixed = finish(prompt_ids, home, back, own, own_lse, steps, group)
     plane = [mixed] + [along_x(mixed, k) for k in range(1, nx)]
     half = nz // 2
-    theirs = project(jnp.stack([x, (1 - core) * half]), plane, weight, BF16)
+    theirs, ours = project(jnp.stack([x, core, y % 2]), plane, load(weight, nz))
     theirs = lax.ppermute(theirs, "tensor", [(t, t ^ 1) for t in range(2 * ny)])
-    ours = project(jnp.stack([x, core * half]), plane, weight, F32)
-    pair = (ours + theirs.astype(F32)).astype(BF16)
-    column = lax.all_to_all(pair, "tensor", 0, 0, axis_index_groups=y_groups, tiled=True)
-    column = jnp.sum(column.astype(F32), axis=0).astype(BF16)
-    nt = 2 * ny
-    pairs = [
-        ((z * nx + i) * nt + y * 2 + c, ((c * half + y) * nx + i) * nt + z)
-        for z in range(nz)
-        for i in range(nx)
-        for y in range(ny)
-        for c in range(2)
-    ]
-    result = lax.ppermute(column, ("cache", "tensor"), pairs)
-    return result.reshape(-1, steps, result.shape[-1])
+    keep = ours[:2] + theirs[:2].astype(F32)
+    give = (ours[2:] + theirs[2:].astype(F32)).astype(BF16)
+    keep = (keep + lax.ppermute(give, "tensor", [(t, t ^ 2) for t in range(2 * ny)])).astype(BF16)
+    pieces = []
+    for k in range(2):
+        pairs = [
+            (
+                ((z * nx + i) * ny + j) * 2 + c,
+                ((c * half + (j % 2) * 2 + (k + j // 2) % 2) * nx + i) * 2 * ny + z,
+            )
+            for z in range(nz)
+            for i in range(nx)
+            for j in range(ny)
+            for c in range(2)
+        ]
+        block = lax.dynamic_index_in_dim(keep, (k + y // 2) % 2, 0, keepdims=False)
+        pieces.append(lax.ppermute(block, ("cache", "tensor"), pairs))
+    return sum_pieces(pieces, steps)
 
 
 def solution(mesh):

time: 124 us -> 134 us (1.081); the launches traced: 122 us -> 134 us
  blocking collectives: 23.6 us -> 0 us
  Pallas kernels: 33 us -> 56 us
  starting transfers between devices: 26.9 us -> 39.9 us
  local copies, waits for them, and re-layouts: 8.49 us -> 1.64 us
  waiting for transfers between devices: 16 us -> 22.1 us
    all_to_all x2 -> x0, blocking collectives: 23.6 us -> none  [the longest x1 15.8 us: per_device(): lax.all_to_all(packed, 'cache', 0, 0, axis_index_groups=z_groups, tiled=T...]
    pallas_call x6 -> x8, Pallas kernels: 27.1 us -> 49.1 us  [the longest x4 43 us: attend(): pl.pallas_call(functools.partial(attend_kernel, PART), in_specs=[whole(),...]
    all_to_all x0 -> x1, starting transfers between devices: none -> 8.2 us  [per_device(): lax.all_to_all(packed, 'cache', 0, 0, axis_index_groups=z_groups, tiled=T...]
    all_to_all x0 -> x1, waiting for transfers between devices: none -> 5.87 us  [per_device(): lax.all_to_all(packed, 'cache', 0, 0, axis_index_groups=z_groups, tiled=T...]
    unnamed x17 -> x9, local copies, waits for them, and re-layouts: 6.97 us -> 1.61 us
    ppermute x1 -> x3, starting transfers between devices: 5.44 us -> 10.2 us  [the longest x2 9.15 us: per_device(): pieces.append(lax.ppermute(block, ('cache', 'tensor'), pairs))]
    ppermute x1 -> x3, waiting for transfers between devices: 5.78 us -> 8.61 us  [the longest x2 4.91 us: per_device(): pieces.append(lax.ppermute(block, ('cache', 'tensor'), pairs))]
    ppermute x9, waiting for transfers between devices: 5.28 us -> 3.04 us  [along_x(): return lax.ppermute(value, 'cache', pairs)]
  transfers between devices with their start and end apart: 13 -> 16, of which waited for: 5 -> 8; matrix products, arithmetic and copies ran while one was open for 1% -> 0% of each run, Pallas kernels for 26% -> 41%
where the time goes in v2:
time: 134 us
  Pallas kernels  56 us (42%)
  starting transfers between devices  39.9 us (30%)
  waiting for transfers between devices  22.1 us (16%)
  between operations  13.7 us (10%)
  local copies, waits for them, and re-layouts  1.64 us (1%)
    pallas_call x4, Pallas kernels, attend(): pl.pallas_call(functools.partial(attend_kernel, PART), in_specs=[whole(),...  43 us
    ppermute x9, starting transfers between devices, along_x(): return lax.ppermute(value, 'cache', pairs)  10.6 us
    ppermute x2, starting transfers between devices, per_device(): pieces.append(lax.ppermute(block, ('cache', 'tensor'), pairs))  9.15 us
    all_to_all x1, starting transfers between devices, per_device(): lax.all_to_all(packed, 'cache', 0, 0, axis_index_groups=z_groups, tiled=T...  8.2 us
    ppermute x1, starting transfers between devices, per_device(): theirs = lax.ppermute(theirs, 'tensor', [(t, t ^ 1) for t in range(2 * ny)])  7.47 us
    all_to_all x1, waiting for transfers between devices, per_device(): lax.all_to_all(packed, 'cache', 0, 0, axis_index_groups=z_groups, tiled=T...  5.87 us
    ppermute x2, waiting for transfers between devices, per_device(): pieces.append(lax.ppermute(block, ('cache', 'tensor'), pairs))  4.91 us
    pallas_call x2, Pallas kernels, load(): pl.pallas_call(functools.partial(load_kernel, count), in_specs=[whole(pl....  4.11 us
  transfers between devices with their start and end apart: 16, of which 8 were waited for; matrix products, arithmetic and copies ran while one was open for 0% of the time, Pallas kernels for 41%

profile of v2, /device:TPU:17, one launch (start us, length us, event | category | flops | bytes accessed | tf_op | source)
XLA Modules:
  0.0 133.5 jit_solution(1443023315431942195)
XLA Ops:
  7.3 1.6 %pack_queries.1 = (bf16[8,64,128]{2,1,0:T(8,128)(2,1)}, bf16[8,32,128]{2,1,0:T(8,128)(2,1)S(1)}) custom-call(s32[8]{0:T(128)} %bitcast.18, bf16[8,4,1024]{2,1,0:T(4,128)(2,1)} %q_hbm.1), custom_call_target="tpu_custom_call" | custom-call | tf_op jit(solution)/shard_map/pack_queries/pallas_call | solution.py:71
  8.8 8.2 %all-to-all-start = ((bf16[8,64,128]{2,1,0:T(8,128)(2,1)}), bf16[8,64,128]{2,1,0:T(8,128)(2,1)S(1)}, u32[]{:S(2)}, u32[]{:S(2)}) async-start(bf16[8,64,128]{2,1,0:T(8,128)(2,1)} %get-tuple-element.13), calls=%async_computation | async-start | bytes 262144 | tf_op jit(solution)/shard_map/all_to_all | solution.py:377
  17.0 1.9 %load.2.kv_ref = bf16[2,6144,128]{2,1,0:T(8,128)(2,1)S(1)} custom-call(bf16[2,6144,128]{2,1,0:T(8,128)(2,1)} %source_ref.1), custom_call_target="tpu_custom_call" | custom-call | bytes 6291456 | tf_op jit(solution)/shard_map/load/pallas_call | solution.py:297
  18.9 5.9 %all-to-all-done = bf16[8,64,128]{2,1,0:T(8,128)(2,1)S(1)} async-done(((bf16[8,64,128]{2,1,0:T(8,128)(2,1)}), bf16[8,64,128]{2,1,0:T(8,128)(2,1)S(1)}, u32[]{:S(2)}, u32[]{:S(2)}) %all-to-all-start) | async-done | bytes 131104 | tf_op jit(solution)/shard_map/all_to_all | solution.py:377
  24.8 1.2 collective-permute-start
  26.0 1.5 %collective-permute-start.4 = (bf16[512,128]{1,0:T(8,128)(2,1)S(1)}, bf16[512,128]{1,0:T(8,128)(2,1)S(1)}, u32[]{:S(2)}, u32[]{:S(2)}) collective-permute-start(bf16[512,128]{1,0:T(8,128)(2,1)S(1)} %bitcast.15), channel_id=1, source_target_pairs={{0,24},{8,0},{16,8},{24,16},{32,56},{40,32},{48,40},{56,48},{64,88... | collective-permute-start | bytes 393224 | tf_op jit(solution)/shard_map/ppermute | solution.py:372
  27.5 1.5 %collective-permute-start.2 = (bf16[512,128]{1,0:T(8,128)(2,1)S(1)}, bf16[512,128]{1,0:T(8,128)(2,1)S(1)}, u32[]{:S(2)}, u32[]{:S(2)}) collective-permute-start(bf16[512,128]{1,0:T(8,128)(2,1)S(1)} %bitcast.16), channel_id=1, source_target_pairs={{0,16},{8,24},{16,0},{24,8},{32,48},{40,56},{48,32},{56,40},{64,80... | collective-permute-start | bytes 393224 | tf_op jit(solution)/shard_map/ppermute | solution.py:372
  29.0 1.2 collective-permute-done.q_ref
  30.2 10.8 %prefix_attention.5 = bf16[144,512]{1,0:T(8,128)(2,1)S(1)} custom-call(bf16[512,128]{1,0:T(8,128)(2,1)S(1)} %collective-permute-done.q_ref, bf16[2,6144,128]{2,1,0:T(8,128)(2,1)S(1)} %load.2.kv_ref), custom_call_target="tpu_custom_call" | custom-call | flops 3221225472 | bytes 3145728 | tf_op jit(solution)/shard_map/prefix_attention/pallas_call | solution.py:151
  41.0 1.3 %collective-permute-start.1 = (bf16[144,512]{1,0:T(8,128)(2,1)S(1)}, bf16[144,512]{1,0:T(8,128)(2,1)S(1)}, u32[]{:S(2)}, u32[]{:S(2)}) collective-permute-start(bf16[144,512]{1,0:T(8,128)(2,1)S(1)} %prefix_attention.5), channel_id=1, source_target_pairs={{0,24},{8,0},{16,8},{24,16},{32,56},{40,32},{48,40},{56,48},{64,88... | collective-permute-start | bytes 442376 | tf_op jit(solution)/shard_map/ppermute | solution.py:372
  42.3 10.7 %prefix_attention.6 = bf16[144,512]{1,0:T(8,128)(2,1)S(1)} custom-call(bf16[512,128]{1,0:T(8,128)(2,1)S(1)} %collective-permute-done.2.q_ref, bf16[2,6144,128]{2,1,0:T(8,128)(2,1)S(1)} %load.2.kv_ref), custom_call_target="tpu_custom_call" | custom-call | flops 3221225472 | bytes 3145728 | tf_op jit(solution)/shard_map/prefix_attention/pallas_call | solution.py:151
  53.1 0.8 collective-permute-start.3
  53.9 10.8 %prefix_attention.7 = bf16[144,512]{1,0:T(8,128)(2,1)S(1)} custom-call(bf16[512,128]{1,0:T(8,128)(2,1)S(1)} %collective-permute-done.4.q_ref, bf16[2,6144,128]{2,1,0:T(8,128)(2,1)S(1)} %load.2.kv_ref), custom_call_target="tpu_custom_call" | custom-call | flops 3221225472 | bytes 3145728 | tf_op jit(solution)/shard_map/prefix_attention/pallas_call | solution.py:151
  65.4 10.8 %prefix_attention.4.refs_0_ = bf16[144,512]{1,0:T(8,128)(2,1)S(1)} custom-call(bf16[512,128]{1,0:T(8,128)(2,1)S(1)} %bitcast.17, bf16[2,6144,128]{2,1,0:T(8,128)(2,1)S(1)} %load.2.kv_ref), custom_call_target="tpu_custom_call" | custom-call | flops 3221225472 | bytes 3145728 | tf_op jit(solution)/shard_map/prefix_attention/pallas_call | solution.py:151
  76.2 0.9 merge_parts.1
  77.0 3.4 %all-to-all-start.1 = ((bf16[8,80,128]{2,1,0:T(8,128)(2,1)}), bf16[8,80,128]{2,1,0:T(8,128)(2,1)S(1)}, u32[]{:S(2)}, u32[]{:S(2)}) async-start(bf16[8,80,128]{2,1,0:T(8,128)(2,1)} %merge_parts.1), calls=%async_computation.1 | async-start | bytes 327680 | tf_op jit(solution)/shard_map/all_to_all | solution.py:388
  80.6 1.6 %copy-done = bf16[8,2,512,128]{3,2,1,0:T(8,128)(2,1)S(1)} copy-done((bf16[8,2,512,128]{3,2,1,0:T(8,128)(2,1)S(1)}, bf16[8,2,512,128]{3,2,1,0:T(8,128)(2,1)}, u32[]{:S(2)}) %copy-start) | copy-done | bytes 2097176
  82.2 3.7 %suffix_attention.1 = (f32[8,32,128]{2,1,0:T(8,128)S(1)}, f32[8,32,128]{2,1,0:T(8,128)S(1)}) custom-call(s32[8]{0:T(128)S(1)} %copy-done.2, bf16[8,32,128]{2,1,0:T(8,128)(2,1)S(1)} %get-tuple-element.16.q_ref, bf16[8,2,512,128]{3,2,1,0:T(8,128)(2,1)S(1)} %copy-done, bf16[8,2,16,128]{3,2,1,0:T(8,128)(2,1)S(1)} %pad.4.new_ref), custom_call_target="tpu_custom_call" | custom-call | tf_op jit(solution)/shard_map/suffix_attention/pallas_call | solution.py:195
  85.9 2.7 %all-to-all-done.1.back_ref = bf16[8,80,128]{2,1,0:T(8,128)(2,1)S(1)} async-done(((bf16[8,80,128]{2,1,0:T(8,128)(2,1)}), bf16[8,80,128]{2,1,0:T(8,128)(2,1)S(1)}, u32[]{:S(2)}, u32[]{:S(2)}) %all-to-all-start.1) | async-done | bytes 163872 | tf_op jit(solution)/shard_map/all_to_all | solution.py:388
  89.4 2.1 %collective-permute-start.8 = (bf16[32,1024]{1,0:T(8,128)(2,1)S(1)}, bf16[32,1024]{1,0:T(8,128)(2,1)S(1)}, u32[]{:S(2)}, u32[]{:S(2)}) collective-permute-start(bf16[32,1024]{1,0:T(8,128)(2,1)S(1)} %finish_attention.1.refs_0_), channel_id=1, source_target_pairs={{0,24},{8,0},{16,8},{24,16},{32,56},{40,32},{48,40},{56,48},{64,88... | collective-permute-start | bytes 196616 | tf_op jit(solution)/shard_map/ppermute | solution.py:372
  91.6 1.2 collective-permute-start.7
  93.1 2.2 %load.3.refs_4_ = bf16[8,1024,256]{2,1,0:T(8,128)(2,1)S(1)} custom-call(bf16[8,1024,256]{2,1,0:T(8,128)(2,1)} %bitcast.20), custom_call_target="tpu_custom_call" | custom-call | bytes 8388608 | tf_op jit(solution)/shard_map/load/pallas_call | solution.py:297
  95.3 0.9 collective-permute-done.7.refs_2_
  96.2 0.9 collective-permute-done.6.refs_1_
  97.1 1.3 project.1
  98.4 7.5 %collective-permute-start.9 = (bf16[4,128,256]{2,1,0:T(8,128)(2,1)S(1)}, bf16[4,128,256]{2,1,0:T(8,128)(2,1)S(1)}, u32[]{:S(2)}, u32[]{:S(2)}) collective-permute-start(bf16[4,128,256]{2,1,0:T(8,128)(2,1)S(1)} %get-tuple-element.20), channel_id=1, source_target_pairs={{0,1},{1,0},{2,3},{3,2},{4,5},{5,4},{6,7},{7,6},{8,9},{9,8},{10,11... | collective-permute-start | bytes 786440 | tf_op jit(solution)/shard_map/ppermute | solution.py:394
  105.9 1.2 collective-permute-done.9
  107.1 1.1 collective-permute-start.10
  108.1 3.7 %collective-permute-done.10 = bf16[2,128,256]{2,1,0:T(8,128)(2,1)S(1)} collective-permute-done((bf16[2,128,256]{2,1,0:T(8,128)(2,1)S(1)}, bf16[2,128,256]{2,1,0:T(8,128)(2,1)S(1)}, u32[]{:S(2)}, u32[]{:S(2)}) %collective-permute-start.10) | collective-permute-done | bytes 131104 | tf_op jit(solution)/shard_map/ppermute | solution.py:397
  111.9 2.6 %collective-permute-start.12 = (bf16[128,256]{1,0:T(8,128)(2,1)S(1)}, bf16[128,256]{1,0:T(8,128)(2,1)S(1)}, u32[]{:S(2)}, u32[]{:S(2)}) collective-permute-start(bf16[128,256]{1,0:T(8,128)(2,1)S(1)} %get-tuple-element.21), channel_id=1, source_target_pairs={{0,32},{1,160},{2,96},{3,224},{4,0},{5,128},{6,64},{7,192},{8,40},... | collective-permute-start | bytes 196616 | tf_op jit(solution)/shard_map/ppermute | solution.py:411
  114.5 6.6 %collective-permute-start.11 = (bf16[128,256]{1,0:T(8,128)(2,1)S(1)}, bf16[128,256]{1,0:T(8,128)(2,1)S(1)}, u32[]{:S(2)}, u32[]{:S(2)}) collective-permute-start(bf16[128,256]{1,0:T(8,128)(2,1)S(1)} %get-tuple-element.22), channel_id=1, source_target_pairs={{0,0},{1,128},{2,64},{3,192},{4,32},{5,160},{6,96},{7,224},{8,8},{... | collective-permute-start | bytes 196616 | tf_op jit(solution)/shard_map/ppermute | solution.py:411
  121.1 4.9 %collective-permute-done.11.refs_0_ = bf16[128,256]{1,0:T(8,128)(2,1)S(1)} collective-permute-done((bf16[128,256]{1,0:T(8,128)(2,1)S(1)}, bf16[128,256]{1,0:T(8,128)(2,1)S(1)}, u32[]{:S(2)}, u32[]{:S(2)}) %collective-permute-start.11) | collective-permute-done | bytes 65568 | tf_op jit(solution)/shard_map/ppermute | solution.py:411
  (27 shorter events, 3.3 us)
Async XLA Ops:
  6.5 86.5 %all-gather.3.cloned.1.call-start = ((), (), s32[]{:S(2)}) async-start(), calls=%async_computation.2 | async-start | bytes 4718592 | tf_op jit(solution)/shard_map/all_gather | solution.py:376
  8.8 16.0 %all-to-all-start = ((bf16[8,64,128]{2,1,0:T(8,128)(2,1)}), bf16[8,64,128]{2,1,0:T(8,128)(2,1)S(1)}, u32[]{:S(2)}, u32[]{:S(2)}) async-start(bf16[8,64,128]{2,1,0:T(8,128)(2,1)} %get-tuple-element.13), calls=%async_computation | async-start | bytes 262144 | tf_op jit(solution)/shard_map/all_to_all | solution.py:377
  24.8 5.4 %collective-permute-start = (bf16[512,128]{1,0:T(8,128)(2,1)S(1)}, bf16[512,128]{1,0:T(8,128)(2,1)S(1)}, u32[]{:S(2)}, u32[]{:S(2)}) collective-permute-start(bf16[512,128]{1,0:T(8,128)(2,1)S(1)} %bitcast.14), channel_id=1, source_target_pairs={{0,8},{8,16},{16,24},{24,0},{32,40},{40,48},{48,56},{56,32},{64,72... | collective-permute-start | bytes 393224 | tf_op jit(solution)/shard_map/ppermute | solution.py:372
  26.0 27.9 %collective-permute-start.4 = (bf16[512,128]{1,0:T(8,128)(2,1)S(1)}, bf16[512,128]{1,0:T(8,128)(2,1)S(1)}, u32[]{:S(2)}, u32[]{:S(2)}) collective-permute-start(bf16[512,128]{1,0:T(8,128)(2,1)S(1)} %bitcast.15), channel_id=1, source_target_pairs={{0,24},{8,0},{16,8},{24,16},{32,56},{40,32},{48,40},{56,48},{64,88... | collective-permute-start | bytes 393224 | tf_op jit(solution)/shard_map/ppermute | solution.py:372
  27.5 14.9 %collective-permute-start.2 = (bf16[512,128]{1,0:T(8,128)(2,1)S(1)}, bf16[512,128]{1,0:T(8,128)(2,1)S(1)}, u32[]{:S(2)}, u32[]{:S(2)}) collective-permute-start(bf16[512,128]{1,0:T(8,128)(2,1)S(1)} %bitcast.16), channel_id=1, source_target_pairs={{0,16},{8,24},{16,0},{24,8},{32,48},{40,56},{48,32},{56,40},{64,80... | collective-permute-start | bytes 393224 | tf_op jit(solution)/shard_map/ppermute | solution.py:372
  41.0 35.2 %collective-permute-start.1 = (bf16[144,512]{1,0:T(8,128)(2,1)S(1)}, bf16[144,512]{1,0:T(8,128)(2,1)S(1)}, u32[]{:S(2)}, u32[]{:S(2)}) collective-permute-start(bf16[144,512]{1,0:T(8,128)(2,1)S(1)} %prefix_attention.5), channel_id=1, source_target_pairs={{0,24},{8,0},{16,8},{24,16},{32,56},{40,32},{48,40},{56,48},{64,88... | collective-permute-start | bytes 442376 | tf_op jit(solution)/shard_map/ppermute | solution.py:372
  53.1 23.1 %collective-permute-start.3 = (bf16[144,512]{1,0:T(8,128)(2,1)S(1)}, bf16[144,512]{1,0:T(8,128)(2,1)S(1)}, u32[]{:S(2)}, u32[]{:S(2)}) collective-permute-start(bf16[144,512]{1,0:T(8,128)(2,1)S(1)} %prefix_attention.6), channel_id=1, source_target_pairs={{0,16},{8,24},{16,0},{24,8},{32,48},{40,56},{48,32},{56,40},{64,80... | collective-permute-start | bytes 442376 | tf_op jit(solution)/shard_map/ppermute | solution.py:372
  64.6 15.8 %copy-start.3 = (bf16[8,4,2,128]{3,2,1,0:T(2,128)(2,1)S(1)}, bf16[8,4,2,128]{3,2,1,0:T(2,128)(2,1)}, u32[]{:S(2)}) copy-start(bf16[8,4,2,128]{3,2,1,0:T(2,128)(2,1)} %param.8) | copy-start | bytes 49156
  64.7 15.9 %copy-start.2 = (s32[8]{0:T(128)S(1)}, s32[8]{0:T(128)}, u32[]{:S(2)}) copy-start(s32[8]{0:T(128)} %len_ref.1) | copy-start | bytes 100
  64.7 11.5 %collective-permute-start.5 = (bf16[144,512]{1,0:T(8,128)(2,1)S(1)}, bf16[144,512]{1,0:T(8,128)(2,1)S(1)}, u32[]{:S(2)}, u32[]{:S(2)}) collective-permute-start(bf16[144,512]{1,0:T(8,128)(2,1)S(1)} %prefix_attention.7), channel_id=1, source_target_pairs={{0,8},{8,16},{16,24},{24,0},{32,40},{40,48},{48,56},{56,32},{64,72... | collective-permute-start | bytes 442376 | tf_op jit(solution)/shard_map/ppermute | solution.py:372
  76.1 12.5 %copy-start.1 = (s32[8,1]{0,1:T(1,128)S(1)}, s32[8,1]{0,1:T(1,128)}, u32[]{:S(2)}) copy-start(s32[8,1]{0,1:T(1,128)} %param.12) | copy-start | bytes 100
  77.0 11.6 %all-to-all-start.1 = ((bf16[8,80,128]{2,1,0:T(8,128)(2,1)}), bf16[8,80,128]{2,1,0:T(8,128)(2,1)S(1)}, u32[]{:S(2)}, u32[]{:S(2)}) async-start(bf16[8,80,128]{2,1,0:T(8,128)(2,1)} %merge_parts.1), calls=%async_computation.1 | async-start | bytes 327680 | tf_op jit(solution)/shard_map/all_to_all | solution.py:388
  80.6 1.6 %copy-start = (bf16[8,2,512,128]{3,2,1,0:T(8,128)(2,1)S(1)}, bf16[8,2,512,128]{3,2,1,0:T(8,128)(2,1)}, u32[]{:S(2)}) copy-start(bf16[8,2,512,128]{3,2,1,0:T(8,128)(2,1)} %kv_ref.1) | copy-start | bytes 6291460
  89.4 5.9 %collective-permute-start.8 = (bf16[32,1024]{1,0:T(8,128)(2,1)S(1)}, bf16[32,1024]{1,0:T(8,128)(2,1)S(1)}, u32[]{:S(2)}, u32[]{:S(2)}) collective-permute-start(bf16[32,1024]{1,0:T(8,128)(2,1)S(1)} %finish_attention.1.refs_0_), channel_id=1, source_target_pairs={{0,24},{8,0},{16,8},{24,16},{32,56},{40,32},{48,40},{56,48},{64,88... | collective-permute-start | bytes 196616 | tf_op jit(solution)/shard_map/ppermute | solution.py:372
  91.6 4.6 %collective-permute-start.7 = (bf16[32,1024]{1,0:T(8,128)(2,1)S(1)}, bf16[32,1024]{1,0:T(8,128)(2,1)S(1)}, u32[]{:S(2)}, u32[]{:S(2)}) collective-permute-start(bf16[32,1024]{1,0:T(8,128)(2,1)S(1)} %finish_attention.1.refs_0_), channel_id=1, source_target_pairs={{0,16},{8,24},{16,0},{24,8},{32,48},{40,56},{48,32},{56,40},{64,80... | collective-permute-start | bytes 196616 | tf_op jit(solution)/shard_map/ppermute | solution.py:372
  92.8 4.3 %collective-permute-start.6 = (bf16[32,1024]{1,0:T(8,128)(2,1)S(1)}, bf16[32,1024]{1,0:T(8,128)(2,1)S(1)}, u32[]{:S(2)}, u32[]{:S(2)}) collective-permute-start(bf16[32,1024]{1,0:T(8,128)(2,1)S(1)} %finish_attention.1.refs_0_), channel_id=1, source_target_pairs={{0,8},{8,16},{16,24},{24,0},{32,40},{40,48},{48,56},{56,32},{64,72... | collective-permute-start | bytes 196616 | tf_op jit(solution)/shard_map/ppermute | solution.py:372
  98.4 8.6 %collective-permute-start.9 = (bf16[4,128,256]{2,1,0:T(8,128)(2,1)S(1)}, bf16[4,128,256]{2,1,0:T(8,128)(2,1)S(1)}, u32[]{:S(2)}, u32[]{:S(2)}) collective-permute-start(bf16[4,128,256]{2,1,0:T(8,128)(2,1)S(1)} %get-tuple-element.20), channel_id=1, source_target_pairs={{0,1},{1,0},{2,3},{3,2},{4,5},{5,4},{6,7},{7,6},{8,9},{9,8},{10,11... | collective-permute-start | bytes 786440 | tf_op jit(solution)/shard_map/ppermute | solution.py:394
  107.1 4.8 %collective-permute-start.10 = (bf16[2,128,256]{2,1,0:T(8,128)(2,1)S(1)}, bf16[2,128,256]{2,1,0:T(8,128)(2,1)S(1)}, u32[]{:S(2)}, u32[]{:S(2)}) collective-permute-start(bf16[2,128,256]{2,1,0:T(8,128)(2,1)S(1)} %add_convert_fusion.1), channel_id=1, source_target_pairs={{0,2},{1,3},{2,0},{3,1},{4,6},{5,7},{6,4},{7,5},{8,10},{9,11},{10,... | collective-permute-start | bytes 393224 | tf_op jit(solution)/shard_map/ppermute | solution.py:397
  111.9 9.2 %collective-permute-start.12 = (bf16[128,256]{1,0:T(8,128)(2,1)S(1)}, bf16[128,256]{1,0:T(8,128)(2,1)S(1)}, u32[]{:S(2)}, u32[]{:S(2)}) collective-permute-start(bf16[128,256]{1,0:T(8,128)(2,1)S(1)} %get-tuple-element.21), channel_id=1, source_target_pairs={{0,32},{1,160},{2,96},{3,224},{4,0},{5,128},{6,64},{7,192},{8,40},... | collective-permute-start | bytes 196616 | tf_op jit(solution)/shard_map/ppermute | solution.py:411
  114.5 11.5 %collective-permute-start.11 = (bf16[128,256]{1,0:T(8,128)(2,1)S(1)}, bf16[128,256]{1,0:T(8,128)(2,1)S(1)}, u32[]{:S(2)}, u32[]{:S(2)}) collective-permute-start(bf16[128,256]{1,0:T(8,128)(2,1)S(1)} %get-tuple-element.22), channel_id=1, source_target_pairs={{0,0},{1,128},{2,64},{3,192},{4,32},{5,160},{6,96},{7,224},{8,8},{... | collective-permute-start | bytes 196616 | tf_op jit(solution)/shard_map/ppermute | solution.py:411
Sparse Core Ops, SparseCore 0:
  9.1 57.5 all-gather.2

commit v3 on v2

--- a/solution.py
+++ b/solution.py
@@ -308,6 +308,33 @@
     )(value)
 
 
+def load_all_kernel(up, place_ref, *refs):
+    *source_refs, out_ref, sem = refs
+    count = len(source_refs)
+    copies = []
+    for k, ref in enumerate(source_refs):
+        away = -k if k < up else k - up + 1
+        at = lax.rem(place_ref[0] + count + away, count)
+        copies.append(pltpu.make_async_copy(ref, out_ref.at[at], sem.at[k]))
+        copies[k].start()
+    for copy in copies:
+        copy.wait()
+
+
+def load_all(place, values, nz):
+    count = len(values)
+    shape = (count,) + values[0].shape
+    return pl.pallas_call(
+        functools.partial(load_all_kernel, count // 2 + 1),
+        in_specs=[whole(pltpu.SMEM)] + [whole(pl.ANY)] * count,
+        out_specs=whole(),
+        out_shape=pltpu.VMEM(shape, values[0].dtype),
+        scratch_shapes=[pltpu.SemaphoreType.DMA((count,))],
+        compiler_params=params(),
+        name="load_all",
+    )(place, *values)
+
+
 def project_kernel(place_ref, *refs):
     *mixed_refs, weight_ref, theirs_ref, ours_ref, rows_ref = refs
     count = len(mixed_refs)
@@ -371,26 +398,51 @@
         pairs = [(z * nx + i, z * nx + (i + k) % nx) for z in range(nz) for i in range(nx)]
         return lax.ppermute(value, "cache", pairs)
 
+    def along_z(value, k):
+        pairs = [(z * nx + i, (z + k) % nz * nx + i) for z in range(nz) for i in range(nx)]
+        return lax.ppermute(value, "cache", pairs)
+
     prompt_ids = branch_prompt[:, 0]
+    up, down = [out_weight], [out_weight]
+
+    def pass_on(steps_up, steps_down):
+        if steps_up:
+            up.append(along_z(up[-1], 1))
+        if steps_down:
+            down.append(along_z(down[-1], nz - 1))
+
+    def after(value):
+        value, up[-1], down[-1] = lax.optimization_barrier((value, up[-1], down[-1]))
+        return value
+
+    pass_on(1, 1)
     packed, q_rows = pack(prompt_ids, queries, group)
-    weight = lax.all_gather(out_weight, "cache", axis_index_groups=z_groups)
     mine = lax.all_to_all(packed, "cache", 0, 0, axis_index_groups=z_groups, tiled=True)
     kv = load(prefix_kv, 2)
     mine, kv = lax.optimization_barrier((mine, kv))
+    mine = after(mine)
+    pass_on(1, 1)
     mine = mine.reshape(nz * SLOTS * height, HEAD_DIM)
     sent = [along_x(mine, k) for k in range(1, nx)]
     fresh = jnp.pad(new_kv.transpose(0, 2, 1, 3), ((0, 0), (0, 0), (0, 16 - steps), (0, 0)))
     own, own_lse = suffix(suffix_len, q_rows, suffix_kv, fresh, steps)
     parts = [attend(mine, kv)]
     for k in range(1, nx):
-        parts.append(along_x(attend(sent[k - 1], kv), nx - k))
+        part = attend(sent[k - 1], kv)
+        if k == 1:
+            part = after(part)
+            pass_on(1, 1)
+        if k == 3:
+            part = after(part)
+            pass_on(1, 0)
+        parts.append(along_x(part, nx - k))
     merged = merge(parts, nz)
     back = lax.all_to_all(merged, "cache", 0, 0, axis_index_groups=z_groups, tiled=True)
     home = (cache // nx).reshape(1)
     mixed = finish(prompt_ids, home, back, own, own_lse, steps, group)
     plane = [mixed] + [along_x(mixed, k) for k in range(1, nx)]
     half = nz // 2
-    theirs, ours = project(jnp.stack([x, core, y % 2]), plane, load(weight, nz))
+    theirs, ours = project(jnp.stack([x, core, y % 2]), plane, load_all(home, up + down[1:], nz))
     theirs = lax.ppermute(theirs, "tensor", [(t, t ^ 1) for t in range(2 * ny)])
     keep = ours[:2] + theirs[:2].astype(F32)
     give = (ours[2:] + theirs[2:].astype(F32)).astype(BF16)

time: 134 us -> 131 us (0.978)
  between operations: 13.7 us -> 0.32 us
  starting transfers between devices: 39.9 us -> 50.5 us
    ppermute x0 -> x7, starting transfers between devices: none -> 11 us  [along_z(): return lax.ppermute(value, 'cache', pairs)]
    all_to_all x1, starting transfers between devices: 8.2 us -> 5.29 us  [per_device(): lax.all_to_all(packed, 'cache', 0, 0, axis_index_groups=z_groups, tiled=T...]
    pallas_call x2 -> x1, Pallas kernels: 4.11 us -> 1.9 us  [load(): pl.pallas_call(functools.partial(load_kernel, count), in_specs=[whole(pl....]
    pallas_call x0 -> x1, Pallas kernels: none -> 1.97 us  [load_all(): pl.pallas_call(functools.partial(load_all_kernel, count // 2 + 1), in_spe...]
    ppermute x1, starting transfers between devices: 7.47 us -> 9.12 us  [per_device(): theirs = lax.ppermute(theirs, 'tensor', [(t, t ^ 1) for t in range(2 * ny)])]
  transfers between devices with their start and end apart: 16 -> 22, of which waited for: 8 -> 8; matrix products, arithmetic and copies ran while one was open for 0% -> 0% of each run, Pallas kernels for 41% -> 41%
where the time goes in v3:
time: 131 us
  Pallas kernels  55.9 us (43%)
  starting transfers between devices  50.5 us (39%)
  waiting for transfers between devices  22.1 us (17%)
  local copies, waits for them, and re-layouts  1.67 us (1%)
    pallas_call x4, Pallas kernels, attend(): pl.pallas_call(functools.partial(attend_kernel, PART), in_specs=[whole(),...  43.2 us
    ppermute x7, starting transfers between devices, along_z(): return lax.ppermute(value, 'cache', pairs)  11 us
    ppermute x9, starting transfers between devices, along_x(): return lax.ppermute(value, 'cache', pairs)  10.9 us
    ppermute x2, starting transfers between devices, per_device(): pieces.append(lax.ppermute(block, ('cache', 'tensor'), pairs))  9.14 us
    ppermute x1, starting transfers between devices, per_device(): theirs = lax.ppermute(theirs, 'tensor', [(t, t ^ 1) for t in range(2 * ny)])  9.12 us
    all_to_all x1, waiting for transfers between devices, per_device(): lax.all_to_all(packed, 'cache', 0, 0, axis_index_groups=z_groups, tiled=T...  6.26 us
    all_to_all x1, starting transfers between devices, per_device(): lax.all_to_all(packed, 'cache', 0, 0, axis_index_groups=z_groups, tiled=T...  5.29 us
    ppermute x2, waiting for transfers between devices, per_device(): pieces.append(lax.ppermute(block, ('cache', 'tensor'), pairs))  4.92 us
  transfers between devices with their start and end apart: 22, of which 8 were waited for; matrix products, arithmetic and copies ran while one was open for 0% of the time, Pallas kernels for 41%

profile of v3, /device:TPU:17, one launch (start us, length us, event | category | flops | bytes accessed | tf_op | source)
XLA Modules:
  0.0 130.6 jit_solution(12508930429542847174)
XLA Ops:
  0.0 1.6 %collective-permute-start = (bf16[1024,256]{1,0:T(8,128)(2,1)}, bf16[1024,256]{1,0:T(8,128)(2,1)}, u32[]{:S(2)}, u32[]{:S(2)}) collective-permute-start(bf16[1024,256]{1,0:T(8,128)(2,1)} %refs_0_.1), channel_id=1, source_target_pairs={{0,32},{8,40},{16,48},{24,56},{32,64},{40,72},{48,80},{56,88},{64,... | collective-permute-start | bytes 1572872 | tf_op jit(solution)/shard_map/ppermute | solution.py:403
  1.6 3.9 %collective-permute-start.1 = (bf16[1024,256]{1,0:T(8,128)(2,1)}, bf16[1024,256]{1,0:T(8,128)(2,1)}, u32[]{:S(2)}, u32[]{:S(2)}) collective-permute-start(bf16[1024,256]{1,0:T(8,128)(2,1)} %refs_0_.1), channel_id=1, source_target_pairs={{0,224},{8,232},{16,240},{24,248},{32,0},{40,8},{48,16},{56,24},{6... | collective-permute-start | bytes 1572872 | tf_op jit(solution)/shard_map/ppermute | solution.py:403
  5.6 1.6 %pack_queries.1 = (bf16[8,64,128]{2,1,0:T(8,128)(2,1)}, bf16[8,32,128]{2,1,0:T(8,128)(2,1)S(1)}) custom-call(s32[8]{0:T(128)} %bitcast.17, bf16[8,4,1024]{2,1,0:T(4,128)(2,1)} %q_hbm.1), custom_call_target="tpu_custom_call" | custom-call | tf_op jit(solution)/shard_map/pack_queries/pallas_call | solution.py:71
  7.1 5.3 %all-to-all-start = ((bf16[8,64,128]{2,1,0:T(8,128)(2,1)}), bf16[8,64,128]{2,1,0:T(8,128)(2,1)S(1)}, u32[]{:S(2)}, u32[]{:S(2)}) async-start(bf16[8,64,128]{2,1,0:T(8,128)(2,1)} %get-tuple-element.22), calls=%async_computation | async-start | bytes 262144 | tf_op jit(solution)/shard_map/all_to_all | solution.py:420
  12.4 1.9 %load.1.kv_ref = bf16[2,6144,128]{2,1,0:T(8,128)(2,1)S(1)} custom-call(bf16[2,6144,128]{2,1,0:T(8,128)(2,1)} %source_ref.1), custom_call_target="tpu_custom_call" | custom-call | bytes 6291456 | tf_op jit(solution)/shard_map/load/pallas_call | solution.py:297
  14.3 6.3 %all-to-all-done = bf16[8,64,128]{2,1,0:T(8,128)(2,1)S(1)} async-done(((bf16[8,64,128]{2,1,0:T(8,128)(2,1)}), bf16[8,64,128]{2,1,0:T(8,128)(2,1)S(1)}, u32[]{:S(2)}, u32[]{:S(2)}) %all-to-all-start) | async-done | bytes 131104 | tf_op jit(solution)/shard_map/all_to_all | solution.py:420
  20.6 2.1 %collective-permute-start.3 = (bf16[1024,256]{1,0:T(8,128)(2,1)}, bf16[1024,256]{1,0:T(8,128)(2,1)S(1)}, u32[]{:S(2)}, u32[]{:S(2)}) collective-permute-start(bf16[1024,256]{1,0:T(8,128)(2,1)} %collective-permute-done.refs_1_), channel_id=1, source_target_pairs={{0,32},{8,40},{16,48},{24,56},{32,64},{40,72},{48,80},{56,88},{64,... | collective-permute-start | bytes 1572872 | tf_op jit(solution)/shard_map/ppermute | solution.py:403
  23.3 1.2 collective-permute-start.2
  24.5 1.5 %collective-permute-start.8 = (bf16[512,128]{1,0:T(8,128)(2,1)S(1)}, bf16[512,128]{1,0:T(8,128)(2,1)S(1)}, u32[]{:S(2)}, u32[]{:S(2)}) collective-permute-start(bf16[512,128]{1,0:T(8,128)(2,1)S(1)} %bitcast.14), channel_id=1, source_target_pairs={{0,24},{8,0},{16,8},{24,16},{32,56},{40,32},{48,40},{56,48},{64,88... | collective-permute-start | bytes 393224 | tf_op jit(solution)/shard_map/ppermute | solution.py:399
  26.0 1.5 %collective-permute-start.6 = (bf16[512,128]{1,0:T(8,128)(2,1)S(1)}, bf16[512,128]{1,0:T(8,128)(2,1)S(1)}, u32[]{:S(2)}, u32[]{:S(2)}) collective-permute-start(bf16[512,128]{1,0:T(8,128)(2,1)S(1)} %bitcast.15), channel_id=1, source_target_pairs={{0,16},{8,24},{16,0},{24,8},{32,48},{40,56},{48,32},{56,40},{64,80... | collective-permute-start | bytes 393224 | tf_op jit(solution)/shard_map/ppermute | solution.py:399
  27.5 1.1 collective-permute-done.2.q_ref
  28.6 10.7 %prefix_attention.5 = bf16[144,512]{1,0:T(8,128)(2,1)S(1)} custom-call(bf16[512,128]{1,0:T(8,128)(2,1)S(1)} %collective-permute-done.2.q_ref, bf16[2,6144,128]{2,1,0:T(8,128)(2,1)S(1)} %load.1.kv_ref), custom_call_target="tpu_custom_call" | custom-call | flops 3221225472 | bytes 3145728 | tf_op jit(solution)/shard_map/prefix_attention/pallas_call | solution.py:151
  40.1 2.1 %collective-permute-start.10 = (bf16[1024,256]{1,0:T(8,128)(2,1)S(1)}, bf16[1024,256]{1,0:T(8,128)(2,1)S(1)}, u32[]{:S(2)}, u32[]{:S(2)}) collective-permute-start(bf16[1024,256]{1,0:T(8,128)(2,1)S(1)} %collective-permute-done.4.refs_6_), channel_id=1, source_target_pairs={{0,224},{8,232},{16,240},{24,248},{32,0},{40,8},{48,16},{56,24},{6... | collective-permute-start | bytes 1572872 | tf_op jit(solution)/shard_map/ppermute | solution.py:403
  42.2 10.8 %prefix_attention.6 = bf16[144,512]{1,0:T(8,128)(2,1)S(1)} custom-call(bf16[512,128]{1,0:T(8,128)(2,1)S(1)} %collective-permute-done.6.q_ref, bf16[2,6144,128]{2,1,0:T(8,128)(2,1)S(1)} %load.1.kv_ref), custom_call_target="tpu_custom_call" | custom-call | flops 3221225472 | bytes 3145728 | tf_op jit(solution)/shard_map/prefix_attention/pallas_call | solution.py:151
  52.9 1.6 %collective-permute-start.7 = (bf16[144,512]{1,0:T(8,128)(2,1)S(1)}, bf16[144,512]{1,0:T(8,128)(2,1)S(1)}, u32[]{:S(2)}, u32[]{:S(2)}) collective-permute-start(bf16[144,512]{1,0:T(8,128)(2,1)S(1)} %prefix_attention.6), channel_id=1, source_target_pairs={{0,16},{8,24},{16,0},{24,8},{32,48},{40,56},{48,32},{56,40},{64,80... | collective-permute-start | bytes 442376 | tf_op jit(solution)/shard_map/ppermute | solution.py:399
  54.6 10.8 %prefix_attention.7 = bf16[144,512]{1,0:T(8,128)(2,1)S(1)} custom-call(bf16[512,128]{1,0:T(8,128)(2,1)S(1)} %collective-permute-done.8.q_ref, bf16[2,6144,128]{2,1,0:T(8,128)(2,1)S(1)} %load.1.kv_ref), custom_call_target="tpu_custom_call" | custom-call | flops 3221225472 | bytes 3145728 | tf_op jit(solution)/shard_map/prefix_attention/pallas_call | solution.py:151
  67.0 11.0 %prefix_attention.4.refs_0_ = bf16[144,512]{1,0:T(8,128)(2,1)S(1)} custom-call(bf16[512,128]{1,0:T(8,128)(2,1)S(1)} %bitcast.16, bf16[2,6144,128]{2,1,0:T(8,128)(2,1)S(1)} %load.1.kv_ref), custom_call_target="tpu_custom_call" | custom-call | flops 3221225472 | bytes 3145728 | tf_op jit(solution)/shard_map/prefix_attention/pallas_call | solution.py:151
  78.9 4.0 %all-to-all-start.1 = ((bf16[8,80,128]{2,1,0:T(8,128)(2,1)}), bf16[8,80,128]{2,1,0:T(8,128)(2,1)S(1)}, u32[]{:S(2)}, u32[]{:S(2)}) async-start(bf16[8,80,128]{2,1,0:T(8,128)(2,1)} %merge_parts.1), calls=%async_computation.1 | async-start | bytes 327680 | tf_op jit(solution)/shard_map/all_to_all | solution.py:440
  83.0 1.6 %copy-done = bf16[8,2,512,128]{3,2,1,0:T(8,128)(2,1)S(1)} copy-done((bf16[8,2,512,128]{3,2,1,0:T(8,128)(2,1)S(1)}, bf16[8,2,512,128]{3,2,1,0:T(8,128)(2,1)}, u32[]{:S(2)}) %copy-start) | copy-done | bytes 2097176
  84.6 3.7 %suffix_attention.1 = (f32[8,32,128]{2,1,0:T(8,128)S(1)}, f32[8,32,128]{2,1,0:T(8,128)S(1)}) custom-call(s32[8]{0:T(128)S(1)} %copy-done.5, bf16[8,32,128]{2,1,0:T(8,128)(2,1)S(1)} %get-tuple-element.32.q_ref, bf16[8,2,512,128]{3,2,1,0:T(8,128)(2,1)S(1)} %copy-done, bf16[8,2,16,128]{3,2,1,0:T(8,128)(2,1)S(1)} %pad.4.new_ref), custom_call_target="tpu_custom_call" | custom-call | tf_op jit(solution)/shard_map/suffix_attention/pallas_call | solution.py:195
  88.3 2.9 %all-to-all-done.1.back_ref = bf16[8,80,128]{2,1,0:T(8,128)(2,1)S(1)} async-done(((bf16[8,80,128]{2,1,0:T(8,128)(2,1)}), bf16[8,80,128]{2,1,0:T(8,128)(2,1)S(1)}, u32[]{:S(2)}, u32[]{:S(2)}) %all-to-all-start.1) | async-done | bytes 163872 | tf_op jit(solution)/shard_map/all_to_all | solution.py:440
  92.0 2.1 %collective-permute-start.14 = (bf16[32,1024]{1,0:T(8,128)(2,1)S(1)}, bf16[32,1024]{1,0:T(8,128)(2,1)S(1)}, u32[]{:S(2)}, u32[]{:S(2)}) collective-permute-start(bf16[32,1024]{1,0:T(8,128)(2,1)S(1)} %finish_attention.1.refs_0_), channel_id=1, source_target_pairs={{0,24},{8,0},{16,8},{24,16},{32,56},{40,32},{48,40},{56,48},{64,88... | collective-permute-start | bytes 196616 | tf_op jit(solution)/shard_map/ppermute | solution.py:399
  95.5 2.0 %load_all.1.refs_4_ = bf16[8,1024,256]{2,1,0:T(8,128)(2,1)S(1)} custom-call(s32[1]{0:T(128)} %bitcast.4.home_ref.place_ref, bf16[1024,256]{1,0:T(8,128)(2,1)S(1)} %copy-done.1, bf16[1024,256]{1,0:T(8,128)(2,1)} %collective-permute-done.refs_1_, bf16[1024,256]{1,0:T(8,128)(2,1)S(1)} %copy-done.3, bf16[1024,256]{1,0:T(8,128)(2,1)} %collective-permute-done.9.refs_3_, ...), custom_call_target="tpu_custom_call" | custom-call | tf_op jit(solution)/shard_map/load_all/pallas_call | solution.py:327
  97.5 1.3 collective-permute-done.13.refs_2_
  99.4 1.3 project.1
  100.7 9.1 %collective-permute-start.16 = (bf16[4,128,256]{2,1,0:T(8,128)(2,1)S(1)}, bf16[4,128,256]{2,1,0:T(8,128)(2,1)S(1)}, u32[]{:S(2)}, u32[]{:S(2)}) collective-permute-start(bf16[4,128,256]{2,1,0:T(8,128)(2,1)S(1)} %get-tuple-element.38), channel_id=1, source_target_pairs={{0,1},{1,0},{2,3},{3,2},{4,5},{5,4},{6,7},{7,6},{8,9},{9,8},{10,11... | collective-permute-start | bytes 786440 | tf_op jit(solution)/shard_map/ppermute | solution.py:446
  109.8 1.2 collective-permute-done.16
  111.0 1.1 collective-permute-start.17
  112.1 3.7 %collective-permute-done.17 = bf16[2,128,256]{2,1,0:T(8,128)(2,1)S(1)} collective-permute-done((bf16[2,128,256]{2,1,0:T(8,128)(2,1)S(1)}, bf16[2,128,256]{2,1,0:T(8,128)(2,1)S(1)}, u32[]{:S(2)}, u32[]{:S(2)}) %collective-permute-start.17) | collective-permute-done | bytes 131104 | tf_op jit(solution)/shard_map/ppermute | solution.py:449
  115.9 2.6 %collective-permute-start.19 = (bf16[128,256]{1,0:T(8,128)(2,1)S(1)}, bf16[128,256]{1,0:T(8,128)(2,1)S(1)}, u32[]{:S(2)}, u32[]{:S(2)}) collective-permute-start(bf16[128,256]{1,0:T(8,128)(2,1)S(1)} %get-tuple-element.39), channel_id=1, source_target_pairs={{0,32},{1,160},{2,96},{3,224},{4,0},{5,128},{6,64},{7,192},{8,40},... | collective-permute-start | bytes 196616 | tf_op jit(solution)/shard_map/ppermute | solution.py:463
  118.4 6.6 %collective-permute-start.18 = (bf16[128,256]{1,0:T(8,128)(2,1)S(1)}, bf16[128,256]{1,0:T(8,128)(2,1)S(1)}, u32[]{:S(2)}, u32[]{:S(2)}) collective-permute-start(bf16[128,256]{1,0:T(8,128)(2,1)S(1)} %get-tuple-element.40), channel_id=1, source_target_pairs={{0,0},{1,128},{2,64},{3,192},{4,32},{5,160},{6,96},{7,224},{8,8},{... | collective-permute-start | bytes 196616 | tf_op jit(solution)/shard_map/ppermute | solution.py:463
  125.0 4.9 %collective-permute-done.18.refs_0_ = bf16[128,256]{1,0:T(8,128)(2,1)S(1)} collective-permute-done((bf16[128,256]{1,0:T(8,128)(2,1)S(1)}, bf16[128,256]{1,0:T(8,128)(2,1)S(1)}, u32[]{:S(2)}, u32[]{:S(2)}) %collective-permute-start.18) | collective-permute-done | bytes 65568 | tf_op jit(solution)/shard_map/ppermute | solution.py:463
  (48 shorter events, 7.4 us)
Async XLA Ops:
  0.0 20.6 %collective-permute-start = (bf16[1024,256]{1,0:T(8,128)(2,1)}, bf16[1024,256]{1,0:T(8,128)(2,1)}, u32[]{:S(2)}, u32[]{:S(2)}) collective-permute-start(bf16[1024,256]{1,0:T(8,128)(2,1)} %refs_0_.1), channel_id=1, source_target_pairs={{0,32},{8,40},{16,48},{24,56},{32,64},{40,72},{48,80},{56,88},{64,... | collective-permute-start | bytes 1572872 | tf_op jit(solution)/shard_map/ppermute | solution.py:403
  1.6 19.0 %collective-permute-start.1 = (bf16[1024,256]{1,0:T(8,128)(2,1)}, bf16[1024,256]{1,0:T(8,128)(2,1)}, u32[]{:S(2)}, u32[]{:S(2)}) collective-permute-start(bf16[1024,256]{1,0:T(8,128)(2,1)} %refs_0_.1), channel_id=1, source_target_pairs={{0,224},{8,232},{16,240},{24,248},{32,0},{40,8},{48,16},{56,24},{6... | collective-permute-start | bytes 1572872 | tf_op jit(solution)/shard_map/ppermute | solution.py:403
  7.1 13.5 %all-to-all-start = ((bf16[8,64,128]{2,1,0:T(8,128)(2,1)}), bf16[8,64,128]{2,1,0:T(8,128)(2,1)S(1)}, u32[]{:S(2)}, u32[]{:S(2)}) async-start(bf16[8,64,128]{2,1,0:T(8,128)(2,1)} %get-tuple-element.22), calls=%async_computation | async-start | bytes 262144 | tf_op jit(solution)/shard_map/all_to_all | solution.py:420
  20.6 18.7 %collective-permute-start.3 = (bf16[1024,256]{1,0:T(8,128)(2,1)}, bf16[1024,256]{1,0:T(8,128)(2,1)S(1)}, u32[]{:S(2)}, u32[]{:S(2)}) collective-permute-start(bf16[1024,256]{1,0:T(8,128)(2,1)} %collective-permute-done.refs_1_), channel_id=1, source_target_pairs={{0,32},{8,40},{16,48},{24,56},{32,64},{40,72},{48,80},{56,88},{64,... | collective-permute-start | bytes 1572872 | tf_op jit(solution)/shard_map/ppermute | solution.py:403
  22.7 16.7 %collective-permute-start.4 = (bf16[1024,256]{1,0:T(8,128)(2,1)}, bf16[1024,256]{1,0:T(8,128)(2,1)S(1)}, u32[]{:S(2)}, u32[]{:S(2)}) collective-permute-start(bf16[1024,256]{1,0:T(8,128)(2,1)} %collective-permute-done.1.refs_5_), channel_id=1, source_target_pairs={{0,224},{8,232},{16,240},{24,248},{32,0},{40,8},{48,16},{56,24},{6... | collective-permute-start | bytes 1572872 | tf_op jit(solution)/shard_map/ppermute | solution.py:403
  23.3 5.3 %collective-permute-start.2 = (bf16[512,128]{1,0:T(8,128)(2,1)S(1)}, bf16[512,128]{1,0:T(8,128)(2,1)S(1)}, u32[]{:S(2)}, u32[]{:S(2)}) collective-permute-start(bf16[512,128]{1,0:T(8,128)(2,1)S(1)} %bitcast.13), channel_id=1, source_target_pairs={{0,8},{8,16},{16,24},{24,0},{32,40},{40,48},{48,56},{56,32},{64,72... | collective-permute-start | bytes 393224 | tf_op jit(solution)/shard_map/ppermute | solution.py:399
  24.5 30.1 %collective-permute-start.8 = (bf16[512,128]{1,0:T(8,128)(2,1)S(1)}, bf16[512,128]{1,0:T(8,128)(2,1)S(1)}, u32[]{:S(2)}, u32[]{:S(2)}) collective-permute-start(bf16[512,128]{1,0:T(8,128)(2,1)S(1)} %bitcast.14), channel_id=1, source_target_pairs={{0,24},{8,0},{16,8},{24,16},{32,56},{40,32},{48,40},{56,48},{64,88... | collective-permute-start | bytes 393224 | tf_op jit(solution)/shard_map/ppermute | solution.py:399
  26.0 16.2 %collective-permute-start.6 = (bf16[512,128]{1,0:T(8,128)(2,1)S(1)}, bf16[512,128]{1,0:T(8,128)(2,1)S(1)}, u32[]{:S(2)}, u32[]{:S(2)}) collective-permute-start(bf16[512,128]{1,0:T(8,128)(2,1)S(1)} %bitcast.15), channel_id=1, source_target_pairs={{0,16},{8,24},{16,0},{24,8},{32,48},{40,56},{48,32},{56,40},{64,80... | collective-permute-start | bytes 393224 | tf_op jit(solution)/shard_map/ppermute | solution.py:399
  39.4 13.6 %copy-start.2 = (bf16[1024,256]{1,0:T(8,128)(2,1)}, bf16[1024,256]{1,0:T(8,128)(2,1)S(1)}, u32[]{:S(2)}) copy-start(bf16[1024,256]{1,0:T(8,128)(2,1)S(1)} %collective-permute-done.3.refs_2_) | copy-start | bytes 1572868
  39.4 13.5 %copy-start.6 = (bf16[1024,256]{1,0:T(8,128)(2,1)}, bf16[1024,256]{1,0:T(8,128)(2,1)S(1)}, u32[]{:S(2)}) copy-start(bf16[1024,256]{1,0:T(8,128)(2,1)S(1)} %collective-permute-done.4.refs_6_) | copy-start | bytes 1572868
  39.4 26.9 %collective-permute-start.9 = (bf16[1024,256]{1,0:T(8,128)(2,1)S(1)}, bf16[1024,256]{1,0:T(8,128)(2,1)}, u32[]{:S(2)}, u32[]{:S(2)}) collective-permute-start(bf16[1024,256]{1,0:T(8,128)(2,1)S(1)} %collective-permute-done.3.refs_2_), channel_id=1, source_target_pairs={{0,32},{8,40},{16,48},{24,56},{32,64},{40,72},{48,80},{56,88},{64,... | collective-permute-start | bytes 1572872 | tf_op jit(solution)/shard_map/ppermute | solution.py:403
  40.1 26.2 %collective-permute-start.10 = (bf16[1024,256]{1,0:T(8,128)(2,1)S(1)}, bf16[1024,256]{1,0:T(8,128)(2,1)S(1)}, u32[]{:S(2)}, u32[]{:S(2)}) collective-permute-start(bf16[1024,256]{1,0:T(8,128)(2,1)S(1)} %collective-permute-done.4.refs_6_), channel_id=1, source_target_pairs={{0,224},{8,232},{16,240},{24,248},{32,0},{40,8},{48,16},{56,24},{6... | collective-permute-start | bytes 1572872 | tf_op jit(solution)/shard_map/ppermute | solution.py:403
  52.9 25.1 %collective-permute-start.7 = (bf16[144,512]{1,0:T(8,128)(2,1)S(1)}, bf16[144,512]{1,0:T(8,128)(2,1)S(1)}, u32[]{:S(2)}, u32[]{:S(2)}) collective-permute-start(bf16[144,512]{1,0:T(8,128)(2,1)S(1)} %prefix_attention.6), channel_id=1, source_target_pairs={{0,16},{8,24},{16,0},{24,8},{32,48},{40,56},{48,32},{56,40},{64,80... | collective-permute-start | bytes 442376 | tf_op jit(solution)/shard_map/ppermute | solution.py:399
  65.3 17.5 %copy-start.8 = (bf16[8,4,2,128]{3,2,1,0:T(2,128)(2,1)S(1)}, bf16[8,4,2,128]{3,2,1,0:T(2,128)(2,1)}, u32[]{:S(2)}) copy-start(bf16[8,4,2,128]{3,2,1,0:T(2,128)(2,1)} %param.8) | copy-start | bytes 49156
  65.4 17.6 %copy-start.5 = (s32[8]{0:T(128)S(1)}, s32[8]{0:T(128)}, u32[]{:S(2)}) copy-start(s32[8]{0:T(128)} %len_ref.1) | copy-start | bytes 100
  65.4 12.7 %collective-permute-start.5 = (bf16[144,512]{1,0:T(8,128)(2,1)S(1)}, bf16[144,512]{1,0:T(8,128)(2,1)S(1)}, u32[]{:S(2)}, u32[]{:S(2)}) collective-permute-start(bf16[144,512]{1,0:T(8,128)(2,1)S(1)} %prefix_attention.5), channel_id=1, source_target_pairs={{0,24},{8,0},{16,8},{24,16},{32,56},{40,32},{48,40},{56,48},{64,88... | collective-permute-start | bytes 442376 | tf_op jit(solution)/shard_map/ppermute | solution.py:399
  66.3 11.7 %copy-start.7 = (bf16[1024,256]{1,0:T(8,128)(2,1)}, bf16[1024,256]{1,0:T(8,128)(2,1)S(1)}, u32[]{:S(2)}) copy-start(bf16[1024,256]{1,0:T(8,128)(2,1)S(1)} %collective-permute-done.10.refs_7_) | copy-start | bytes 1572868
  66.3 11.7 %collective-permute-start.11 = (bf16[144,512]{1,0:T(8,128)(2,1)S(1)}, bf16[144,512]{1,0:T(8,128)(2,1)S(1)}, u32[]{:S(2)}, u32[]{:S(2)}) collective-permute-start(bf16[144,512]{1,0:T(8,128)(2,1)S(1)} %prefix_attention.7), channel_id=1, source_target_pairs={{0,8},{8,16},{16,24},{24,0},{32,40},{40,48},{48,56},{56,32},{64,72... | collective-permute-start | bytes 442376 | tf_op jit(solution)/shard_map/ppermute | solution.py:399
  67.0 28.5 %collective-permute-start.15 = (bf16[1024,256]{1,0:T(8,128)(2,1)}, bf16[1024,256]{1,0:T(8,128)(2,1)}, u32[]{:S(2)}, u32[]{:S(2)}) collective-permute-start(bf16[1024,256]{1,0:T(8,128)(2,1)} %collective-permute-done.9.refs_3_), channel_id=1, source_target_pairs={{0,32},{8,40},{16,48},{24,56},{32,64},{40,72},{48,80},{56,88},{64,... | collective-permute-start | bytes 1572872 | tf_op jit(solution)/shard_map/ppermute | solution.py:403
  78.0 13.2 %copy-start.4 = (s32[8,1]{0,1:T(1,128)S(1)}, s32[8,1]{0,1:T(1,128)}, u32[]{:S(2)}) copy-start(s32[8,1]{0,1:T(1,128)} %param.12) | copy-start | bytes 100
  78.0 17.5 %copy-start.1 = (bf16[1024,256]{1,0:T(8,128)(2,1)S(1)}, bf16[1024,256]{1,0:T(8,128)(2,1)}, u32[]{:S(2)}) copy-start(bf16[1024,256]{1,0:T(8,128)(2,1)} %refs_0_.1) | copy-start | bytes 1572868
  78.0 17.5 %copy-start.3 = (bf16[1024,256]{1,0:T(8,128)(2,1)S(1)}, bf16[1024,256]{1,0:T(8,128)(2,1)}, u32[]{:S(2)}) copy-start(bf16[1024,256]{1,0:T(8,128)(2,1)} %copy-done.2) | copy-start | bytes 1572868
  78.9 12.2 %all-to-all-start.1 = ((bf16[8,80,128]{2,1,0:T(8,128)(2,1)}), bf16[8,80,128]{2,1,0:T(8,128)(2,1)S(1)}, u32[]{:S(2)}, u32[]{:S(2)}) async-start(bf16[8,80,128]{2,1,0:T(8,128)(2,1)} %merge_parts.1), calls=%async_computation.1 | async-start | bytes 327680 | tf_op jit(solution)/shard_map/all_to_all | solution.py:440
  83.0 1.6 %copy-start = (bf16[8,2,512,128]{3,2,1,0:T(8,128)(2,1)S(1)}, bf16[8,2,512,128]{3,2,1,0:T(8,128)(2,1)}, u32[]{:S(2)}) copy-start(bf16[8,2,512,128]{3,2,1,0:T(8,128)(2,1)} %kv_ref.1) | copy-start | bytes 6291460
  92.0 5.5 %collective-permute-start.14 = (bf16[32,1024]{1,0:T(8,128)(2,1)S(1)}, bf16[32,1024]{1,0:T(8,128)(2,1)S(1)}, u32[]{:S(2)}, u32[]{:S(2)}) collective-permute-start(bf16[32,1024]{1,0:T(8,128)(2,1)S(1)} %finish_attention.1.refs_0_), channel_id=1, source_target_pairs={{0,24},{8,0},{16,8},{24,16},{32,56},{40,32},{48,40},{56,48},{64,88... | collective-permute-start | bytes 196616 | tf_op jit(solution)/shard_map/ppermute | solution.py:399
  94.1 4.7 %collective-permute-start.13 = (bf16[32,1024]{1,0:T(8,128)(2,1)S(1)}, bf16[32,1024]{1,0:T(8,128)(2,1)S(1)}, u32[]{:S(2)}, u32[]{:S(2)}) collective-permute-start(bf16[32,1024]{1,0:T(8,128)(2,1)S(1)} %finish_attention.1.refs_0_), channel_id=1, source_target_pairs={{0,16},{8,24},{16,0},{24,8},{32,48},{40,56},{48,32},{56,40},{64,80... | collective-permute-start | bytes 196616 | tf_op jit(solution)/shard_map/ppermute | solution.py:399
  94.6 4.8 %collective-permute-start.12 = (bf16[32,1024]{1,0:T(8,128)(2,1)S(1)}, bf16[32,1024]{1,0:T(8,128)(2,1)S(1)}, u32[]{:S(2)}, u32[]{:S(2)}) collective-permute-start(bf16[32,1024]{1,0:T(8,128)(2,1)S(1)} %finish_attention.1.refs_0_), channel_id=1, source_target_pairs={{0,8},{8,16},{16,24},{24,0},{32,40},{40,48},{48,56},{56,32},{64,72... | collective-permute-start | bytes 196616 | tf_op jit(solution)/shard_map/ppermute | solution.py:399
  100.7 10.3 %collective-permute-start.16 = (bf16[4,128,256]{2,1,0:T(8,128)(2,1)S(1)}, bf16[4,128,256]{2,1,0:T(8,128)(2,1)S(1)}, u32[]{:S(2)}, u32[]{:S(2)}) collective-permute-start(bf16[4,128,256]{2,1,0:T(8,128)(2,1)S(1)} %get-tuple-element.38), channel_id=1, source_target_pairs={{0,1},{1,0},{2,3},{3,2},{4,5},{5,4},{6,7},{7,6},{8,9},{9,8},{10,11... | collective-permute-start | bytes 786440 | tf_op jit(solution)/shard_map/ppermute | solution.py:446
  111.0 4.8 %collective-permute-start.17 = (bf16[2,128,256]{2,1,0:T(8,128)(2,1)S(1)}, bf16[2,128,256]{2,1,0:T(8,128)(2,1)S(1)}, u32[]{:S(2)}, u32[]{:S(2)}) collective-permute-start(bf16[2,128,256]{2,1,0:T(8,128)(2,1)S(1)} %add_convert_fusion.1), channel_id=1, source_target_pairs={{0,2},{1,3},{2,0},{3,1},{4,6},{5,7},{6,4},{7,5},{8,10},{9,11},{10,... | collective-permute-start | bytes 393224 | tf_op jit(solution)/shard_map/ppermute | solution.py:449
  115.9 9.2 %collective-permute-start.19 = (bf16[128,256]{1,0:T(8,128)(2,1)S(1)}, bf16[128,256]{1,0:T(8,128)(2,1)S(1)}, u32[]{:S(2)}, u32[]{:S(2)}) collective-permute-start(bf16[128,256]{1,0:T(8,128)(2,1)S(1)} %get-tuple-element.39), channel_id=1, source_target_pairs={{0,32},{1,160},{2,96},{3,224},{4,0},{5,128},{6,64},{7,192},{8,40},... | collective-permute-start | bytes 196616 | tf_op jit(solution)/shard_map/ppermute | solution.py:463
  118.4 11.5 %collective-permute-start.18 = (bf16[128,256]{1,0:T(8,128)(2,1)S(1)}, bf16[128,256]{1,0:T(8,128)(2,1)S(1)}, u32[]{:S(2)}, u32[]{:S(2)}) collective-permute-start(bf16[128,256]{1,0:T(8,128)(2,1)S(1)} %get-tuple-element.40), channel_id=1, source_target_pairs={{0,0},{1,128},{2,64},{3,192},{4,32},{5,160},{6,96},{7,224},{8,8},{... | collective-permute-start | bytes 196616 | tf_op jit(solution)/shard_map/ppermute | solution.py:463

commit v4 on v3

--- a/solution.py
+++ b/solution.py
@@ -429,13 +429,12 @@
     parts = [attend(mine, kv)]
     for k in range(1, nx):
         part = attend(sent[k - 1], kv)
-        if k == 1:
+        if k == 2:
             part = after(part)
             pass_on(1, 1)
-        if k == 3:
-            part = after(part)
-            pass_on(1, 0)
         parts.append(along_x(part, nx - k))
+    parts[0] = after(parts[0])
+    pass_on(1, 0)
     merged = merge(parts, nz)
     back = lax.all_to_all(merged, "cache", 0, 0, axis_index_groups=z_groups, tiled=True)
     home = (cache // nx).reshape(1)

time: 131 us -> 130 us (level)
  Pallas kernels: 55.9 us -> 48.1 us
  starting transfers between devices: 50.5 us -> 56.3 us
    pallas_call x4, Pallas kernels: 43.2 us -> 35.4 us  [attend(): pl.pallas_call(functools.partial(attend_kernel, PART), in_specs=[whole(),...]
    ppermute x9, starting transfers between devices: 10.9 us -> 17.5 us  [along_x(): return lax.ppermute(value, 'cache', pairs)]
    ppermute x1, starting transfers between devices: 9.12 us -> 5.62 us  [per_device(): theirs = lax.ppermute(theirs, 'tensor', [(t, t ^ 1) for t in range(2 * ny)])]
    ppermute x9, waiting for transfers between devices: 3.08 us -> 1.48 us  [along_x(): return lax.ppermute(value, 'cache', pairs)]
    all_to_all x1, starting transfers between devices: 3.96 us -> 5.4 us  [per_device(): lax.all_to_all(merged, 'cache', 0, 0, axis_index_groups=z_groups, tiled=T...]
    unnamed x19 -> x21, local copies, waits for them, and re-layouts: 1.64 us -> 2.79 us
  transfers between devices with their start and end apart: 22 -> 22, of which waited for: 8 -> 6; matrix products, arithmetic and copies ran while one was open for 0% -> 0% of each run, Pallas kernels for 41% -> 36%
where the time goes in v4:
time: 130 us; the launch traced here: 129 us
  starting transfers between devices  56.3 us (43%)
  Pallas kernels  48.1 us (37%)
  waiting for transfers between devices  21.7 us (17%)
  local copies, waits for them, and re-layouts  2.82 us (2%)
    pallas_call x4, Pallas kernels, attend(): pl.pallas_call(functools.partial(attend_kernel, PART), in_specs=[whole(),...  35.4 us
    ppermute x9, starting transfers between devices, along_x(): return lax.ppermute(value, 'cache', pairs)  17.5 us
    ppermute x7, starting transfers between devices, along_z(): return lax.ppermute(value, 'cache', pairs)  11.4 us
    ppermute x2, starting transfers between devices, per_device(): pieces.append(lax.ppermute(block, ('cache', 'tensor'), pairs))  10 us
    all_to_all x1, waiting for transfers between devices, per_device(): lax.all_to_all(packed, 'cache', 0, 0, axis_index_groups=z_groups, tiled=T...  6.26 us
    ppermute x1, starting transfers between devices, per_device(): theirs = lax.ppermute(theirs, 'tensor', [(t, t ^ 1) for t in range(2 * ny)])  5.62 us
    all_to_all x1, starting transfers between devices, per_device(): lax.all_to_all(merged, 'cache', 0, 0, axis_index_groups=z_groups, tiled=T...  5.4 us
    all_to_all x1, starting transfers between devices, per_device(): lax.all_to_all(packed, 'cache', 0, 0, axis_index_groups=z_groups, tiled=T...  5.29 us
  transfers between devices with their start and end apart: 22, of which 6 were waited for; matrix products, arithmetic and copies ran while one was open for 0% of the time, Pallas kernels for 36%

profile of v4, /device:TPU:17, one launch (start us, length us, event | category | flops | bytes accessed | tf_op | source)
XLA Modules:
  0.0 129.5 jit_solution(9628234528777266663)
XLA Ops:
  0.0 1.6 %collective-permute-start = (bf16[1024,256]{1,0:T(8,128)(2,1)}, bf16[1024,256]{1,0:T(8,128)(2,1)}, u32[]{:S(2)}, u32[]{:S(2)}) collective-permute-start(bf16[1024,256]{1,0:T(8,128)(2,1)} %refs_0_.1), channel_id=1, source_target_pairs={{0,32},{8,40},{16,48},{24,56},{32,64},{40,72},{48,80},{56,88},{64,... | collective-permute-start | bytes 1572872 | tf_op jit(solution)/shard_map/ppermute | solution.py:403
  1.6 3.9 %collective-permute-start.1 = (bf16[1024,256]{1,0:T(8,128)(2,1)}, bf16[1024,256]{1,0:T(8,128)(2,1)}, u32[]{:S(2)}, u32[]{:S(2)}) collective-permute-start(bf16[1024,256]{1,0:T(8,128)(2,1)} %refs_0_.1), channel_id=1, source_target_pairs={{0,224},{8,232},{16,240},{24,248},{32,0},{40,8},{48,16},{56,24},{6... | collective-permute-start | bytes 1572872 | tf_op jit(solution)/shard_map/ppermute | solution.py:403
  5.6 1.6 %pack_queries.1 = (bf16[8,64,128]{2,1,0:T(8,128)(2,1)}, bf16[8,32,128]{2,1,0:T(8,128)(2,1)S(1)}) custom-call(s32[8]{0:T(128)} %bitcast.17, bf16[8,4,1024]{2,1,0:T(4,128)(2,1)} %q_hbm.1), custom_call_target="tpu_custom_call" | custom-call | tf_op jit(solution)/shard_map/pack_queries/pallas_call | solution.py:71
  7.1 5.3 %all-to-all-start = ((bf16[8,64,128]{2,1,0:T(8,128)(2,1)}), bf16[8,64,128]{2,1,0:T(8,128)(2,1)S(1)}, u32[]{:S(2)}, u32[]{:S(2)}) async-start(bf16[8,64,128]{2,1,0:T(8,128)(2,1)} %get-tuple-element.22), calls=%async_computation | async-start | bytes 262144 | tf_op jit(solution)/shard_map/all_to_all | solution.py:420
  12.4 1.9 %load.1.kv_ref = bf16[2,6144,128]{2,1,0:T(8,128)(2,1)S(1)} custom-call(bf16[2,6144,128]{2,1,0:T(8,128)(2,1)} %source_ref.1), custom_call_target="tpu_custom_call" | custom-call | bytes 6291456 | tf_op jit(solution)/shard_map/load/pallas_call | solution.py:297
  14.3 6.3 %all-to-all-done = bf16[8,64,128]{2,1,0:T(8,128)(2,1)S(1)} async-done(((bf16[8,64,128]{2,1,0:T(8,128)(2,1)}), bf16[8,64,128]{2,1,0:T(8,128)(2,1)S(1)}, u32[]{:S(2)}, u32[]{:S(2)}) %all-to-all-start) | async-done | bytes 131104 | tf_op jit(solution)/shard_map/all_to_all | solution.py:420
  20.6 1.2 collective-permute-start.7
  21.8 1.5 %collective-permute-start.10 = (bf16[512,128]{1,0:T(8,128)(2,1)S(1)}, bf16[512,128]{1,0:T(8,128)(2,1)S(1)}, u32[]{:S(2)}, u32[]{:S(2)}) collective-permute-start(bf16[512,128]{1,0:T(8,128)(2,1)S(1)} %bitcast.14), channel_id=1, source_target_pairs={{0,24},{8,0},{16,8},{24,16},{32,56},{40,32},{48,40},{56,48},{64,88... | collective-permute-start | bytes 393224 | tf_op jit(solution)/shard_map/ppermute | solution.py:399
  23.3 1.5 %collective-permute-start.2 = (bf16[512,128]{1,0:T(8,128)(2,1)S(1)}, bf16[512,128]{1,0:T(8,128)(2,1)S(1)}, u32[]{:S(2)}, u32[]{:S(2)}) collective-permute-start(bf16[512,128]{1,0:T(8,128)(2,1)S(1)} %bitcast.15), channel_id=1, source_target_pairs={{0,16},{8,24},{16,0},{24,8},{32,48},{40,56},{48,32},{56,40},{64,80... | collective-permute-start | bytes 393224 | tf_op jit(solution)/shard_map/ppermute | solution.py:399
  24.8 2.1 %collective-permute-start.3 = (bf16[1024,256]{1,0:T(8,128)(2,1)}, bf16[1024,256]{1,0:T(8,128)(2,1)S(1)}, u32[]{:S(2)}, u32[]{:S(2)}) collective-permute-start(bf16[1024,256]{1,0:T(8,128)(2,1)} %collective-permute-done.refs_1_), channel_id=1, source_target_pairs={{0,32},{8,40},{16,48},{24,56},{32,64},{40,72},{48,80},{56,88},{64,... | collective-permute-start | bytes 1572872 | tf_op jit(solution)/shard_map/ppermute | solution.py:403
  27.5 10.7 %prefix_attention.6 = bf16[144,512]{1,0:T(8,128)(2,1)S(1)} custom-call(bf16[512,128]{1,0:T(8,128)(2,1)S(1)} %collective-permute-done.7.q_ref, bf16[2,6144,128]{2,1,0:T(8,128)(2,1)S(1)} %load.1.kv_ref), custom_call_target="tpu_custom_call" | custom-call | flops 3221225472 | bytes 3145728 | tf_op jit(solution)/shard_map/prefix_attention/pallas_call | solution.py:151
  39.2 10.9 %prefix_attention.5 = bf16[144,512]{1,0:T(8,128)(2,1)S(1)} custom-call(bf16[512,128]{1,0:T(8,128)(2,1)S(1)} %collective-permute-done.2.q_ref, bf16[2,6144,128]{2,1,0:T(8,128)(2,1)S(1)} %load.1.kv_ref), custom_call_target="tpu_custom_call" | custom-call | flops 3221225472 | bytes 3145728 | tf_op jit(solution)/shard_map/prefix_attention/pallas_call | solution.py:151
  51.1 1.8 %collective-permute-start.6 = (bf16[1024,256]{1,0:T(8,128)(2,1)S(1)}, bf16[1024,256]{1,0:T(8,128)(2,1)S(1)}, u32[]{:S(2)}, u32[]{:S(2)}) collective-permute-start(bf16[1024,256]{1,0:T(8,128)(2,1)S(1)} %collective-permute-done.4.refs_6_), channel_id=1, source_target_pairs={{0,224},{8,232},{16,240},{24,248},{32,0},{40,8},{48,16},{56,24},{6... | collective-permute-start | bytes 1572872 | tf_op jit(solution)/shard_map/ppermute | solution.py:403
  53.0 3.0 %prefix_attention.7 = bf16[144,512]{1,0:T(8,128)(2,1)S(1)} custom-call(bf16[512,128]{1,0:T(8,128)(2,1)S(1)} %collective-permute-done.10.q_ref, bf16[2,6144,128]{2,1,0:T(8,128)(2,1)S(1)} %load.1.kv_ref), custom_call_target="tpu_custom_call" | custom-call | flops 3221225472 | bytes 3145728 | tf_op jit(solution)/shard_map/prefix_attention/pallas_call | solution.py:151
  56.0 8.5 %collective-permute-start.11 = (bf16[144,512]{1,0:T(8,128)(2,1)S(1)}, bf16[144,512]{1,0:T(8,128)(2,1)S(1)}, u32[]{:S(2)}, u32[]{:S(2)}) collective-permute-start(bf16[144,512]{1,0:T(8,128)(2,1)S(1)} %prefix_attention.7), channel_id=1, source_target_pairs={{0,8},{8,16},{16,24},{24,0},{32,40},{40,48},{48,56},{56,32},{64,72... | collective-permute-start | bytes 442376 | tf_op jit(solution)/shard_map/ppermute | solution.py:399
  65.2 10.8 %prefix_attention.4.refs_0_ = bf16[144,512]{1,0:T(8,128)(2,1)S(1)} custom-call(bf16[512,128]{1,0:T(8,128)(2,1)S(1)} %bitcast.16, bf16[2,6144,128]{2,1,0:T(8,128)(2,1)S(1)} %load.1.kv_ref), custom_call_target="tpu_custom_call" | custom-call | flops 3221225472 | bytes 3145728 | tf_op jit(solution)/shard_map/prefix_attention/pallas_call | solution.py:151
  77.7 5.4 %all-to-all-start.1 = ((bf16[8,80,128]{2,1,0:T(8,128)(2,1)}), bf16[8,80,128]{2,1,0:T(8,128)(2,1)S(1)}, u32[]{:S(2)}, u32[]{:S(2)}) async-start(bf16[8,80,128]{2,1,0:T(8,128)(2,1)} %merge_parts.1), calls=%async_computation.1 | async-start | bytes 327680 | tf_op jit(solution)/shard_map/all_to_all | solution.py:439
  83.2 1.6 %copy-done = bf16[8,2,512,128]{3,2,1,0:T(8,128)(2,1)S(1)} copy-done((bf16[8,2,512,128]{3,2,1,0:T(8,128)(2,1)S(1)}, bf16[8,2,512,128]{3,2,1,0:T(8,128)(2,1)}, u32[]{:S(2)}) %copy-start) | copy-done | bytes 2097176
  84.8 3.7 %suffix_attention.1 = (f32[8,32,128]{2,1,0:T(8,128)S(1)}, f32[8,32,128]{2,1,0:T(8,128)S(1)}) custom-call(s32[8]{0:T(128)S(1)} %copy-done.5, bf16[8,32,128]{2,1,0:T(8,128)(2,1)S(1)} %get-tuple-element.32.q_ref, bf16[8,2,512,128]{3,2,1,0:T(8,128)(2,1)S(1)} %copy-done, bf16[8,2,16,128]{3,2,1,0:T(8,128)(2,1)S(1)} %pad.4.new_ref), custom_call_target="tpu_custom_call" | custom-call | tf_op jit(solution)/shard_map/suffix_attention/pallas_call | solution.py:195
  88.5 3.8 %all-to-all-done.1.back_ref = bf16[8,80,128]{2,1,0:T(8,128)(2,1)S(1)} async-done(((bf16[8,80,128]{2,1,0:T(8,128)(2,1)}), bf16[8,80,128]{2,1,0:T(8,128)(2,1)S(1)}, u32[]{:S(2)}, u32[]{:S(2)}) %all-to-all-start.1) | async-done | bytes 163872 | tf_op jit(solution)/shard_map/all_to_all | solution.py:439
  93.1 1.3 %collective-permute-start.14 = (bf16[32,1024]{1,0:T(8,128)(2,1)S(1)}, bf16[32,1024]{1,0:T(8,128)(2,1)S(1)}, u32[]{:S(2)}, u32[]{:S(2)}) collective-permute-start(bf16[32,1024]{1,0:T(8,128)(2,1)S(1)} %finish_attention.1.refs_0_), channel_id=1, source_target_pairs={{0,24},{8,0},{16,8},{24,16},{32,56},{40,32},{48,40},{56,48},{64,88... | collective-permute-start | bytes 196616 | tf_op jit(solution)/shard_map/ppermute | solution.py:399
  94.4 1.8 %collective-permute-start.13 = (bf16[32,1024]{1,0:T(8,128)(2,1)S(1)}, bf16[32,1024]{1,0:T(8,128)(2,1)S(1)}, u32[]{:S(2)}, u32[]{:S(2)}) collective-permute-start(bf16[32,1024]{1,0:T(8,128)(2,1)S(1)} %finish_attention.1.refs_0_), channel_id=1, source_target_pairs={{0,16},{8,24},{16,0},{24,8},{32,48},{40,56},{48,32},{56,40},{64,80... | collective-permute-start | bytes 196616 | tf_op jit(solution)/shard_map/ppermute | solution.py:399
  97.1 2.0 %load_all.1.refs_4_ = bf16[8,1024,256]{2,1,0:T(8,128)(2,1)S(1)} custom-call(s32[1]{0:T(128)} %bitcast.4.home_ref.place_ref, bf16[1024,256]{1,0:T(8,128)(2,1)S(1)} %copy-done.1, bf16[1024,256]{1,0:T(8,128)(2,1)} %collective-permute-done.refs_1_, bf16[1024,256]{1,0:T(8,128)(2,1)S(1)} %copy-done.3, bf16[1024,256]{1,0:T(8,128)(2,1)} %collective-permute-done.5.refs_3_, ...), custom_call_target="tpu_custom_call" | custom-call | tf_op jit(solution)/shard_map/load_all/pallas_call | solution.py:327
  99.1 1.5 %collective-permute-done.12.refs_1_ = bf16[32,1024]{1,0:T(8,128)(2,1)S(1)} collective-permute-done((bf16[32,1024]{1,0:T(8,128)(2,1)S(1)}, bf16[32,1024]{1,0:T(8,128)(2,1)S(1)}, u32[]{:S(2)}, u32[]{:S(2)}) %collective-permute-start.12) | collective-permute-done | bytes 65568 | tf_op jit(solution)/shard_map/ppermute | solution.py:399
  100.5 1.3 project.1
  101.8 5.6 %collective-permute-start.16 = (bf16[4,128,256]{2,1,0:T(8,128)(2,1)S(1)}, bf16[4,128,256]{2,1,0:T(8,128)(2,1)S(1)}, u32[]{:S(2)}, u32[]{:S(2)}) collective-permute-start(bf16[4,128,256]{2,1,0:T(8,128)(2,1)S(1)} %get-tuple-element.38), channel_id=1, source_target_pairs={{0,1},{1,0},{2,3},{3,2},{4,5},{5,4},{6,7},{7,6},{8,9},{9,8},{10,11... | collective-permute-start | bytes 786440 | tf_op jit(solution)/shard_map/ppermute | solution.py:445
  107.4 1.2 collective-permute-done.16
  108.6 1.1 collective-permute-start.17
  109.7 3.7 %collective-permute-done.17 = bf16[2,128,256]{2,1,0:T(8,128)(2,1)S(1)} collective-permute-done((bf16[2,128,256]{2,1,0:T(8,128)(2,1)S(1)}, bf16[2,128,256]{2,1,0:T(8,128)(2,1)S(1)}, u32[]{:S(2)}, u32[]{:S(2)}) %collective-permute-start.17) | collective-permute-done | bytes 131104 | tf_op jit(solution)/shard_map/ppermute | solution.py:448
  113.5 4.3 %collective-permute-start.19 = (bf16[128,256]{1,0:T(8,128)(2,1)S(1)}, bf16[128,256]{1,0:T(8,128)(2,1)S(1)}, u32[]{:S(2)}, u32[]{:S(2)}) collective-permute-start(bf16[128,256]{1,0:T(8,128)(2,1)S(1)} %get-tuple-element.39), channel_id=1, source_target_pairs={{0,32},{1,160},{2,96},{3,224},{4,0},{5,128},{6,64},{7,192},{8,40},... | collective-permute-start | bytes 196616 | tf_op jit(solution)/shard_map/ppermute | solution.py:462
  117.8 5.7 %collective-permute-start.18 = (bf16[128,256]{1,0:T(8,128)(2,1)S(1)}, bf16[128,256]{1,0:T(8,128)(2,1)S(1)}, u32[]{:S(2)}, u32[]{:S(2)}) collective-permute-start(bf16[128,256]{1,0:T(8,128)(2,1)S(1)} %get-tuple-element.40), channel_id=1, source_target_pairs={{0,0},{1,128},{2,64},{3,192},{4,32},{5,160},{6,96},{7,224},{8,8},{... | collective-permute-start | bytes 196616 | tf_op jit(solution)/shard_map/ppermute | solution.py:462
  123.5 5.3 %collective-permute-done.18.refs_0_ = bf16[128,256]{1,0:T(8,128)(2,1)S(1)} collective-permute-done((bf16[128,256]{1,0:T(8,128)(2,1)S(1)}, bf16[128,256]{1,0:T(8,128)(2,1)S(1)}, u32[]{:S(2)}, u32[]{:S(2)}) %collective-permute-start.18) | collective-permute-done | bytes 65568 | tf_op jit(solution)/shard_map/ppermute | solution.py:462
  (50 shorter events, 7.4 us)
Async XLA Ops:
  0.0 20.6 %collective-permute-start = (bf16[1024,256]{1,0:T(8,128)(2,1)}, bf16[1024,256]{1,0:T(8,128)(2,1)}, u32[]{:S(2)}, u32[]{:S(2)}) collective-permute-start(bf16[1024,256]{1,0:T(8,128)(2,1)} %refs_0_.1), channel_id=1, source_target_pairs={{0,32},{8,40},{16,48},{24,56},{32,64},{40,72},{48,80},{56,88},{64,... | collective-permute-start | bytes 1572872 | tf_op jit(solution)/shard_map/ppermute | solution.py:403
  1.6 19.0 %collective-permute-start.1 = (bf16[1024,256]{1,0:T(8,128)(2,1)}, bf16[1024,256]{1,0:T(8,128)(2,1)}, u32[]{:S(2)}, u32[]{:S(2)}) collective-permute-start(bf16[1024,256]{1,0:T(8,128)(2,1)} %refs_0_.1), channel_id=1, source_target_pairs={{0,224},{8,232},{16,240},{24,248},{32,0},{40,8},{48,16},{56,24},{6... | collective-permute-start | bytes 1572872 | tf_op jit(solution)/shard_map/ppermute | solution.py:403
  7.1 13.5 %all-to-all-start = ((bf16[8,64,128]{2,1,0:T(8,128)(2,1)}), bf16[8,64,128]{2,1,0:T(8,128)(2,1)S(1)}, u32[]{:S(2)}, u32[]{:S(2)}) async-start(bf16[8,64,128]{2,1,0:T(8,128)(2,1)} %get-tuple-element.22), calls=%async_computation | async-start | bytes 262144 | tf_op jit(solution)/shard_map/all_to_all | solution.py:420
  20.6 6.9 %collective-permute-start.7 = (bf16[512,128]{1,0:T(8,128)(2,1)S(1)}, bf16[512,128]{1,0:T(8,128)(2,1)S(1)}, u32[]{:S(2)}, u32[]{:S(2)}) collective-permute-start(bf16[512,128]{1,0:T(8,128)(2,1)S(1)} %bitcast.13), channel_id=1, source_target_pairs={{0,8},{8,16},{16,24},{24,0},{32,40},{40,48},{48,56},{56,32},{64,72... | collective-permute-start | bytes 393224 | tf_op jit(solution)/shard_map/ppermute | solution.py:399
  21.8 31.1 %collective-permute-start.10 = (bf16[512,128]{1,0:T(8,128)(2,1)S(1)}, bf16[512,128]{1,0:T(8,128)(2,1)S(1)}, u32[]{:S(2)}, u32[]{:S(2)}) collective-permute-start(bf16[512,128]{1,0:T(8,128)(2,1)S(1)} %bitcast.14), channel_id=1, source_target_pairs={{0,24},{8,0},{16,8},{24,16},{32,56},{40,32},{48,40},{56,48},{64,88... | collective-permute-start | bytes 393224 | tf_op jit(solution)/shard_map/ppermute | solution.py:399
  23.3 15.9 %collective-permute-start.2 = (bf16[512,128]{1,0:T(8,128)(2,1)S(1)}, bf16[512,128]{1,0:T(8,128)(2,1)S(1)}, u32[]{:S(2)}, u32[]{:S(2)}) collective-permute-start(bf16[512,128]{1,0:T(8,128)(2,1)S(1)} %bitcast.15), channel_id=1, source_target_pairs={{0,16},{8,24},{16,0},{24,8},{32,48},{40,56},{48,32},{56,40},{64,80... | collective-permute-start | bytes 393224 | tf_op jit(solution)/shard_map/ppermute | solution.py:399
  24.8 25.3 %collective-permute-start.3 = (bf16[1024,256]{1,0:T(8,128)(2,1)}, bf16[1024,256]{1,0:T(8,128)(2,1)S(1)}, u32[]{:S(2)}, u32[]{:S(2)}) collective-permute-start(bf16[1024,256]{1,0:T(8,128)(2,1)} %collective-permute-done.refs_1_), channel_id=1, source_target_pairs={{0,32},{8,40},{16,48},{24,56},{32,64},{40,72},{48,80},{56,88},{64,... | collective-permute-start | bytes 1572872 | tf_op jit(solution)/shard_map/ppermute | solution.py:403
  26.9 23.3 %collective-permute-start.4 = (bf16[1024,256]{1,0:T(8,128)(2,1)}, bf16[1024,256]{1,0:T(8,128)(2,1)S(1)}, u32[]{:S(2)}, u32[]{:S(2)}) collective-permute-start(bf16[1024,256]{1,0:T(8,128)(2,1)} %collective-permute-done.1.refs_5_), channel_id=1, source_target_pairs={{0,224},{8,232},{16,240},{24,248},{32,0},{40,8},{48,16},{56,24},{6... | collective-permute-start | bytes 1572872 | tf_op jit(solution)/shard_map/ppermute | solution.py:403
  38.3 38.2 %collective-permute-start.8 = (bf16[144,512]{1,0:T(8,128)(2,1)S(1)}, bf16[144,512]{1,0:T(8,128)(2,1)S(1)}, u32[]{:S(2)}, u32[]{:S(2)}) collective-permute-start(bf16[144,512]{1,0:T(8,128)(2,1)S(1)} %prefix_attention.6), channel_id=1, source_target_pairs={{0,24},{8,0},{16,8},{24,16},{32,56},{40,32},{48,40},{56,48},{64,88... | collective-permute-start | bytes 442376 | tf_op jit(solution)/shard_map/ppermute | solution.py:399
  50.2 5.8 %copy-start.2 = (bf16[1024,256]{1,0:T(8,128)(2,1)}, bf16[1024,256]{1,0:T(8,128)(2,1)S(1)}, u32[]{:S(2)}) copy-start(bf16[1024,256]{1,0:T(8,128)(2,1)S(1)} %collective-permute-done.3.refs_2_) | copy-start | bytes 1572868
  50.2 5.7 %copy-start.6 = (bf16[1024,256]{1,0:T(8,128)(2,1)}, bf16[1024,256]{1,0:T(8,128)(2,1)S(1)}, u32[]{:S(2)}) copy-start(bf16[1024,256]{1,0:T(8,128)(2,1)S(1)} %collective-permute-done.4.refs_6_) | copy-start | bytes 1572868
  50.2 25.8 %collective-permute-start.5 = (bf16[1024,256]{1,0:T(8,128)(2,1)S(1)}, bf16[1024,256]{1,0:T(8,128)(2,1)}, u32[]{:S(2)}, u32[]{:S(2)}) collective-permute-start(bf16[1024,256]{1,0:T(8,128)(2,1)S(1)} %collective-permute-done.3.refs_2_), channel_id=1, source_target_pairs={{0,32},{8,40},{16,48},{24,56},{32,64},{40,72},{48,80},{56,88},{64,... | collective-permute-start | bytes 1572872 | tf_op jit(solution)/shard_map/ppermute | solution.py:403
  51.1 24.9 %collective-permute-start.6 = (bf16[1024,256]{1,0:T(8,128)(2,1)S(1)}, bf16[1024,256]{1,0:T(8,128)(2,1)S(1)}, u32[]{:S(2)}, u32[]{:S(2)}) collective-permute-start(bf16[1024,256]{1,0:T(8,128)(2,1)S(1)} %collective-permute-done.4.refs_6_), channel_id=1, source_target_pairs={{0,224},{8,232},{16,240},{24,248},{32,0},{40,8},{48,16},{56,24},{6... | collective-permute-start | bytes 1572872 | tf_op jit(solution)/shard_map/ppermute | solution.py:403
  55.9 27.1 %copy-start.9 = (bf16[8,4,2,128]{3,2,1,0:T(2,128)(2,1)S(1)}, bf16[8,4,2,128]{3,2,1,0:T(2,128)(2,1)}, u32[]{:S(2)}) copy-start(bf16[8,4,2,128]{3,2,1,0:T(2,128)(2,1)} %param.8) | copy-start | bytes 49156
  56.0 27.2 %copy-start.5 = (s32[8]{0:T(128)S(1)}, s32[8]{0:T(128)}, u32[]{:S(2)}) copy-start(s32[8]{0:T(128)} %len_ref.1) | copy-start | bytes 100
  56.0 20.5 %collective-permute-start.11 = (bf16[144,512]{1,0:T(8,128)(2,1)S(1)}, bf16[144,512]{1,0:T(8,128)(2,1)S(1)}, u32[]{:S(2)}, u32[]{:S(2)}) collective-permute-start(bf16[144,512]{1,0:T(8,128)(2,1)S(1)} %prefix_attention.7), channel_id=1, source_target_pairs={{0,8},{8,16},{16,24},{24,0},{32,40},{40,48},{48,56},{56,32},{64,72... | collective-permute-start | bytes 442376 | tf_op jit(solution)/shard_map/ppermute | solution.py:399
  64.4 12.0 %collective-permute-start.9 = (bf16[144,512]{1,0:T(8,128)(2,1)S(1)}, bf16[144,512]{1,0:T(8,128)(2,1)S(1)}, u32[]{:S(2)}, u32[]{:S(2)}) collective-permute-start(bf16[144,512]{1,0:T(8,128)(2,1)S(1)} %prefix_attention.5), channel_id=1, source_target_pairs={{0,16},{8,24},{16,0},{24,8},{32,48},{40,56},{48,32},{56,40},{64,80... | collective-permute-start | bytes 442376 | tf_op jit(solution)/shard_map/ppermute | solution.py:399
  76.0 16.4 %copy-start.4 = (s32[8,1]{0,1:T(1,128)S(1)}, s32[8,1]{0,1:T(1,128)}, u32[]{:S(2)}) copy-start(s32[8,1]{0,1:T(1,128)} %param.12) | copy-start | bytes 100
  76.0 21.1 %copy-start.1 = (bf16[1024,256]{1,0:T(8,128)(2,1)S(1)}, bf16[1024,256]{1,0:T(8,128)(2,1)}, u32[]{:S(2)}) copy-start(bf16[1024,256]{1,0:T(8,128)(2,1)} %refs_0_.1) | copy-start | bytes 1572868
  76.0 21.1 %copy-start.3 = (bf16[1024,256]{1,0:T(8,128)(2,1)S(1)}, bf16[1024,256]{1,0:T(8,128)(2,1)}, u32[]{:S(2)}) copy-start(bf16[1024,256]{1,0:T(8,128)(2,1)} %copy-done.2) | copy-start | bytes 1572868
  76.0 0.8 copy-start.7
  76.0 20.3 %collective-permute-start.15 = (bf16[1024,256]{1,0:T(8,128)(2,1)}, bf16[1024,256]{1,0:T(8,128)(2,1)S(1)}, u32[]{:S(2)}, u32[]{:S(2)}) collective-permute-start(bf16[1024,256]{1,0:T(8,128)(2,1)} %collective-permute-done.5.refs_3_), channel_id=1, source_target_pairs={{0,32},{8,40},{16,48},{24,56},{32,64},{40,72},{48,80},{56,88},{64,... | collective-permute-start | bytes 1572872 | tf_op jit(solution)/shard_map/ppermute | solution.py:403
  77.7 14.6 %all-to-all-start.1 = ((bf16[8,80,128]{2,1,0:T(8,128)(2,1)}), bf16[8,80,128]{2,1,0:T(8,128)(2,1)S(1)}, u32[]{:S(2)}, u32[]{:S(2)}) async-start(bf16[8,80,128]{2,1,0:T(8,128)(2,1)} %merge_parts.1), calls=%async_computation.1 | async-start | bytes 327680 | tf_op jit(solution)/shard_map/all_to_all | solution.py:439
  83.2 1.6 %copy-start = (bf16[8,2,512,128]{3,2,1,0:T(8,128)(2,1)S(1)}, bf16[8,2,512,128]{3,2,1,0:T(8,128)(2,1)}, u32[]{:S(2)}) copy-start(bf16[8,2,512,128]{3,2,1,0:T(8,128)(2,1)} %kv_ref.1) | copy-start | bytes 6291460
  93.1 5.9 %collective-permute-start.14 = (bf16[32,1024]{1,0:T(8,128)(2,1)S(1)}, bf16[32,1024]{1,0:T(8,128)(2,1)S(1)}, u32[]{:S(2)}, u32[]{:S(2)}) collective-permute-start(bf16[32,1024]{1,0:T(8,128)(2,1)S(1)} %finish_attention.1.refs_0_), channel_id=1, source_target_pairs={{0,24},{8,0},{16,8},{24,16},{32,56},{40,32},{48,40},{56,48},{64,88... | collective-permute-start | bytes 196616 | tf_op jit(solution)/shard_map/ppermute | solution.py:399
  94.4 4.6 %collective-permute-start.13 = (bf16[32,1024]{1,0:T(8,128)(2,1)S(1)}, bf16[32,1024]{1,0:T(8,128)(2,1)S(1)}, u32[]{:S(2)}, u32[]{:S(2)}) collective-permute-start(bf16[32,1024]{1,0:T(8,128)(2,1)S(1)} %finish_attention.1.refs_0_), channel_id=1, source_target_pairs={{0,16},{8,24},{16,0},{24,8},{32,48},{40,56},{48,32},{56,40},{64,80... | collective-permute-start | bytes 196616 | tf_op jit(solution)/shard_map/ppermute | solution.py:399
  96.2 4.3 %collective-permute-start.12 = (bf16[32,1024]{1,0:T(8,128)(2,1)S(1)}, bf16[32,1024]{1,0:T(8,128)(2,1)S(1)}, u32[]{:S(2)}, u32[]{:S(2)}) collective-permute-start(bf16[32,1024]{1,0:T(8,128)(2,1)S(1)} %finish_attention.1.refs_0_), channel_id=1, source_target_pairs={{0,8},{8,16},{16,24},{24,0},{32,40},{40,48},{48,56},{56,32},{64,72... | collective-permute-start | bytes 196616 | tf_op jit(solution)/shard_map/ppermute | solution.py:399
  96.3 0.8 copy-start.8
  101.8 6.8 %collective-permute-start.16 = (bf16[4,128,256]{2,1,0:T(8,128)(2,1)S(1)}, bf16[4,128,256]{2,1,0:T(8,128)(2,1)S(1)}, u32[]{:S(2)}, u32[]{:S(2)}) collective-permute-start(bf16[4,128,256]{2,1,0:T(8,128)(2,1)S(1)} %get-tuple-element.38), channel_id=1, source_target_pairs={{0,1},{1,0},{2,3},{3,2},{4,5},{5,4},{6,7},{7,6},{8,9},{9,8},{10,11... | collective-permute-start | bytes 786440 | tf_op jit(solution)/shard_map/ppermute | solution.py:445
  108.6 4.8 %collective-permute-start.17 = (bf16[2,128,256]{2,1,0:T(8,128)(2,1)S(1)}, bf16[2,128,256]{2,1,0:T(8,128)(2,1)S(1)}, u32[]{:S(2)}, u32[]{:S(2)}) collective-permute-start(bf16[2,128,256]{2,1,0:T(8,128)(2,1)S(1)} %add_convert_fusion.1), channel_id=1, source_target_pairs={{0,2},{1,3},{2,0},{3,1},{4,6},{5,7},{6,4},{7,5},{8,10},{9,11},{10,... | collective-permute-start | bytes 393224 | tf_op jit(solution)/shard_map/ppermute | solution.py:448
  113.5 10.0 %collective-permute-start.19 = (bf16[128,256]{1,0:T(8,128)(2,1)S(1)}, bf16[128,256]{1,0:T(8,128)(2,1)S(1)}, u32[]{:S(2)}, u32[]{:S(2)}) collective-permute-start(bf16[128,256]{1,0:T(8,128)(2,1)S(1)} %get-tuple-element.39), channel_id=1, source_target_pairs={{0,32},{1,160},{2,96},{3,224},{4,0},{5,128},{6,64},{7,192},{8,40},... | collective-permute-start | bytes 196616 | tf_op jit(solution)/shard_map/ppermute | solution.py:462
  117.8 11.0 %collective-permute-start.18 = (bf16[128,256]{1,0:T(8,128)(2,1)S(1)}, bf16[128,256]{1,0:T(8,128)(2,1)S(1)}, u32[]{:S(2)}, u32[]{:S(2)}) collective-permute-start(bf16[128,256]{1,0:T(8,128)(2,1)S(1)} %get-tuple-element.40), channel_id=1, source_target_pairs={{0,0},{1,128},{2,64},{3,192},{4,32},{5,160},{6,96},{7,224},{8,8},{... | collective-permute-start | bytes 196616 | tf_op jit(solution)/shard_map/ppermute | solution.py:462

commit v5 on v4

--- a/solution.py
+++ b/solution.py
@@ -42,19 +42,9 @@
     return high, middle, rest - middle
 
 
-def pack_kernel(
-    branches, steps, group, prompt_hbm, q_hbm, packed_ref, rows_ref, prompt_ref, q_ref, sem
-):
+def pack_kernel(branches, steps, group, prompt_ref, q_ref, packed_ref, rows_ref):
     height = steps * group
-    copies = [
-        pltpu.make_async_copy(prompt_hbm, prompt_ref, sem.at[0]),
-        pltpu.make_async_copy(q_hbm, q_ref, sem.at[1]),
-    ]
-    for copy in copies:
-        copy.start()
     packed_ref[...] = jnp.zeros_like(packed_ref)
-    for copy in copies:
-        copy.wait()
     for b in range(branches):
         own = q_ref[b].astype(F32)
         rows = jnp.concatenate(
@@ -70,23 +60,15 @@
     height = steps * group
     return pl.pallas_call(
         functools.partial(pack_kernel, branches, steps, group),
-        in_specs=[whole(pltpu.HBM), whole(pltpu.HBM)],
+        in_specs=[whole(pltpu.SMEM), whole()],
         out_specs=[whole(), whole()],
         out_shape=[
             jax.ShapeDtypeStruct((PROMPTS, SLOTS * height, HEAD_DIM), BF16),
             jax.ShapeDtypeStruct((branches, height, HEAD_DIM), BF16),
         ],
-        scratch_shapes=[
-            pltpu.SMEM((branches,), jnp.int32),
-            pltpu.VMEM(queries.shape, BF16),
-            pltpu.SemaphoreType.DMA((2,)),
-        ],
         compiler_params=params(),
         name="pack_queries",
-    )(
-        pltpu.with_memory_space_constraint(prompt_ids, pltpu.HBM),
-        pltpu.with_memory_space_constraint(queries, pltpu.HBM),
-    )
+    )(prompt_ids, queries)
 
 
 def attend_kernel(part, q_ref, kv_ref, out_ref, qt_ref, top_ref, total_ref, acc_ref):

time: 130 us -> 130 us (level)
  starting transfers between devices: 56.3 us -> 48.4 us
  Pallas kernels: 48.1 us -> 55.6 us
  local copies, waits for them, and re-layouts: 2.82 us -> 4.62 us
  waiting for transfers between devices: 21.7 us -> 20.4 us
    pallas_call x4, Pallas kernels: 35.4 us -> 43.2 us  [attend(): pl.pallas_call(functools.partial(attend_kernel, PART), in_specs=[whole(),...]
    ppermute x9, starting transfers between devices: 17.5 us -> 10.4 us  [along_x(): return lax.ppermute(value, 'cache', pairs)]
    unnamed x21 -> x25, local copies, waits for them, and re-layouts: 2.79 us -> 4.59 us
  transfers between devices with their start and end apart: 22 -> 22, of which waited for: 6 -> 6; matrix products, arithmetic and copies ran while one was open for 0% -> 0% of each run, Pallas kernels for 36% -> 41%
where the time goes in v5:
time: 130 us; the launch traced here: 129 us
  Pallas kernels  55.6 us (43%)
  starting transfers between devices  48.4 us (37%)
  waiting for transfers between devices  20.4 us (16%)
  local copies, waits for them, and re-layouts  4.62 us (4%)
    pallas_call x4, Pallas kernels, attend(): pl.pallas_call(functools.partial(attend_kernel, PART), in_specs=[whole(),...  43.2 us
    ppermute x7, starting transfers between devices, along_z(): return lax.ppermute(value, 'cache', pairs)  11.1 us
    ppermute x9, starting transfers between devices, along_x(): return lax.ppermute(value, 'cache', pairs)  10.4 us
    ppermute x2, starting transfers between devices, per_device(): pieces.append(lax.ppermute(block, ('cache', 'tensor'), pairs))  9.8 us
    ppermute x1, starting transfers between devices, per_device(): theirs = lax.ppermute(theirs, 'tensor', [(t, t ^ 1) for t in range(2 * ny)])  6.3 us
    all_to_all x1, waiting for transfers between devices, per_device(): lax.all_to_all(packed, 'cache', 0, 0, axis_index_groups=z_groups, tiled=T...  5.34 us
    all_to_all x1, starting transfers between devices, per_device(): lax.all_to_all(packed, 'cache', 0, 0, axis_index_groups=z_groups, tiled=T...  5.28 us
    ppermute x2, waiting for transfers between devices, per_device(): pieces.append(lax.ppermute(block, ('cache', 'tensor'), pairs))  4.79 us
  transfers between devices with their start and end apart: 22, of which 6 were waited for; matrix products, arithmetic and copies ran while one was open for 0% of the time, Pallas kernels for 41%

profile of v5, /device:TPU:17, one launch (start us, length us, event | category | flops | bytes accessed | tf_op | source)
XLA Modules:
  0.0 129.5 jit_solution(14636559442386337018)
XLA Ops:
  0.0 1.6 %collective-permute-start = (bf16[1024,256]{1,0:T(8,128)(2,1)}, bf16[1024,256]{1,0:T(8,128)(2,1)}, u32[]{:S(2)}, u32[]{:S(2)}) collective-permute-start(bf16[1024,256]{1,0:T(8,128)(2,1)} %refs_0_.1), channel_id=1, source_target_pairs={{0,32},{8,40},{16,48},{24,56},{32,64},{40,72},{48,80},{56,88},{64,... | collective-permute-start | bytes 1572872 | tf_op jit(solution)/shard_map/ppermute | solution.py:385
  1.6 3.9 %collective-permute-start.1 = (bf16[1024,256]{1,0:T(8,128)(2,1)}, bf16[1024,256]{1,0:T(8,128)(2,1)}, u32[]{:S(2)}, u32[]{:S(2)}) collective-permute-start(bf16[1024,256]{1,0:T(8,128)(2,1)} %refs_0_.1), channel_id=1, source_target_pairs={{0,224},{8,232},{16,240},{24,248},{32,0},{40,8},{48,16},{56,24},{6... | collective-permute-start | bytes 1572872 | tf_op jit(solution)/shard_map/ppermute | solution.py:385
  7.1 1.2 pack_queries.1
  8.3 5.3 %all-to-all-start = ((bf16[8,64,128]{2,1,0:T(8,128)(2,1)}), bf16[8,64,128]{2,1,0:T(8,128)(2,1)S(1)}, u32[]{:S(2)}, u32[]{:S(2)}) async-start(bf16[8,64,128]{2,1,0:T(8,128)(2,1)} %get-tuple-element.22), calls=%async_computation | async-start | bytes 262144 | tf_op jit(solution)/shard_map/all_to_all | solution.py:402
  13.6 1.9 %load.1.kv_ref = bf16[2,6144,128]{2,1,0:T(8,128)(2,1)S(1)} custom-call(bf16[2,6144,128]{2,1,0:T(8,128)(2,1)} %source_ref.1), custom_call_target="tpu_custom_call" | custom-call | bytes 6291456 | tf_op jit(solution)/shard_map/load/pallas_call | solution.py:279
  15.5 5.3 %all-to-all-done = bf16[8,64,128]{2,1,0:T(8,128)(2,1)S(1)} async-done(((bf16[8,64,128]{2,1,0:T(8,128)(2,1)}), bf16[8,64,128]{2,1,0:T(8,128)(2,1)S(1)}, u32[]{:S(2)}, u32[]{:S(2)}) %all-to-all-start) | async-done | bytes 131104 | tf_op jit(solution)/shard_map/all_to_all | solution.py:402
  20.9 1.2 collective-permute-start.7
  22.1 1.5 %collective-permute-start.10 = (bf16[512,128]{1,0:T(8,128)(2,1)S(1)}, bf16[512,128]{1,0:T(8,128)(2,1)S(1)}, u32[]{:S(2)}, u32[]{:S(2)}) collective-permute-start(bf16[512,128]{1,0:T(8,128)(2,1)S(1)} %bitcast.14), channel_id=1, source_target_pairs={{0,24},{8,0},{16,8},{24,16},{32,56},{40,32},{48,40},{56,48},{64,88... | collective-permute-start | bytes 393224 | tf_op jit(solution)/shard_map/ppermute | solution.py:381
  23.5 1.5 %collective-permute-start.2 = (bf16[512,128]{1,0:T(8,128)(2,1)S(1)}, bf16[512,128]{1,0:T(8,128)(2,1)S(1)}, u32[]{:S(2)}, u32[]{:S(2)}) collective-permute-start(bf16[512,128]{1,0:T(8,128)(2,1)S(1)} %bitcast.15), channel_id=1, source_target_pairs={{0,16},{8,24},{16,0},{24,8},{32,48},{40,56},{48,32},{56,40},{64,80... | collective-permute-start | bytes 393224 | tf_op jit(solution)/shard_map/ppermute | solution.py:381
  25.1 1.9 %collective-permute-start.3 = (bf16[1024,256]{1,0:T(8,128)(2,1)}, bf16[1024,256]{1,0:T(8,128)(2,1)S(1)}, u32[]{:S(2)}, u32[]{:S(2)}) collective-permute-start(bf16[1024,256]{1,0:T(8,128)(2,1)} %collective-permute-done.refs_1_), channel_id=1, source_target_pairs={{0,32},{8,40},{16,48},{24,56},{32,64},{40,72},{48,80},{56,88},{64,... | collective-permute-start | bytes 1572872 | tf_op jit(solution)/shard_map/ppermute | solution.py:385
  27.8 10.7 %prefix_attention.6 = bf16[144,512]{1,0:T(8,128)(2,1)S(1)} custom-call(bf16[512,128]{1,0:T(8,128)(2,1)S(1)} %collective-permute-done.7.q_ref, bf16[2,6144,128]{2,1,0:T(8,128)(2,1)S(1)} %load.1.kv_ref), custom_call_target="tpu_custom_call" | custom-call | flops 3221225472 | bytes 3145728 | tf_op jit(solution)/shard_map/prefix_attention/pallas_call | solution.py:133
  39.5 10.9 %prefix_attention.5 = bf16[144,512]{1,0:T(8,128)(2,1)S(1)} custom-call(bf16[512,128]{1,0:T(8,128)(2,1)S(1)} %collective-permute-done.2.q_ref, bf16[2,6144,128]{2,1,0:T(8,128)(2,1)S(1)} %load.1.kv_ref), custom_call_target="tpu_custom_call" | custom-call | flops 3221225472 | bytes 3145728 | tf_op jit(solution)/shard_map/prefix_attention/pallas_call | solution.py:133
  50.5 2.7 %collective-permute-start.6 = (bf16[1024,256]{1,0:T(8,128)(2,1)S(1)}, bf16[1024,256]{1,0:T(8,128)(2,1)S(1)}, u32[]{:S(2)}, u32[]{:S(2)}) collective-permute-start(bf16[1024,256]{1,0:T(8,128)(2,1)S(1)} %collective-permute-done.4.refs_6_), channel_id=1, source_target_pairs={{0,224},{8,232},{16,240},{24,248},{32,0},{40,8},{48,16},{56,24},{6... | collective-permute-start | bytes 1572872 | tf_op jit(solution)/shard_map/ppermute | solution.py:385
  53.2 10.8 %prefix_attention.7 = bf16[144,512]{1,0:T(8,128)(2,1)S(1)} custom-call(bf16[512,128]{1,0:T(8,128)(2,1)S(1)} %collective-permute-done.10.q_ref, bf16[2,6144,128]{2,1,0:T(8,128)(2,1)S(1)} %load.1.kv_ref), custom_call_target="tpu_custom_call" | custom-call | flops 3221225472 | bytes 3145728 | tf_op jit(solution)/shard_map/prefix_attention/pallas_call | solution.py:133
  64.7 1.4 %collective-permute-start.9 = (bf16[144,512]{1,0:T(8,128)(2,1)S(1)}, bf16[144,512]{1,0:T(8,128)(2,1)S(1)}, u32[]{:S(2)}, u32[]{:S(2)}) collective-permute-start(bf16[144,512]{1,0:T(8,128)(2,1)S(1)} %prefix_attention.5), channel_id=1, source_target_pairs={{0,16},{8,24},{16,0},{24,8},{32,48},{40,56},{48,32},{56,40},{64,80... | collective-permute-start | bytes 442376 | tf_op jit(solution)/shard_map/ppermute | solution.py:381
  66.1 10.8 %prefix_attention.4.refs_0_ = bf16[144,512]{1,0:T(8,128)(2,1)S(1)} custom-call(bf16[512,128]{1,0:T(8,128)(2,1)S(1)} %bitcast.16, bf16[2,6144,128]{2,1,0:T(8,128)(2,1)S(1)} %load.1.kv_ref), custom_call_target="tpu_custom_call" | custom-call | flops 3221225472 | bytes 3145728 | tf_op jit(solution)/shard_map/prefix_attention/pallas_call | solution.py:133
  78.6 4.5 %all-to-all-start.1 = ((bf16[8,80,128]{2,1,0:T(8,128)(2,1)}), bf16[8,80,128]{2,1,0:T(8,128)(2,1)S(1)}, u32[]{:S(2)}, u32[]{:S(2)}) async-start(bf16[8,80,128]{2,1,0:T(8,128)(2,1)} %merge_parts.1), calls=%async_computation.1 | async-start | bytes 327680 | tf_op jit(solution)/shard_map/all_to_all | solution.py:421
  83.2 1.6 %copy-done = bf16[8,2,512,128]{3,2,1,0:T(8,128)(2,1)S(1)} copy-done((bf16[8,2,512,128]{3,2,1,0:T(8,128)(2,1)S(1)}, bf16[8,2,512,128]{3,2,1,0:T(8,128)(2,1)}, u32[]{:S(2)}) %copy-start) | copy-done | bytes 2097176
  84.8 3.7 %suffix_attention.1 = (f32[8,32,128]{2,1,0:T(8,128)S(1)}, f32[8,32,128]{2,1,0:T(8,128)S(1)}) custom-call(s32[8]{0:T(128)S(1)} %copy-done.7, bf16[8,32,128]{2,1,0:T(8,128)(2,1)S(1)} %get-tuple-element.32.q_ref, bf16[8,2,512,128]{3,2,1,0:T(8,128)(2,1)S(1)} %copy-done, bf16[8,2,16,128]{3,2,1,0:T(8,128)(2,1)S(1)} %pad.4.new_ref), custom_call_target="tpu_custom_call" | custom-call | tf_op jit(solution)/shard_map/suffix_attention/pallas_call | solution.py:177
  88.5 3.8 %all-to-all-done.1.back_ref = bf16[8,80,128]{2,1,0:T(8,128)(2,1)S(1)} async-done(((bf16[8,80,128]{2,1,0:T(8,128)(2,1)}), bf16[8,80,128]{2,1,0:T(8,128)(2,1)S(1)}, u32[]{:S(2)}, u32[]{:S(2)}) %all-to-all-start.1) | async-done | bytes 163872 | tf_op jit(solution)/shard_map/all_to_all | solution.py:421
  93.1 1.3 %collective-permute-start.14 = (bf16[32,1024]{1,0:T(8,128)(2,1)S(1)}, bf16[32,1024]{1,0:T(8,128)(2,1)S(1)}, u32[]{:S(2)}, u32[]{:S(2)}) collective-permute-start(bf16[32,1024]{1,0:T(8,128)(2,1)S(1)} %finish_attention.1.refs_0_), channel_id=1, source_target_pairs={{0,24},{8,0},{16,8},{24,16},{32,56},{40,32},{48,40},{56,48},{64,88... | collective-permute-start | bytes 196616 | tf_op jit(solution)/shard_map/ppermute | solution.py:381
  94.4 1.8 %collective-permute-start.13 = (bf16[32,1024]{1,0:T(8,128)(2,1)S(1)}, bf16[32,1024]{1,0:T(8,128)(2,1)S(1)}, u32[]{:S(2)}, u32[]{:S(2)}) collective-permute-start(bf16[32,1024]{1,0:T(8,128)(2,1)S(1)} %finish_attention.1.refs_0_), channel_id=1, source_target_pairs={{0,16},{8,24},{16,0},{24,8},{32,48},{40,56},{48,32},{56,40},{64,80... | collective-permute-start | bytes 196616 | tf_op jit(solution)/shard_map/ppermute | solution.py:381
  97.1 2.0 %load_all.1.refs_4_ = bf16[8,1024,256]{2,1,0:T(8,128)(2,1)S(1)} custom-call(s32[1]{0:T(128)} %bitcast.4.home_ref.place_ref, bf16[1024,256]{1,0:T(8,128)(2,1)S(1)} %copy-done.1, bf16[1024,256]{1,0:T(8,128)(2,1)} %collective-permute-done.refs_1_, bf16[1024,256]{1,0:T(8,128)(2,1)S(1)} %copy-done.3, bf16[1024,256]{1,0:T(8,128)(2,1)} %collective-permute-done.5.refs_3_, ...), custom_call_target="tpu_custom_call" | custom-call | tf_op jit(solution)/shard_map/load_all/pallas_call | solution.py:309
  99.1 1.5 %collective-permute-done.12.refs_1_ = bf16[32,1024]{1,0:T(8,128)(2,1)S(1)} collective-permute-done((bf16[32,1024]{1,0:T(8,128)(2,1)S(1)}, bf16[32,1024]{1,0:T(8,128)(2,1)S(1)}, u32[]{:S(2)}, u32[]{:S(2)}) %collective-permute-start.12) | collective-permute-done | bytes 65568 | tf_op jit(solution)/shard_map/ppermute | solution.py:381
  100.5 1.3 project.1
  101.8 6.3 %collective-permute-start.16 = (bf16[4,128,256]{2,1,0:T(8,128)(2,1)S(1)}, bf16[4,128,256]{2,1,0:T(8,128)(2,1)S(1)}, u32[]{:S(2)}, u32[]{:S(2)}) collective-permute-start(bf16[4,128,256]{2,1,0:T(8,128)(2,1)S(1)} %get-tuple-element.38), channel_id=1, source_target_pairs={{0,1},{1,0},{2,3},{3,2},{4,5},{5,4},{6,7},{7,6},{8,9},{9,8},{10,11... | collective-permute-start | bytes 786440 | tf_op jit(solution)/shard_map/ppermute | solution.py:427
  108.1 1.2 collective-permute-done.16
  109.3 1.1 collective-permute-start.17
  110.4 3.7 %collective-permute-done.17 = bf16[2,128,256]{2,1,0:T(8,128)(2,1)S(1)} collective-permute-done((bf16[2,128,256]{2,1,0:T(8,128)(2,1)S(1)}, bf16[2,128,256]{2,1,0:T(8,128)(2,1)S(1)}, u32[]{:S(2)}, u32[]{:S(2)}) %collective-permute-start.17) | collective-permute-done | bytes 131104 | tf_op jit(solution)/shard_map/ppermute | solution.py:430
  114.2 3.6 %collective-permute-start.19 = (bf16[128,256]{1,0:T(8,128)(2,1)S(1)}, bf16[128,256]{1,0:T(8,128)(2,1)S(1)}, u32[]{:S(2)}, u32[]{:S(2)}) collective-permute-start(bf16[128,256]{1,0:T(8,128)(2,1)S(1)} %get-tuple-element.39), channel_id=1, source_target_pairs={{0,32},{1,160},{2,96},{3,224},{4,0},{5,128},{6,64},{7,192},{8,40},... | collective-permute-start | bytes 196616 | tf_op jit(solution)/shard_map/ppermute | solution.py:444
  117.8 6.2 %collective-permute-start.18 = (bf16[128,256]{1,0:T(8,128)(2,1)S(1)}, bf16[128,256]{1,0:T(8,128)(2,1)S(1)}, u32[]{:S(2)}, u32[]{:S(2)}) collective-permute-start(bf16[128,256]{1,0:T(8,128)(2,1)S(1)} %get-tuple-element.40), channel_id=1, source_target_pairs={{0,0},{1,128},{2,64},{3,192},{4,32},{5,160},{6,96},{7,224},{8,8},{... | collective-permute-start | bytes 196616 | tf_op jit(solution)/shard_map/ppermute | solution.py:444
  124.0 4.8 %collective-permute-done.18.refs_0_ = bf16[128,256]{1,0:T(8,128)(2,1)S(1)} collective-permute-done((bf16[128,256]{1,0:T(8,128)(2,1)S(1)}, bf16[128,256]{1,0:T(8,128)(2,1)S(1)}, u32[]{:S(2)}, u32[]{:S(2)}) %collective-permute-start.18) | collective-permute-done | bytes 65568 | tf_op jit(solution)/shard_map/ppermute | solution.py:444
  (54 shorter events, 8.1 us)
Async XLA Ops:
  0.0 20.9 %collective-permute-start = (bf16[1024,256]{1,0:T(8,128)(2,1)}, bf16[1024,256]{1,0:T(8,128)(2,1)}, u32[]{:S(2)}, u32[]{:S(2)}) collective-permute-start(bf16[1024,256]{1,0:T(8,128)(2,1)} %refs_0_.1), channel_id=1, source_target_pairs={{0,32},{8,40},{16,48},{24,56},{32,64},{40,72},{48,80},{56,88},{64,... | collective-permute-start | bytes 1572872 | tf_op jit(solution)/shard_map/ppermute | solution.py:385
  1.6 19.2 %collective-permute-start.1 = (bf16[1024,256]{1,0:T(8,128)(2,1)}, bf16[1024,256]{1,0:T(8,128)(2,1)}, u32[]{:S(2)}, u32[]{:S(2)}) collective-permute-start(bf16[1024,256]{1,0:T(8,128)(2,1)} %refs_0_.1), channel_id=1, source_target_pairs={{0,224},{8,232},{16,240},{24,248},{32,0},{40,8},{48,16},{56,24},{6... | collective-permute-start | bytes 1572872 | tf_op jit(solution)/shard_map/ppermute | solution.py:385
  5.6 0.8 copy-start.4
  8.3 12.5 %all-to-all-start = ((bf16[8,64,128]{2,1,0:T(8,128)(2,1)}), bf16[8,64,128]{2,1,0:T(8,128)(2,1)S(1)}, u32[]{:S(2)}, u32[]{:S(2)}) async-start(bf16[8,64,128]{2,1,0:T(8,128)(2,1)} %get-tuple-element.22), calls=%async_computation | async-start | bytes 262144 | tf_op jit(solution)/shard_map/all_to_all | solution.py:402
  20.9 6.9 %collective-permute-start.7 = (bf16[512,128]{1,0:T(8,128)(2,1)S(1)}, bf16[512,128]{1,0:T(8,128)(2,1)S(1)}, u32[]{:S(2)}, u32[]{:S(2)}) collective-permute-start(bf16[512,128]{1,0:T(8,128)(2,1)S(1)} %bitcast.13), channel_id=1, source_target_pairs={{0,8},{8,16},{16,24},{24,0},{32,40},{40,48},{48,56},{56,32},{64,72... | collective-permute-start | bytes 393224 | tf_op jit(solution)/shard_map/ppermute | solution.py:381
  22.1 31.1 %collective-permute-start.10 = (bf16[512,128]{1,0:T(8,128)(2,1)S(1)}, bf16[512,128]{1,0:T(8,128)(2,1)S(1)}, u32[]{:S(2)}, u32[]{:S(2)}) collective-permute-start(bf16[512,128]{1,0:T(8,128)(2,1)S(1)} %bitcast.14), channel_id=1, source_target_pairs={{0,24},{8,0},{16,8},{24,16},{32,56},{40,32},{48,40},{56,48},{64,88... | collective-permute-start | bytes 393224 | tf_op jit(solution)/shard_map/ppermute | solution.py:381
  23.5 15.9 %collective-permute-start.2 = (bf16[512,128]{1,0:T(8,128)(2,1)S(1)}, bf16[512,128]{1,0:T(8,128)(2,1)S(1)}, u32[]{:S(2)}, u32[]{:S(2)}) collective-permute-start(bf16[512,128]{1,0:T(8,128)(2,1)S(1)} %bitcast.15), channel_id=1, source_target_pairs={{0,16},{8,24},{16,0},{24,8},{32,48},{40,56},{48,32},{56,40},{64,80... | collective-permute-start | bytes 393224 | tf_op jit(solution)/shard_map/ppermute | solution.py:381
  25.1 25.3 %collective-permute-start.3 = (bf16[1024,256]{1,0:T(8,128)(2,1)}, bf16[1024,256]{1,0:T(8,128)(2,1)S(1)}, u32[]{:S(2)}, u32[]{:S(2)}) collective-permute-start(bf16[1024,256]{1,0:T(8,128)(2,1)} %collective-permute-done.refs_1_), channel_id=1, source_target_pairs={{0,32},{8,40},{16,48},{24,56},{32,64},{40,72},{48,80},{56,88},{64,... | collective-permute-start | bytes 1572872 | tf_op jit(solution)/shard_map/ppermute | solution.py:385
  26.9 23.5 %collective-permute-start.4 = (bf16[1024,256]{1,0:T(8,128)(2,1)}, bf16[1024,256]{1,0:T(8,128)(2,1)S(1)}, u32[]{:S(2)}, u32[]{:S(2)}) collective-permute-start(bf16[1024,256]{1,0:T(8,128)(2,1)} %collective-permute-done.1.refs_5_), channel_id=1, source_target_pairs={{0,224},{8,232},{16,240},{24,248},{32,0},{40,8},{48,16},{56,24},{6... | collective-permute-start | bytes 1572872 | tf_op jit(solution)/shard_map/ppermute | solution.py:385
  38.5 38.5 %collective-permute-start.8 = (bf16[144,512]{1,0:T(8,128)(2,1)S(1)}, bf16[144,512]{1,0:T(8,128)(2,1)S(1)}, u32[]{:S(2)}, u32[]{:S(2)}) collective-permute-start(bf16[144,512]{1,0:T(8,128)(2,1)S(1)} %prefix_attention.6), channel_id=1, source_target_pairs={{0,24},{8,0},{16,8},{24,16},{32,56},{40,32},{48,40},{56,48},{64,88... | collective-permute-start | bytes 442376 | tf_op jit(solution)/shard_map/ppermute | solution.py:381
  50.4 13.6 %copy-start.2 = (bf16[1024,256]{1,0:T(8,128)(2,1)}, bf16[1024,256]{1,0:T(8,128)(2,1)S(1)}, u32[]{:S(2)}) copy-start(bf16[1024,256]{1,0:T(8,128)(2,1)S(1)} %collective-permute-done.3.refs_2_) | copy-start | bytes 1572868
  50.4 13.6 %copy-start.8 = (bf16[1024,256]{1,0:T(8,128)(2,1)}, bf16[1024,256]{1,0:T(8,128)(2,1)S(1)}, u32[]{:S(2)}) copy-start(bf16[1024,256]{1,0:T(8,128)(2,1)S(1)} %collective-permute-done.4.refs_6_) | copy-start | bytes 1572868
  50.5 26.5 %collective-permute-start.5 = (bf16[1024,256]{1,0:T(8,128)(2,1)S(1)}, bf16[1024,256]{1,0:T(8,128)(2,1)}, u32[]{:S(2)}, u32[]{:S(2)}) collective-permute-start(bf16[1024,256]{1,0:T(8,128)(2,1)S(1)} %collective-permute-done.3.refs_2_), channel_id=1, source_target_pairs={{0,32},{8,40},{16,48},{24,56},{32,64},{40,72},{48,80},{56,88},{64,... | collective-permute-start | bytes 1572872 | tf_op jit(solution)/shard_map/ppermute | solution.py:385
  50.5 26.4 %collective-permute-start.6 = (bf16[1024,256]{1,0:T(8,128)(2,1)S(1)}, bf16[1024,256]{1,0:T(8,128)(2,1)S(1)}, u32[]{:S(2)}, u32[]{:S(2)}) collective-permute-start(bf16[1024,256]{1,0:T(8,128)(2,1)S(1)} %collective-permute-done.4.refs_6_), channel_id=1, source_target_pairs={{0,224},{8,232},{16,240},{24,248},{32,0},{40,8},{48,16},{56,24},{6... | collective-permute-start | bytes 1572872 | tf_op jit(solution)/shard_map/ppermute | solution.py:385
  64.0 19.1 %copy-start.11 = (bf16[8,4,2,128]{3,2,1,0:T(2,128)(2,1)S(1)}, bf16[8,4,2,128]{3,2,1,0:T(2,128)(2,1)}, u32[]{:S(2)}) copy-start(bf16[8,4,2,128]{3,2,1,0:T(2,128)(2,1)} %param.8) | copy-start | bytes 49156
  64.0 19.1 %copy-start.7 = (s32[8]{0:T(128)S(1)}, s32[8]{0:T(128)}, u32[]{:S(2)}) copy-start(s32[8]{0:T(128)} %len_ref.1) | copy-start | bytes 100
  64.0 13.0 %collective-permute-start.11 = (bf16[144,512]{1,0:T(8,128)(2,1)S(1)}, bf16[144,512]{1,0:T(8,128)(2,1)S(1)}, u32[]{:S(2)}, u32[]{:S(2)}) collective-permute-start(bf16[144,512]{1,0:T(8,128)(2,1)S(1)} %prefix_attention.7), channel_id=1, source_target_pairs={{0,8},{8,16},{16,24},{24,0},{32,40},{40,48},{48,56},{56,32},{64,72... | collective-permute-start | bytes 442376 | tf_op jit(solution)/shard_map/ppermute | solution.py:381
  64.7 12.4 %collective-permute-start.9 = (bf16[144,512]{1,0:T(8,128)(2,1)S(1)}, bf16[144,512]{1,0:T(8,128)(2,1)S(1)}, u32[]{:S(2)}, u32[]{:S(2)}) collective-permute-start(bf16[144,512]{1,0:T(8,128)(2,1)S(1)} %prefix_attention.5), channel_id=1, source_target_pairs={{0,16},{8,24},{16,0},{24,8},{32,48},{40,56},{48,32},{56,40},{64,80... | collective-permute-start | bytes 442376 | tf_op jit(solution)/shard_map/ppermute | solution.py:381
  76.9 15.4 %copy-start.6 = (s32[8,1]{0,1:T(1,128)S(1)}, s32[8,1]{0,1:T(1,128)}, u32[]{:S(2)}) copy-start(s32[8,1]{0,1:T(1,128)} %param.12) | copy-start | bytes 100
  76.9 20.2 %copy-start.1 = (bf16[1024,256]{1,0:T(8,128)(2,1)S(1)}, bf16[1024,256]{1,0:T(8,128)(2,1)}, u32[]{:S(2)}) copy-start(bf16[1024,256]{1,0:T(8,128)(2,1)} %refs_0_.1) | copy-start | bytes 1572868
  76.9 20.2 %copy-start.3 = (bf16[1024,256]{1,0:T(8,128)(2,1)S(1)}, bf16[1024,256]{1,0:T(8,128)(2,1)}, u32[]{:S(2)}) copy-start(bf16[1024,256]{1,0:T(8,128)(2,1)} %copy-done.2) | copy-start | bytes 1572868
  76.9 0.8 copy-start.9
  77.0 19.3 %collective-permute-start.15 = (bf16[1024,256]{1,0:T(8,128)(2,1)}, bf16[1024,256]{1,0:T(8,128)(2,1)S(1)}, u32[]{:S(2)}, u32[]{:S(2)}) collective-permute-start(bf16[1024,256]{1,0:T(8,128)(2,1)} %collective-permute-done.5.refs_3_), channel_id=1, source_target_pairs={{0,32},{8,40},{16,48},{24,56},{32,64},{40,72},{48,80},{56,88},{64,... | collective-permute-start | bytes 1572872 | tf_op jit(solution)/shard_map/ppermute | solution.py:385
  78.6 13.7 %all-to-all-start.1 = ((bf16[8,80,128]{2,1,0:T(8,128)(2,1)}), bf16[8,80,128]{2,1,0:T(8,128)(2,1)S(1)}, u32[]{:S(2)}, u32[]{:S(2)}) async-start(bf16[8,80,128]{2,1,0:T(8,128)(2,1)} %merge_parts.1), calls=%async_computation.1 | async-start | bytes 327680 | tf_op jit(solution)/shard_map/all_to_all | solution.py:421
  83.2 1.6 %copy-start = (bf16[8,2,512,128]{3,2,1,0:T(8,128)(2,1)S(1)}, bf16[8,2,512,128]{3,2,1,0:T(8,128)(2,1)}, u32[]{:S(2)}) copy-start(bf16[8,2,512,128]{3,2,1,0:T(8,128)(2,1)} %kv_ref.1) | copy-start | bytes 6291460
  93.1 5.9 %collective-permute-start.14 = (bf16[32,1024]{1,0:T(8,128)(2,1)S(1)}, bf16[32,1024]{1,0:T(8,128)(2,1)S(1)}, u32[]{:S(2)}, u32[]{:S(2)}) collective-permute-start(bf16[32,1024]{1,0:T(8,128)(2,1)S(1)} %finish_attention.1.refs_0_), channel_id=1, source_target_pairs={{0,24},{8,0},{16,8},{24,16},{32,56},{40,32},{48,40},{56,48},{64,88... | collective-permute-start | bytes 196616 | tf_op jit(solution)/shard_map/ppermute | solution.py:381
  94.4 4.6 %collective-permute-start.13 = (bf16[32,1024]{1,0:T(8,128)(2,1)S(1)}, bf16[32,1024]{1,0:T(8,128)(2,1)S(1)}, u32[]{:S(2)}, u32[]{:S(2)}) collective-permute-start(bf16[32,1024]{1,0:T(8,128)(2,1)S(1)} %finish_attention.1.refs_0_), channel_id=1, source_target_pairs={{0,16},{8,24},{16,0},{24,8},{32,48},{40,56},{48,32},{56,40},{64,80... | collective-permute-start | bytes 196616 | tf_op jit(solution)/shard_map/ppermute | solution.py:381
  96.2 4.3 %collective-permute-start.12 = (bf16[32,1024]{1,0:T(8,128)(2,1)S(1)}, bf16[32,1024]{1,0:T(8,128)(2,1)S(1)}, u32[]{:S(2)}, u32[]{:S(2)}) collective-permute-start(bf16[32,1024]{1,0:T(8,128)(2,1)S(1)} %finish_attention.1.refs_0_), channel_id=1, source_target_pairs={{0,8},{8,16},{16,24},{24,0},{32,40},{40,48},{48,56},{56,32},{64,72... | collective-permute-start | bytes 196616 | tf_op jit(solution)/shard_map/ppermute | solution.py:381
  101.8 7.5 %collective-permute-start.16 = (bf16[4,128,256]{2,1,0:T(8,128)(2,1)S(1)}, bf16[4,128,256]{2,1,0:T(8,128)(2,1)S(1)}, u32[]{:S(2)}, u32[]{:S(2)}) collective-permute-start(bf16[4,128,256]{2,1,0:T(8,128)(2,1)S(1)} %get-tuple-element.38), channel_id=1, source_target_pairs={{0,1},{1,0},{2,3},{3,2},{4,5},{5,4},{6,7},{7,6},{8,9},{9,8},{10,11... | collective-permute-start | bytes 786440 | tf_op jit(solution)/shard_map/ppermute | solution.py:427
  109.3 4.8 %collective-permute-start.17 = (bf16[2,128,256]{2,1,0:T(8,128)(2,1)S(1)}, bf16[2,128,256]{2,1,0:T(8,128)(2,1)S(1)}, u32[]{:S(2)}, u32[]{:S(2)}) collective-permute-start(bf16[2,128,256]{2,1,0:T(8,128)(2,1)S(1)} %add_convert_fusion.1), channel_id=1, source_target_pairs={{0,2},{1,3},{2,0},{3,1},{4,6},{5,7},{6,4},{7,5},{8,10},{9,11},{10,... | collective-permute-start | bytes 393224 | tf_op jit(solution)/shard_map/ppermute | solution.py:430
  114.2 9.8 %collective-permute-start.19 = (bf16[128,256]{1,0:T(8,128)(2,1)S(1)}, bf16[128,256]{1,0:T(8,128)(2,1)S(1)}, u32[]{:S(2)}, u32[]{:S(2)}) collective-permute-start(bf16[128,256]{1,0:T(8,128)(2,1)S(1)} %get-tuple-element.39), channel_id=1, source_target_pairs={{0,32},{1,160},{2,96},{3,224},{4,0},{5,128},{6,64},{7,192},{8,40},... | collective-permute-start | bytes 196616 | tf_op jit(solution)/shard_map/ppermute | solution.py:444
  117.8 11.0 %collective-permute-start.18 = (bf16[128,256]{1,0:T(8,128)(2,1)S(1)}, bf16[128,256]{1,0:T(8,128)(2,1)S(1)}, u32[]{:S(2)}, u32[]{:S(2)}) collective-permute-start(bf16[128,256]{1,0:T(8,128)(2,1)S(1)} %get-tuple-element.40), channel_id=1, source_target_pairs={{0,0},{1,128},{2,64},{3,192},{4,32},{5,160},{6,96},{7,224},{8,8},{... | collective-permute-start | bytes 196616 | tf_op jit(solution)/shard_map/ppermute | solution.py:444
  (2 other events, 1.4 us)
